TPU v7x, 128 devices: a whole 4x4x4 slice. The times are simulated.
128 devices in a mesh: group: 8 (over y_hi, x), replica: 16 (over y_lo, z, core).
Axes of the slice: x: 4, y: 4 (y_hi: 2, y_lo: 2; y = y_hi * 2 + y_lo), z: 4, core: 2. Of those that a mesh axis runs over, the one named last changes fastest.
Arguments:
- hidden_in: bfloat16 [16, 1024, 1536], P('replica', 'group'), may hold values from -6 to 6
- norm_attn: bfloat16 [1536], P('group'), may hold values from 0.099609375 to 1.8984375
- w_qkv: bfloat16 [1536, 2048], P('group'), may hold values from -0.15625 to 0.15625
- b_qkv: bfloat16 [2048], P('group'), may hold values from -3 to 3
- w_out: bfloat16 [1536, 1536], P('group'), may hold values from -0.625 to 0.625
- norm_mlp: bfloat16 [1536], P('group'), may hold values from 0.099609375 to 1.8984375
- w_gate_up: bfloat16 [1536, 17920], P('group'), may hold values from -0.15625 to 0.15625
- w_down: bfloat16 [8960, 1536], P('group'), may hold values from -0.09375 to 0.09375
- cotangent: bfloat16 [16, 1024, 1536], P('replica', 'group'), may hold values from -6 to 6
Outputs:
- hidden_out: bfloat16 [16, 1024, 1536], P('replica', 'group')
- grad_in: float32 [16, 1024, 1536], P('replica', 'group')
- grad_norm_attn: float32 [1536], P('group')
- grad_w_qkv: float32 [1536, 2048], P('group')
- grad_b_qkv: float32 [2048], P('group')
- grad_w_out: float32 [1536, 1536], P('group')
- grad_norm_mlp: float32 [1536], P('group')
- grad_w_gate_up: float32 [1536, 17920], P('group')
- grad_w_down: float32 [8960, 1536], P('group')
All inputs are finite; a program needn't handle non-finite values.
Results may differ from a plain program's by a relative error of at most 0.025.
Values may be sent and summed in bfloat16 or wider, within the bound.
No kernel may reach another device: no remote copies, remote signals or barrier semaphores. Data moves between devices by JAX's collectives and lax.ppermute only.
A program may use at most 320 MiB of HBM per device.

v0:
```python
import jax
import jax.numpy as jnp
from jax import lax
from jax.sharding import PartitionSpec as P

HEADS = 12
KV_HEADS = 2
HEAD = 128
FF = 8960


NORM_EPSILON = 1e-06
ROPE_BASE = 1000000.0


def rope_tables(first_row, row_count, head_size):
    half_width = head_size // 2
    position = (first_row + jnp.arange(row_count, dtype=jnp.int32)).astype(jnp.float32)
    frequency = jnp.power(
        ROPE_BASE, -(jnp.arange(half_width, dtype=jnp.int32).astype(jnp.float32) * 2.0) / head_size
    )
    angles = position[:, None] * frequency[None, :]
    cosine = jnp.concatenate([jnp.cos(angles), jnp.cos(angles)], axis=-1)
    sine_part = jnp.concatenate([jnp.sin(angles), jnp.sin(angles)], axis=-1)
    return (cosine[:, None, :], sine_part[:, None, :])


def rotate_half(vectors):
    half_width = vectors.shape[-1] // 2
    return jnp.concatenate([-vectors[..., half_width:], vectors[..., :half_width]], axis=-1)


def turn(vectors, cosine, sine_part):
    return vectors * cosine + rotate_half(vectors) * sine_part


def turn_back(grads_in, cosine, sine_part):
    return grads_in * cosine - rotate_half(grads_in) * sine_part


def rms_scale(rows_in):
    return lax.rsqrt(jnp.mean(rows_in * rows_in, axis=-1, keepdims=True) + NORM_EPSILON)


def norm_back(grad_normed, rows_in, scale_rows, gain_full):
    gain_grad = jnp.sum(grad_normed * rows_in * scale_rows, axis=0)
    weighted = grad_normed * gain_full
    mean_term = jnp.mean(weighted * rows_in, axis=-1, keepdims=True)
    row_grad = scale_rows * (weighted - rows_in * scale_rows * scale_rows * mean_term)
    return (row_grad, gain_grad)


def contract_rows(left_side, right_side):
    return lax.dot_general(
        left_side, right_side, (((0,), (0,)), ((), ())), preferred_element_type=jnp.float32
    )


def contract_cols(left_side, right_side):
    return lax.dot_general(
        left_side, right_side, (((1,), (1,)), ((), ())), preferred_element_type=jnp.float32
    )


def on_device(hidden_in, norm_attn, w_qkv, b_qkv, w_out, norm_mlp, w_gate_up, w_down, cotangent):
    rows_in = hidden_in[0].astype(jnp.float32)
    row_count = rows_in.shape[0]
    first_row = lax.axis_index("group") * row_count
    width_q = HEADS * HEAD
    width_k = KV_HEADS * HEAD
    groups = HEADS // KV_HEADS
    score_scale = HEAD ** (-0.5)
    gain_one, qkv_full, bias_full, out_full, gain_two = (
        lax.all_gather(norm_attn, "group", axis=0, tiled=True),
        lax.all_gather(w_qkv, "group", axis=0, tiled=True),
        lax.all_gather(b_qkv, "group", axis=0, tiled=True),
        lax.all_gather(w_out, "group", axis=0, tiled=True),
        lax.all_gather(norm_mlp, "group", axis=0, tiled=True),
    )
    gain_one = gain_one.astype(jnp.float32)
    gain_two = gain_two.astype(jnp.float32)
    scale_one = rms_scale(rows_in)
    normed_one = (rows_in * scale_one * gain_one).astype(jnp.bfloat16)
    projected = jnp.dot(
        normed_one, qkv_full, preferred_element_type=jnp.float32
    ) + bias_full.astype(jnp.float32)
    cosine, sine_part = rope_tables(first_row, row_count, HEAD)
    queries = turn(
        projected[:, :width_q].reshape(row_count, HEADS, HEAD), cosine, sine_part
    ).astype(jnp.bfloat16)
    keys_own = turn(
        projected[:, width_q : width_q + width_k].reshape(row_count, KV_HEADS, HEAD),
        cosine,
        sine_part,
    )
    kv_own = jnp.concatenate(
        [keys_own.reshape(row_count, width_k), projected[:, width_q + width_k :]], axis=1
    ).astype(jnp.bfloat16)
    kv_all = lax.all_gather(kv_own, "group", axis=0, tiled=True)
    length = kv_all.shape[0]
    keys_all = kv_all[:, :width_k].reshape(length, KV_HEADS, HEAD)
    values_all = kv_all[:, width_k:].reshape(length, KV_HEADS, HEAD)
    query_groups = queries.reshape(row_count, KV_HEADS, groups, HEAD)
    allowed = (first_row + jnp.arange(row_count, dtype=jnp.int32))[:, None] >= jnp.arange(
        length, dtype=jnp.int32
    )[None, :]

    def score_block():
        raw_scores = jnp.einsum(
            "qkgd,skd->kgqs", query_groups, keys_all, preferred_element_type=jnp.float32
        )
        return jnp.where(allowed, raw_scores * score_scale, -1e30)

    scores = score_block()
    row_top = jnp.max(scores, axis=-1, keepdims=True)
    exponent = jnp.exp(scores - row_top)
    row_total = jnp.sum(exponent, axis=-1, keepdims=True)
    attn_probs = exponent / row_total
    log_total = row_top + jnp.log(row_total)
    attended = (
        jnp.einsum(
            "kgqs,skd->qkgd",
            attn_probs.astype(jnp.bfloat16),
            values_all,
            preferred_element_type=jnp.float32,
        )
        .reshape(row_count, width_q)
        .astype(jnp.bfloat16)
    )
    middle = rows_in + jnp.dot(attended, out_full, preferred_element_type=jnp.float32)
    scale_two = rms_scale(middle)
    normed_two = (middle * scale_two * gain_two).astype(jnp.bfloat16)
    columns = normed_two
    gate_up = jnp.dot(
        columns,
        lax.all_gather(w_gate_up, "group", axis=0, tiled=True),
        preferred_element_type=jnp.float32,
    )
    gate_part = gate_up[:, :FF]
    up_part = gate_up[:, FF:]
    gate_sig = jax.nn.sigmoid(gate_part)
    activated = (gate_part * gate_sig * up_part).astype(jnp.bfloat16)
    columns = activated
    branch_two = jnp.dot(
        columns,
        lax.all_gather(w_down, "group", axis=0, tiled=True),
        preferred_element_type=jnp.float32,
    )
    result = (middle + branch_two).astype(jnp.bfloat16)[None]
    grad_out = cotangent[0]
    grad_act = contract_cols(grad_out, lax.all_gather(w_down, "group", axis=0, tiled=True))
    grad_gate = grad_act * up_part * gate_sig * (1.0 + gate_part * (1.0 - gate_sig))
    grad_up = grad_act * gate_part * gate_sig
    grad_gate_up = jnp.concatenate([grad_gate, grad_up], axis=1).astype(jnp.bfloat16)
    down_grad = lax.psum_scatter(
        contract_rows(activated, grad_out).astype(jnp.bfloat16),
        "group",
        scatter_dimension=0,
        tiled=True,
    )
    grad_normed_two = contract_cols(
        grad_gate_up, lax.all_gather(w_gate_up, "group", axis=0, tiled=True)
    )
    gate_up_grad = lax.psum_scatter(
        contract_rows(normed_two, grad_gate_up).astype(jnp.bfloat16),
        "group",
        scatter_dimension=0,
        tiled=True,
    )
    grad_mid_norm, gain_two_grad = norm_back(grad_normed_two, middle, scale_two, gain_two)
    grad_middle = grad_out.astype(jnp.float32) + grad_mid_norm
    grad_branch = grad_middle.astype(jnp.bfloat16)
    grad_attended = (
        contract_cols(grad_branch, out_full)
        .astype(jnp.bfloat16)
        .reshape(row_count, KV_HEADS, groups, HEAD)
    )
    grad_probs = jnp.einsum(
        "qkgd,skd->kgqs", grad_attended, values_all, preferred_element_type=jnp.float32
    )
    scores = score_block()
    attn_probs = jnp.exp(scores - log_total)
    inner_sum = jnp.sum(attn_probs * grad_probs, axis=-1, keepdims=True)
    grad_scores = (attn_probs * (grad_probs - inner_sum)).astype(jnp.bfloat16)
    probs_low = attn_probs.astype(jnp.bfloat16)
    grad_queries = (
        jnp.einsum(
            "kgqs,skd->qkgd", grad_scores, keys_all, preferred_element_type=jnp.float32
        ).reshape(row_count, HEADS, HEAD)
        * score_scale
    )
    grad_keys = (
        jnp.einsum("kgqs,qkgd->skd", grad_scores, query_groups, preferred_element_type=jnp.float32)
        * score_scale
    )
    grad_values = jnp.einsum(
        "kgqs,qkgd->skd", probs_low, grad_attended, preferred_element_type=jnp.float32
    )
    grad_kv_whole = jnp.concatenate(
        [grad_keys.reshape(length, width_k), grad_values.reshape(length, width_k)], axis=1
    )
    grad_kv = lax.psum_scatter(
        grad_kv_whole.astype(jnp.bfloat16), "group", scatter_dimension=0, tiled=True
    ).astype(jnp.float32)
    grad_q_pre = turn_back(grad_queries, cosine, sine_part).reshape(row_count, width_q)
    grad_k_pre = turn_back(
        grad_kv[:, :width_k].reshape(row_count, KV_HEADS, HEAD), cosine, sine_part
    )
    grad_projected = jnp.concatenate(
        [grad_q_pre, grad_k_pre.reshape(row_count, width_k), grad_kv[:, width_k:]], axis=1
    ).astype(jnp.bfloat16)
    grad_normed_one = contract_cols(grad_projected, qkv_full)
    grad_rows_norm, gain_one_grad = norm_back(grad_normed_one, rows_in, scale_one, gain_one)
    grad_in = (grad_middle + grad_rows_norm)[None]
    out_grad = contract_rows(attended, grad_branch)
    bias_grad = jnp.sum(grad_projected.astype(jnp.float32), axis=0)
    qkv_grad = contract_rows(normed_one, grad_projected)
    shards = (
        lax.psum_scatter(
            gain_one_grad.astype(jnp.bfloat16), "group", scatter_dimension=0, tiled=True
        ).astype(jnp.float32),
        lax.psum_scatter(
            qkv_grad.astype(jnp.bfloat16), "group", scatter_dimension=0, tiled=True
        ).astype(jnp.float32),
        lax.psum_scatter(
            bias_grad.astype(jnp.bfloat16), "group", scatter_dimension=0, tiled=True
        ).astype(jnp.float32),
        lax.psum_scatter(
            out_grad.astype(jnp.bfloat16), "group", scatter_dimension=0, tiled=True
        ).astype(jnp.float32),
        lax.psum_scatter(
            gain_two_grad.astype(jnp.bfloat16), "group", scatter_dimension=0, tiled=True
        ).astype(jnp.float32),
    )
    totals = (
        lax.psum(shards[0].astype(jnp.bfloat16), "replica").astype(jnp.float32),
        lax.psum(shards[1].astype(jnp.bfloat16), "replica").astype(jnp.float32),
        lax.psum(shards[2].astype(jnp.bfloat16), "replica").astype(jnp.float32),
        lax.psum(shards[3].astype(jnp.bfloat16), "replica").astype(jnp.float32),
        lax.psum(shards[4].astype(jnp.bfloat16), "replica").astype(jnp.float32),
        lax.psum(gate_up_grad, "replica").astype(jnp.float32),
        lax.psum(down_grad, "replica").astype(jnp.float32),
    )
    return (
        result,
        grad_in,
        totals[0],
        totals[1],
        totals[2],
        totals[3],
        totals[4],
        totals[5],
        totals[6],
    )


def solution(mesh):
    placed = (
        P("replica", "group", None),
        P("group"),
        P("group", None),
        P("group"),
        P("group", None),
        P("group"),
        P("group", None),
        P("group", None),
        P("replica", "group", None),
    )
    return jax.shard_map(
        on_device,
        mesh=mesh,
        in_specs=placed,
        out_specs=(
            P("replica", "group", None),
            P("replica", "group", None),
            P("group"),
            P("group", None),
            P("group"),
            P("group", None),
            P("group"),
            P("group", None),
            P("group", None),
        ),
        check_vma=False,
    )
```

profile of v0, /device:TPU:7, one launch (start us, length us, event | category | flops | bytes accessed | tf_op | source)
XLA Modules:
  0.0 2390.4 jit_solution(82699693179786081)
XLA Ops:
  12.3 15.9 all-reduce.8
  28.3 16.3 all-gather
  46.8 53.4 %all-gather.7.cloned.1.call-done = bf16[1536,2048]{1,0:T(8,128)(2,1)} async-done(((bf16[192,2048]{1,0:T(8,128)(2,1)}), bf16[1536,2048]{1,0:T(8,128)(2,1)}) %all-gather.7.cloned.1.call-update) | async-done | bytes 6291472 | tf_op jit(solution)/shard_map/all_gather | solution.py:75
  108.8 43.0 %all-gather.9.cloned.1.call-done = bf16[1024,512]{1,0:T(8,128)(2,1)} async-done(((bf16[128,512]{1,0:T(8,128)(2,1)}), bf16[1024,512]{1,0:T(8,128)(2,1)}) %all-gather.9.cloned.1.call-update) | async-done | bytes 1048592 | tf_op jit(solution)/shard_map/all_gather | solution.py:99
  159.1 69.5 %all-gather.11.cloned.1.call-done = bf16[1536,1536]{1,0:T(8,128)(2,1)} async-done(((bf16[192,1536]{1,0:T(8,128)(2,1)}), bf16[1536,1536]{1,0:T(8,128)(2,1)}) %all-gather.11.cloned.1.call-update) | async-done | bytes 4718608 | tf_op jit(solution)/shard_map/all_gather | solution.py:77
  232.0 534.5 %all-gather.13.cloned.1.call-done = bf16[1536,17920]{1,0:T(8,128)(2,1)} async-done(((bf16[192,17920]{1,0:T(8,128)(2,1)}), bf16[1536,17920]{1,0:T(8,128)(2,1)}) %all-gather.13.cloned.1.call-update) | async-done | bytes 55050256 | tf_op jit(solution)/shard_map/all_gather | solution.py:136
  766.5 26.1 %fusion.52 = f32[128,17920]{1,0:T(8,128)} fusion(bf16[1536,17920]{1,0:T(8,128)(2,1)} %all-gather.13.cloned.1.call-done, f32[128,1536]{1,0:T(8,128)S(1)} %get-tuple-element.49, f32[1536]{0:T(1024)S(1)} %convert_element_type.140, f32[128]{0:T(128)S(1)} %add_rsqrt_fusion), kind=kOutput, calls=%fused_computation.106 | convolution fusion | flops 7047020544 | bytes 65018368 | tf_op jit(solution)/shard_map/dot_general | solution.py:134
  792.6 258.7 %all-gather.15.cloned.1.call-done = bf16[8960,1536]{1,0:T(8,128)(2,1)} async-done(((bf16[1120,1536]{1,0:T(8,128)(2,1)}), bf16[8960,1536]{1,0:T(8,128)(2,1)}) %all-gather.15.cloned.1.call-update) | async-done | bytes 27525136 | tf_op jit(solution)/shard_map/all_gather | solution.py:146
  1051.3 17.8 multiply_convert_fusion.1
  1069.0 26.6 %multiply_reduce_fusion = (bf16[1536]{0:T(1024)(128)(2,1)}, f32[128]{0:T(128)S(1)}, f32[128,1536]{1,0:T(8,128)}) fusion(f32[128,1536]{1,0:T(8,128)S(1)} %get-tuple-element.49, f32[128]{0:T(128)S(1)} %add_rsqrt_fusion, f32[1536]{0:T(1024)S(1)} %convert_element_type.140, bf16[1536,17920]{1,0:T(8,128)(2,1)} %all-gather.13.cloned.1.call-done, ...), kind=kOutput, calls=%fused_computation.61 | convolution fusion | flops 7056783872 | bytes 61220864 | tf_op jit(solution)/shard_map/dot_general | solution.py:60
  1106.3 7.2 fusion
  1114.5 5.9 fusion.2
  1133.6 63.0 %reduce-scatter.6.cloned.1.call-done = bf16[128,512]{1,0:T(8,128)(2,1)} async-done(((bf16[1024,512]{1,0:T(8,128)(2,1)}), bf16[128,512]{1,0:T(8,128)(2,1)}) %reduce-scatter.6.cloned.1.call-update) | async-done | bytes 131088 | tf_op jit(solution)/shard_map/reduce_scatter | solution.py:202
  1205.5 13.2 convolution_convert_fusion.1
  1219.8 23.9 %convolution_convert_fusion = bf16[1536,17920]{1,0:T(8,128)(2,1)} fusion(bf16[128,8960]{1,0:T(8,128)(2,1)} %get-tuple-element.26, bf16[128,8960]{1,0:T(8,128)(2,1)} %copy-done.14, f32[128,1536]{1,0:T(8,128)S(1)} %copy-done.2, f32[1536]{0:T(1024)S(1)} %convert_element_type.140, f32[128]{0:T(128)} %copy-done.26), kind=kOutput, calls=%fused_computation | convolution fusion | flops 7083720704 | bytes 60430848 | tf_op jit(solution)/shard_map/dot_general | solution.py:54
  1243.8 45.0 %reduce-scatter.10.cloned.1.call-done = bf16[192,1536]{1,0:T(8,128)(2,1)} async-done(((bf16[1536,1536]{1,0:T(8,128)(2,1)}), bf16[192,1536]{1,0:T(8,128)(2,1)}) %reduce-scatter.10.cloned.1.call-update) | async-done | bytes 589840 | tf_op jit(solution)/shard_map/reduce_scatter | solution.py:228
  1288.8 102.7 %reduce-scatter.8.cloned.1.call-done = bf16[192,2048]{1,0:T(8,128)(2,1)} async-done(((bf16[1536,2048]{1,0:T(8,128)(2,1)}), bf16[192,2048]{1,0:T(8,128)(2,1)}) %reduce-scatter.8.cloned.1.call-update) | async-done | bytes 786448 | tf_op jit(solution)/shard_map/reduce_scatter | solution.py:222
  1391.5 287.6 %reduce-scatter.14.cloned.1.call-done = bf16[1120,1536]{1,0:T(8,128)(2,1)} async-done(((bf16[8960,1536]{1,0:T(8,128)(2,1)}), bf16[1120,1536]{1,0:T(8,128)(2,1)}) %reduce-scatter.14.cloned.1.call-update) | async-done | bytes 3440656 | tf_op jit(solution)/shard_map/reduce_scatter | solution.py:155
  1679.1 530.8 %reduce-scatter.12.cloned.1.call-done = bf16[192,17920]{1,0:T(8,128)(2,1)} async-done(((bf16[1536,17920]{1,0:T(8,128)(2,1)}), bf16[192,17920]{1,0:T(8,128)(2,1)}) %reduce-scatter.12.cloned.1.call-update) | async-done | bytes 6881296 | tf_op jit(solution)/shard_map/reduce_scatter | solution.py:164
  2211.2 11.8 fusion.11
  2228.8 29.7 %all-reduce.7 = (bf16[1536]{0:T(1024)(128)(2,1)S(1)}, bf16[2048]{0:T(1024)(128)(2,1)S(1)}, bf16[1536]{0:T(1024)(128)(2,1)S(1)}) all-reduce(bf16[1536]{0:T(1024)(128)(2,1)S(1)} %get-tuple-element.11, bf16[2048]{0:T(1024)(128)(2,1)S(1)} %fusion.53, ...), channel_id=3, replica_groups=mesh['group'=8,'replica'=16] {'group'}, use_global_device_ids=true, to_apply=%region_9.10.clone | all-reduce | flops 5120 | bytes 20480
  2258.7 35.3 %all-reduce.5 = (bf16[192]{0:T(256)(128)(2,1)S(1)}, bf16[256]{0:T(256)(128)(2,1)S(1)}, bf16[192]{0:T(256)(128)(2,1)S(1)}) all-reduce(bf16[192]{0:T(256)(128)(2,1)S(1)} %dynamic-slice.3, bf16[256]{0:T(256)(128)(2,1)S(1)} %dynamic-slice.5, bf16[192]{0:T(256)(128)(2,1)S(1)} %dynamic-slice.7), channel_id=1, replica_groups=mesh['group'=8,'replica'=16] {'replica'}, use_global_device_ids=true, to_apply=%region_10.11 | all-reduce | flops 640 | bytes 2560 | tf_op jit(solution)/shard_map/psum | solution.py:236
  2296.8 70.9 %all-reduce.11.cloned.1.call-done = (bf16[192,2048]{1,0:T(8,128)(2,1)}, bf16[192,1536]{1,0:T(8,128)(2,1)}, bf16[192,17920]{1,0:T(8,128)(2,1)}, bf16[1120,1536]{1,0:T(8,128)(2,1)}) async-done(((bf16[192,2048]{1,0:T(8,128)(2,1)}, bf16[192,1536]{1,0:T(8,128)(2,1)}, bf16[192,17920]{1,0:T(8,128)(2,1)}, bf16[1120,1536]{1,0:T(8,128)(2,1)}), (bf16[192,2048]{1,0:T(8,128)(2,1)}, bf16[192,1536]{1,0:T(8,128)(2,1)}, ...) | async-done | bytes 11698192 | tf_op jit(solution)/shard_map/psum | solution.py:237
  2376.8 6.7 convert_element_type.159
  (166 shorter events, 78.1 us)
Async XLA Ops:
  7.2 93.0 %all-gather.7.cloned.1.call-start = ((), (), s32[]{:S(2)}) async-start(), calls=%async_computation.5 | async-start | bytes 7077888 | tf_op jit(solution)/shard_map/all_gather | solution.py:75
  7.9 143.9 %all-gather.9.cloned.1.call-start = ((), (), s32[]{:S(2)}) async-start(), calls=%async_computation.6 | async-start | bytes 1179648 | tf_op jit(solution)/shard_map/all_gather | solution.py:99
  44.8 63.9 %copy-start.20 = (f32[128,128]{0,1:T(8,128)}, f32[128,128]{0,1:T(8,128)S(1)}, u32[]{:S(2)}) copy-start(f32[128,128]{0,1:T(8,128)S(1)} %pad_maximum_fusion.7) | copy-start | bytes 196612
  44.9 62.6 %copy-start.23 = (f32[128,128]{1,0:T(8,128)}, f32[128,128]{1,0:T(8,128)S(1)}, u32[]{:S(2)}) copy-start(f32[128,128]{1,0:T(8,128)S(1)} %copy.58) | copy-start | bytes 196612
  46.8 57.4 %copy-start.28 = (f32[128]{0:T(128)}, f32[128]{0:T(128)S(1)}, u32[]{:S(2)}) copy-start(f32[128]{0:T(128)S(1)} %add_rsqrt_fusion.1) | copy-start | bytes 1540
  106.2 122.5 %all-gather.11.cloned.1.call-start = ((), (), s32[]{:S(2)}) async-start(), calls=%async_computation.7 | async-start | bytes 5308416 | tf_op jit(solution)/shard_map/all_gather | solution.py:77
  106.9 659.6 %all-gather.13.cloned.1.call-start = ((), (), s32[]{:S(2)}) async-start(), calls=%async_computation.8 | async-start | bytes 61931520 | tf_op jit(solution)/shard_map/all_gather | solution.py:136
  107.5 943.8 %all-gather.15.cloned.1.call-start = ((), (), s32[]{:S(2)}) async-start(), calls=%async_computation.9 | async-start | bytes 30965760 | tf_op jit(solution)/shard_map/all_gather | solution.py:146
  108.1 1088.6 %reduce-scatter.6.cloned.1.call-start = ((), (), s32[]{:S(2)}) async-start(), calls=%async_computation.10 | async-start | bytes 1179648 | tf_op jit(solution)/shard_map/reduce_scatter | solution.py:202
  108.8 46.3 %copy-start.10 = (bf16[128,2,6,128]{0,3,2,1:T(8,128)(2,1)}, bf16[128,2,6,128]{0,3,2,1:T(8,128)(2,1)S(1)}, u32[]{:S(2)}) copy-start(bf16[128,2,6,128]{0,3,2,1:T(8,128)(2,1)S(1)} %fusion.34) | copy-start | bytes 1179652
  157.9 70.8 %copy-start.6 = (bf16[1,128,1536]{2,1,0:T(8,128)(2,1)S(1)}, bf16[1,128,1536]{2,1,0:T(8,128)(2,1)}, u32[]{:S(2)}) copy-start(bf16[1,128,1536]{2,1,0:T(8,128)(2,1)} %param.9) | copy-start | bytes 1179652
  159.1 633.4 %copy-start.13 = (bf16[2,128,6,128]{3,1,2,0:T(8,128)(2,1)}, bf16[2,128,6,128]{3,1,2,0:T(8,128)(2,1)S(1)}, u32[]{:S(2)}) copy-start(bf16[2,128,6,128]{3,1,2,0:T(8,128)(2,1)S(1)} %fusion.20) | copy-start | bytes 1179652
  231.9 863.7 %copy-start.1 = (f32[128,1536]{1,0:T(8,128)}, f32[128,1536]{1,0:T(8,128)S(1)}, u32[]{:S(2)}) copy-start(f32[128,1536]{1,0:T(8,128)S(1)} %get-tuple-element.49) | copy-start | bytes 2359300
  231.9 863.7 %copy-start.26 = (f32[128]{0:T(128)}, f32[128]{0:T(128)S(1)}, u32[]{:S(2)}) copy-start(f32[128]{0:T(128)S(1)} %add_rsqrt_fusion) | copy-start | bytes 1540
  232.0 874.3 %copy-start.27 = (f32[2,6,128]{2,1,0:T(8,128)}, f32[2,6,128]{2,1,0:T(8,128)S(1)}, u32[]{:S(2)}) copy-start(f32[2,6,128]{2,1,0:T(8,128)S(1)} %log_add_fusion) | copy-start | bytes 18436
  1126.7 162.1 %reduce-scatter.10.cloned.1.call-start = ((), (), s32[]{:S(2)}) async-start(), calls=%async_computation.12 | async-start | bytes 5308416 | tf_op jit(solution)/shard_map/reduce_scatter | solution.py:228
  1131.6 259.9 %reduce-scatter.8.cloned.1.call-start = ((), (), s32[]{:S(2)}) async-start(), calls=%async_computation.11 | async-start | bytes 7077888 | tf_op jit(solution)/shard_map/reduce_scatter | solution.py:222
  1133.3 64.6 %copy-start.24 = (f32[128,128]{1,0:T(8,128)S(1)}, f32[128,128]{1,0:T(8,128)}, u32[]{:S(2)}) copy-start(f32[128,128]{1,0:T(8,128)} %copy-done.23) | copy-start | bytes 196612
  1133.4 64.8 %copy-start.19 = (f32[128,2,128]{2,1,0:T(2,128)S(1)}, f32[128,2,128]{2,1,0:T(2,128)}, u32[]{:S(2)}) copy-start(f32[128,2,128]{2,1,0:T(2,128)} %copy-done.18) | copy-start | bytes 393220
  1133.6 71.8 %copy-start.8 = (bf16[128,1536]{0,1:T(8,128)(2,1)}, bf16[128,1536]{0,1:T(8,128)(2,1)S(1)}, u32[]{:S(2)}) copy-start(bf16[128,1536]{0,1:T(8,128)(2,1)S(1)} %fusion.36) | copy-start | bytes 1179652
  1205.4 473.7 %reduce-scatter.14.cloned.1.call-start = ((), (), s32[]{:S(2)}) async-start(), calls=%async_computation.14 | async-start | bytes 30965760 | tf_op jit(solution)/shard_map/reduce_scatter | solution.py:155
  1218.7 991.2 %reduce-scatter.12.cloned.1.call-start = ((), (), s32[]{:S(2)}) async-start(), calls=%async_computation.13 | async-start | bytes 61931520 | tf_op jit(solution)/shard_map/reduce_scatter | solution.py:164
  1243.8 1123.9 %all-reduce.11.cloned.1.call-start = ((), (), s32[]{:S(2)}) async-start(), calls=%async_computation.15 | async-start | bytes 23396352 | tf_op jit(solution)/shard_map/psum | solution.py:237
  2223.0 72.6 %copy-start.5 = (f32[128,1536]{1,0:T(8,128)S(1)}, f32[128,1536]{1,0:T(8,128)}, u32[]{:S(2)}) copy-start(f32[128,1536]{1,0:T(8,128)} %copy-done.4) | copy-start | bytes 2359300
  (20 other events, 125.6 us)
Sparse Core Ops, SparseCore 0:
  10.3 89.8 all-gather.6
  106.3 45.5 all-gather.8
  154.2 74.4 all-gather.10
  230.9 535.5 all-gather.12
  768.7 282.5 all-gather.14
  1126.8 69.7 reduce-scatter.5
  1201.7 87.0 reduce-scatter.9
  1293.3 98.1 reduce-scatter.7
  1396.0 282.9 reduce-scatter.13
  1683.4 526.4 reduce-scatter.11
  2212.9 154.7 all-reduce.10
where the time goes:
time: 2400 us; the launch traced here: 2390 us
  waiting for transfers between devices  2060 us (86%)
  matrix products  164 us (7%)
  blocking collectives  97.2 us (4%)
  other arithmetic  35.2 us (1%)
    all_gather x1, waiting for transfers between devices, on_device(): lax.all_gather(w_gate_up, 'group', axis=0, tiled=True)  535 us
    reduce_scatter x1, waiting for transfers between devices, on_device(): lax.psum_scatter(contract_rows(normed_two, grad_gate_up).astype(jnp.bfloa...  531 us
    reduce_scatter x1, waiting for transfers between devices, on_device(): lax.psum_scatter(contract_rows(activated, grad_out).astype(jnp.bfloat16),...  288 us
    all_gather x1, waiting for transfers between devices, on_device(): lax.all_gather(w_down, 'group', axis=0, tiled=True)  259 us
    reduce_scatter x1, waiting for transfers between devices, on_device(): lax.psum_scatter(qkv_grad.astype(jnp.bfloat16), 'group', scatter_dimensio...  103 us
    psum x1, waiting for transfers between devices, on_device(): lax.psum(shards[1].astype(jnp.bfloat16), 'replica').astype(jnp.float32)  70.9 us
    all_gather x1, waiting for transfers between devices, on_device(): lax.all_gather(w_out, 'group', axis=0, tiled=True)  69.5 us
    reduce_scatter x1, waiting for transfers between devices, on_device(): lax.psum_scatter(grad_kv_whole.astype(jnp.bfloat16), 'group', scatter_dim...  63 us
  transfers between devices with their start and end apart: 11, of which 11 were waited for; matrix products, arithmetic and copies ran while one was open for 5% of the time, Pallas kernels for 0%

commit v1 on v0

v1 whole, which is shorter than its diff:
```python
import functools

import jax
import jax.numpy as jnp
from jax import lax
from jax.experimental import pallas as pl
from jax.experimental.pallas import tpu as pltpu
from jax.sharding import Mesh, PartitionSpec as P

D = 1536
HEADS = 12
KV_HEADS = 2
HEAD = 128
FF = 8960
QKV = 2048
ROWS = 128
GROUPS = HEADS // KV_HEADS
WIDTH_Q = HEADS * HEAD
WIDTH_K = KV_HEADS * HEAD
ROLES = 14
COLS = FF // ROLES
SHARD = D // 8
PIECE = COLS // 8
PIECES = FF // 8 // PIECE

NORM_EPSILON = 1e-06
ROPE_BASE = 1000000.0
BF = jnp.bfloat16


def cost(micros):
    return pl.CostEstimate(flops=int(micros * SCALE), bytes_accessed=1000, transcendentals=0)


SCALE = 0.58e9
F32 = jnp.float32

GROUP = ("yh", "x")
PLANE = ("yl", "z")
REPLICA = ("yl", "z", "c")
GROUP_CORE = ("yh", "x", "c")
EVERY = ("yh", "x", "yl", "z", "c")

ALL_OFFSETS = ((0, 0), (0, 1), (0, 3), (1, 0), (0, 2), (1, 1), (1, 3), (1, 2))


def shift_pairs(offset):
    dy, dx = offset
    return [
        (y * 4 + x, ((y + dy) % 2) * 4 + (x + dx) % 4) for y in range(2) for x in range(4)
    ]


def back(offset):
    return (offset[0], (4 - offset[1]) % 4)


def send(block, axes, offset):
    return lax.ppermute(block, axes, shift_pairs(offset))


def send_out(block, axes):
    one, three = send(block, axes, (0, 1)), send(block, axes, (0, 3))
    across, two = send(block, axes, (1, 0)), send(block, axes, (0, 2))
    return [
        block,
        one,
        three,
        across,
        two,
        send(across, axes, (0, 1)),
        send(across, axes, (0, 3)),
        send(two, axes, (1, 0)),
    ]


def send_parts(blocks, axes, hold=()):
    first = (
        send(blocks[1, 1], axes, (0, 1)),
        send(blocks[1, 3], axes, (0, 3)),
        send(blocks[1, 2], axes, (1, 0)),
    )
    from_one, from_three, from_across = after(first, *hold)
    two = (blocks[0, 2].astype(F32) + from_across.astype(F32)).astype(BF)
    across = total([blocks[1, 0], from_one, from_three]).astype(BF)
    parts = [
        blocks[0, 0],
        send(blocks[0, 1], axes, (0, 1)),
        send(blocks[0, 3], axes, (0, 3)),
        send(two, axes, (0, 2)),
        send(across, axes, (1, 0)),
    ]
    return parts, first, (two, across)


def after(value, *done):
    return lax.optimization_barrier((value,) + done)[0] if done else value


def total(blocks):
    out = blocks[0].astype(F32)
    for b in blocks[1:]:
        out = out + b.astype(F32)
    return out


def down_pairs():
    pairs = []
    for r in range(ROLES):
        for g in range(8):
            piece = 8 * r + g
            pairs.append(((piece // PIECES) * 16 + piece % PIECES, g * 16 + r))
    return pairs


def rope_tables(first_row, row_count, head_size):
    half_width = head_size // 2
    position = (first_row + jnp.arange(row_count, dtype=jnp.int32)).astype(F32)
    frequency = jnp.power(
        ROPE_BASE, -(jnp.arange(half_width, dtype=jnp.int32).astype(F32) * 2.0) / head_size
    )
    angles = position[:, None] * frequency[None, :]
    cosine = jnp.concatenate([jnp.cos(angles), jnp.cos(angles)], axis=-1)
    signed = jnp.concatenate([-jnp.sin(angles), jnp.sin(angles)], axis=-1)
    return (cosine, signed)


def contract_rows(left_side, right_side):
    return lax.dot_general(
        left_side, right_side, (((0,), (0,)), ((), ())), preferred_element_type=F32
    )


def contract_cols(left_side, right_side):
    return lax.dot_general(
        left_side, right_side, (((1,), (1,)), ((), ())), preferred_element_type=F32
    )


def swap(block):
    return lax.ppermute(block, "c", [(0, 1), (1, 0)])


def gather_direct(block, axes):
    return lax.all_to_all(jnp.broadcast_to(block[None], (8,) + block.shape), axes, 0, 0, tiled=True)


def place(y, x, offset, sign=1):
    return ((y + sign * offset[0]) % 2) * 4 + (x + sign * offset[1]) % 4


def pick(blocks, index):
    return lax.dynamic_index_in_dim(blocks, index, 0, keepdims=False)


def piece_parts():
    for i in range(5):
        for j in range(6):
            low, high = max(96 * i, 80 * j), min(96 * (i + 1), 80 * (j + 1))
            if low < high:
                yield (
                    (slice(low - 96 * i, high - 96 * i), slice(256 * i, 256 * (i + 1))),
                    (slice(low - 80 * j, high - 80 * j), slice(256 * j, 256 * (j + 1))),
                )


def call(kernel, micros, out_shape, in_specs, *args, vmem=48, **more):
    return pl.pallas_call(
        kernel,
        in_specs=in_specs,
        out_specs=[pl.BlockSpec(memory_space=pltpu.VMEM)] * len(out_shape),
        out_shape=[jax.ShapeDtypeStruct(shape, kind) for shape, kind in out_shape],
        compiler_params=pltpu.CompilerParams(vmem_limit_bytes=vmem << 20),
        cost_estimate=cost(micros),
        **more,
    )(*args)


def pack_kernel(works_ref, gate_ref, up_ref, piece_ref, out_ref):
    works = works_ref[0] > 0
    gate, up = gate_ref[...], up_ref[...]
    out_ref[:SHARD, :COLS] = jnp.where(works, gate, jnp.zeros_like(gate))
    out_ref[:SHARD, COLS:] = jnp.where(works, up, jnp.zeros_like(up))
    for (r, c), (rows, cols) in piece_parts():
        out_ref[SHARD + r.start : SHARD + r.stop, c] = piece_ref[rows, cols]


def arrange_kernel(order_ref, *refs):
    for k in range(8):
        refs[8][order_ref[k]] = refs[k][...]


def arrange(order, blocks):
    return call(
        arrange_kernel,
        2,
        [((8,) + blocks[0].shape, BF)],
        [pl.BlockSpec(memory_space=pltpu.SMEM)] + whole(8),
        order,
        *blocks,
    )[0]


def packed_grads(order_ref, refs, up_sum, down_sum, scratch):
    h_all, c_all, grad, act, sems = scratch
    c_ref, grad_ref, act_ref = refs[8:11]
    copies = fetch(
        [(grad_ref, grad)]
        + [(refs[k], rows_of(h_all, k)) for k in range(8)]
        + [(act_ref, act)]
        + [(c_ref.at[order_ref[k]], rows_of(c_all, k)) for k in range(8)],
        sems,
    )
    for copy in copies[:9]:
        copy.wait()
    up_sum[...] = contract_rows(h_all[...], grad[...]).reshape(8, SHARD, 2 * COLS).astype(BF)
    for copy in copies[9:]:
        copy.wait()
    down_sum[...] = contract_rows(act[...], c_all[...]).astype(BF)


GRAD_SCRATCH = [
    pltpu.VMEM((8 * ROWS, D), BF),
    pltpu.VMEM((8 * ROWS, D), BF),
    pltpu.VMEM((8 * ROWS, 2 * COLS), BF),
    pltpu.VMEM((8 * ROWS, COLS), BF),
    pltpu.SemaphoreType.DMA((18,)),
]


def weight_kernel(order_ref, *refs):
    out_ref, down_sum = refs[11:13]
    packed_grads(order_ref, refs, out_ref.at[:, :SHARD], down_sum, refs[13:])
    for g in range(8):
        for (r, c), (rows, cols) in piece_parts():
            out_ref[g, SHARD + r.start : SHARD + r.stop, c] = down_sum[
                PIECE * g + rows.start : PIECE * g + rows.stop, cols
            ]


def weight_grads(order, h_blocks, cot_all, grads, acts):
    return call(
        weight_kernel,
        10.7,
        [((8, SHARD + 96, 2 * COLS), BF)],
        scalars(1) + anywhere(11),
        order,
        *h_blocks,
        cot_all,
        grads,
        acts,
        scratch_shapes=[pltpu.VMEM((COLS, D), BF)] + GRAD_SCRATCH,
    )[0]


def merge_kernel(token_order_ref, order_ref, *refs):
    given_ref, outs, (up_sum, down_sum, given, sem) = refs[11], refs[12:20], refs[20:24]
    copy = fetch([(given_ref, given)], sem)[0]
    packed_grads(token_order_ref, refs, up_sum, down_sum, refs[24:])
    copy.wait()
    for k in range(8):
        g = order_ref[k]
        outs[k][:SHARD] = (up_sum[g].astype(F32) + given[g, :SHARD].astype(F32)).astype(BF)
        first = pl.multiple_of(g * PIECE, PIECE)
        for (r, c), (rows, cols) in piece_parts():
            to = slice(SHARD + r.start, SHARD + r.stop)
            own = down_sum[pl.ds(first + rows.start, rows.stop - rows.start), cols]
            outs[k][to, c] = (own.astype(F32) + given[g, to, c].astype(F32)).astype(BF)


def merged_grads(token_order, order, h_blocks, cot_all, grads, acts, given):
    return call(
        merge_kernel,
        15,
        [((SHARD + 96, 2 * COLS), BF)] * 8,
        scalars(2) + anywhere(12),
        token_order,
        order,
        *h_blocks,
        cot_all,
        grads,
        acts,
        given,
        vmem=56,
        scratch_shapes=[
            pltpu.VMEM((8, SHARD, 2 * COLS), BF),
            pltpu.VMEM((COLS, D), BF),
            pltpu.VMEM((8, SHARD + 96, 2 * COLS), BF),
            pltpu.SemaphoreType.DMA((1,)),
        ]
        + GRAD_SCRATCH,
    )


def finish_kernel(
    core_ref, grad_ref, mine_ref, other_ref, x_ref, gain_ref, mid_ref, out_ref, gain_grad_ref
):
    half = QKV // 2
    grad = grad_ref[...]
    mine, other = halves(core_ref, grad[:, :half], grad[:, half:])
    normed = contract_cols(mine, mine_ref[...]) + contract_cols(other, other_ref[...])
    x = x_ref[...].astype(F32)
    scale = lax.rsqrt(jnp.mean(x * x, axis=-1, keepdims=True) + NORM_EPSILON)
    gain_grad_ref[...] = jnp.sum(normed * x * scale, axis=0, keepdims=True)
    weighted = normed * gain_ref[...]
    mean = jnp.mean(weighted * x, axis=-1, keepdims=True)
    out_ref[...] = mid_ref[...] + scale * (weighted - x * (scale * scale * mean))


def finish(core, grad_projected, mine, other, rows, gain, grad_middle):
    return call(
        finish_kernel, 5,
        [((ROWS, D), F32), ((1, D), F32)],
        [pl.BlockSpec(memory_space=pltpu.SMEM)] + whole(6),
        core,
        grad_projected,
        mine,
        other,
        rows,
        gain,
        grad_middle,
    )


def attention_grads_kernel(core_ref, normed_ref, att_ref, both_ref, keep_ref, give_ref, bias_ref):
    both = both_ref[...].reshape(8 * ROWS, 512)
    role = both[:, :256]
    bias_ref[...] = jnp.sum(role.astype(F32), axis=0, keepdims=True)
    qkv = contract_rows(normed_ref[...].reshape(8 * ROWS, D), role)
    out = contract_rows(att_ref[...].reshape(8 * ROWS, D), both[:, 256:])
    keep, give = halves(core_ref, qkv, out)
    keep_ref[...] = keep
    give_ref[...] = give.astype(BF)


def attention_grads(core, normed, attended, both):
    return call(
        attention_grads_kernel,
        5,
        [((D, 256), F32), ((D, 256), BF), ((1, 256), F32)],
        [pl.BlockSpec(memory_space=pltpu.SMEM)] + whole(3),
        core,
        normed,
        attended,
        both,
    )


def last_kernel(core_ref, group_ref, mine_ref, other_ref, qkv_ref, out_ref, gain_ref, bias_ref):
    gains = jnp.zeros((16, 256), F32)
    for q in range(8):
        mine, other = mine_ref[q].astype(F32), other_ref[q].astype(F32)
        qkv, out = halves(core_ref, mine[:SHARD], other[:SHARD])
        qkv_ref[:, 256 * q : 256 * (q + 1)] = qkv
        if q < 6:
            out_ref[:, 256 * q : 256 * (q + 1)] = out
        gains = gains + mine[SHARD:] + other[SHARD:]
    gain_ref[...] = gains
    g = group_ref[0]
    bias_ref[...] = mine_ref[g, SHARD:].astype(F32) + other_ref[g, SHARD:].astype(F32)


def payload_kernel(keep_ref, other_ref, extra_ref, bias_ref, out_ref):
    row = lax.broadcasted_iota(jnp.int32, (16, 256), 0)
    bias = bias_ref[...].astype(BF).astype(F32)
    for g in range(8):
        rows = slice(SHARD * g, SHARD * (g + 1))
        out_ref[g, :SHARD] = (keep_ref[rows] + other_ref[rows].astype(F32)).astype(BF)
        extra = extra_ref[g].astype(F32)
        out_ref[g, SHARD:] = jnp.where(row == 2, bias, extra).astype(BF)


def sum_kernel(in_ref, out_ref):
    rows = in_ref[0].astype(F32)
    for g in range(1, 8):
        rows = rows + in_ref[g].astype(F32)
    rows = rows.astype(BF)
    for g in range(8):
        out_ref[g] = rows


def write_kernel(low, count, held, core_ref, order_ref, *refs):
    blocks = refs[: 2 * count]
    wide_out, down_out, narrow, wide, down, in_sems, sems = refs[2 * count + held :]
    arrivals = fetch([(blocks[n], narrow.at[n]) for n in range(2 * count)], in_sems)
    for start in (True, False):
        for n in range(2 * count):
            chip = order_ref[low + n % count]
            role = 2 * chip + (core_ref[0] if n < count else 1 - core_ref[0])
            if start:
                arrivals[n].wait()

            @pl.when(chip < ROLES // 2)
            def _(n=n, role=role):
                copies = [
                    pltpu.make_async_copy(
                        wide.at[n, :, :COLS],
                        wide_out.at[:, pl.ds(pl.multiple_of(role * COLS, 128), COLS)],
                        sems.at[n, 0],
                    ),
                    pltpu.make_async_copy(
                        wide.at[n, :, COLS:],
                        wide_out.at[:, pl.ds(pl.multiple_of(FF + role * COLS, 128), COLS)],
                        sems.at[n, 1],
                    ),
                    pltpu.make_async_copy(
                        down.at[n],
                        down_out.at[pl.ds(pl.multiple_of(role * PIECE, PIECE), PIECE)],
                        sems.at[n, 2],
                    ),
                ]
                if start:
                    wide[n] = narrow[n, :SHARD].astype(F32)
                    copies[0].start()
                    copies[1].start()
                    for (r, c), (rows, cols) in piece_parts():
                        down[n, rows, cols] = narrow[
                            n, SHARD + r.start : SHARD + r.stop, c
                        ].astype(F32)
                    copies[2].start()
                else:
                    for copy in copies:
                        copy.wait()


def write_grads(core, order, mine, other, low, high, held):
    count = high - low
    return pl.pallas_call(
        functools.partial(write_kernel, low, count, len(held)),
        in_specs=scalars(2) + anywhere(2 * count + len(held)),
        out_specs=anywhere(2),
        out_shape=[
            jax.ShapeDtypeStruct((SHARD, 2 * FF), F32),
            jax.ShapeDtypeStruct((FF // 8, D), F32),
        ],
        scratch_shapes=[
            pltpu.VMEM((2 * count, SHARD + 96, 2 * COLS), BF),
            pltpu.VMEM((2 * count, SHARD, 2 * COLS), F32),
            pltpu.VMEM((2 * count, PIECE, D), F32),
            pltpu.SemaphoreType.DMA((2 * count,)),
            pltpu.SemaphoreType.DMA((2 * count, 3)),
        ],
        input_output_aliases={2 + 2 * count + k: k for k in range(len(held))},
        compiler_params=pltpu.CompilerParams(vmem_limit_bytes=48 << 20),
        cost_estimate=cost(2 * count),
    )(core, order, *mine[low:high], *other[low:high], *held)


def project_kernel(order_ref, gain_ref, w_ref, bias_ref, cos_ref, sin_ref, *refs):
    normed_ref, heads_ref, x_all, sems = refs[8:]
    copies = fetch([(refs[k], x_all.at[k]) for k in range(8)], sems)
    for k in range(8):
        copies[k].wait()
        rows = x_all[k].astype(F32)
        scale = lax.rsqrt(jnp.mean(rows * rows, axis=-1, keepdims=True) + NORM_EPSILON)
        normed = (rows * scale * gain_ref[...]).astype(BF)
        at = order_ref[k]
        normed_ref[at] = normed
        out = jnp.dot(normed, w_ref[...], preferred_element_type=F32) + bias_ref[...]
        for h in range(2):
            u = out[:, HEAD * h : HEAD * (h + 1)]
            u = u * cos_ref[...] + pltpu.roll(u, HEAD // 2, 1) * sin_ref[...]
            heads_ref[at, :, HEAD * h : HEAD * (h + 1)] = u.astype(BF)


def whole(count):
    return [pl.BlockSpec(memory_space=pltpu.VMEM)] * count


def scalars(count):
    return [pl.BlockSpec(memory_space=pltpu.SMEM)] * count


def anywhere(count):
    return [pl.BlockSpec(memory_space=pl.ANY)] * count


def fetch(pairs, sems):
    copies = [
        pltpu.make_async_copy(source, target, sems.at[k]) for k, (source, target) in enumerate(pairs)
    ]
    for copy in copies:
        copy.start()
    return copies


def rows_of(ref, k):
    return ref.at[ROWS * k : ROWS * (k + 1)]


def project(order, gain, weight, bias, cosine, signed, blocks):
    return pl.pallas_call(
        project_kernel,
        in_specs=scalars(1) + whole(5) + anywhere(8),
        out_specs=whole(2),
        out_shape=[
            jax.ShapeDtypeStruct((8, ROWS, D), BF),
            jax.ShapeDtypeStruct((8, ROWS, 256), BF),
        ],
        scratch_shapes=[pltpu.VMEM((8, ROWS, D), BF), pltpu.SemaphoreType.DMA((8,))],
        compiler_params=pltpu.CompilerParams(vmem_limit_bytes=32 << 20),
        cost_estimate=cost(4),
    )(order, gain, weight, bias, cosine, signed, *blocks)


def head_stack(ref, side):
    return jnp.concatenate(
        [
            ref[h // 2, :, HEAD * (h % 2) : HEAD * (h % 2 + 1)]
            for h in range(GROUPS * side, GROUPS * (side + 1))
        ],
        axis=0,
    )


def scores_of(me_ref, queries, keys):
    raw = lax.dot_general(
        queries, keys, (((1,), (1,)), ((), ())), preferred_element_type=F32
    )
    raw = raw.reshape(GROUPS, ROWS, 8 * ROWS) * HEAD ** (-0.5)
    row = me_ref[0] * ROWS + lax.broadcasted_iota(jnp.int32, (ROWS, 8 * ROWS), 0)
    col = lax.broadcasted_iota(jnp.int32, (ROWS, 8 * ROWS), 1)
    return jnp.where((col <= row)[None], raw, -1e30)


def attend_kernel(me_ref, heads_ref, kv_ref, out_ref, log_ref):
    kv = kv_ref[...].reshape(8 * ROWS, 512)
    for side in range(2):
        keys = kv[:, HEAD * side : HEAD * (side + 1)]
        values = kv[:, 256 + HEAD * side : 256 + HEAD * (side + 1)]
        scores = scores_of(me_ref, head_stack(heads_ref, side), keys)
        top = jnp.max(scores, axis=-1, keepdims=True)
        exponent = jnp.exp(scores - top)
        row_total = jnp.sum(exponent, axis=-1, keepdims=True)
        mixed = jnp.dot(
            exponent.astype(BF).reshape(GROUPS * ROWS, 8 * ROWS),
            values,
            preferred_element_type=F32,
        ).reshape(GROUPS, ROWS, HEAD)
        mixed = mixed / row_total
        logs = top + jnp.log(row_total)
        for i in range(GROUPS):
            h = GROUPS * side + i
            out_ref[:, HEAD * h : HEAD * (h + 1)] = mixed[i].astype(BF)
            log_ref[h] = logs[i]


def attend(me, heads, kv):
    return pl.pallas_call(
        attend_kernel,
        in_specs=[pl.BlockSpec(memory_space=pltpu.SMEM)] + whole(2),
        out_specs=whole(2),
        out_shape=[
            jax.ShapeDtypeStruct((ROWS, WIDTH_Q), BF),
            jax.ShapeDtypeStruct((HEADS, ROWS, 1), F32),
        ],
        compiler_params=pltpu.CompilerParams(vmem_limit_bytes=48 << 20),
        cost_estimate=cost(5),
    )(me, heads, kv)


def attend_back_kernel(
    me_ref, heads_ref, kv_ref, grad_ref, log_ref, cos_ref, sin_ref, dq_ref, dkv_ref
):
    kv = kv_ref[...].reshape(8 * ROWS, 512)
    for side in range(2):
        keys = kv[:, HEAD * side : HEAD * (side + 1)]
        values = kv[:, 256 + HEAD * side : 256 + HEAD * (side + 1)]
        queries = head_stack(heads_ref, side)
        grads = jnp.concatenate(
            [
                grad_ref[:, HEAD * h : HEAD * (h + 1)]
                for h in range(GROUPS * side, GROUPS * (side + 1))
            ],
            axis=0,
        )
        scores = scores_of(me_ref, queries, keys)
        probs = jnp.exp(scores - log_ref[GROUPS * side : GROUPS * (side + 1)])
        grad_probs = contract_cols(grads, values).reshape(GROUPS, ROWS, 8 * ROWS)
        inner = jnp.sum(probs * grad_probs, axis=-1, keepdims=True)
        grad_scores = (probs * (grad_probs - inner)).astype(BF)
        grad_scores = grad_scores.reshape(GROUPS * ROWS, 8 * ROWS)
        probs_low = probs.astype(BF).reshape(GROUPS * ROWS, 8 * ROWS)
        dq = jnp.dot(grad_scores, keys, preferred_element_type=F32) * HEAD ** (-0.5)
        dk = contract_rows(grad_scores, queries) * HEAD ** (-0.5)
        dv = contract_rows(probs_low, grads)
        for i in range(GROUPS):
            h = GROUPS * side + i
            u = dq[ROWS * i : ROWS * (i + 1)]
            u = u * cos_ref[...] - pltpu.roll(u, HEAD // 2, 1) * sin_ref[...]
            dq_ref[:, HEAD * h : HEAD * (h + 1)] = u.astype(BF)
        low, high = HEAD * side, HEAD * (side + 1)
        dkv_ref[:, :, low:high] = dk.astype(BF).reshape(8, ROWS, HEAD)
        dkv_ref[:, :, 256 + low : 256 + high] = dv.astype(BF).reshape(8, ROWS, HEAD)


def attend_back(me, heads, kv, grads, logs, cosine, signed):
    return pl.pallas_call(
        attend_back_kernel,
        in_specs=[pl.BlockSpec(memory_space=pltpu.SMEM)] + whole(6),
        out_specs=whole(2),
        out_shape=[
            jax.ShapeDtypeStruct((ROWS, WIDTH_Q), BF),
            jax.ShapeDtypeStruct((8, ROWS, 512), BF),
        ],
        compiler_params=pltpu.CompilerParams(vmem_limit_bytes=56 << 20),
        cost_estimate=cost(9),
    )(me, heads, kv, grads, logs, cosine, signed)


def halves(core_ref, mine, other):
    first = core_ref[0] == 0
    return jnp.where(first, mine, other), jnp.where(first, other, mine)


def middle_kernel(
    core_ref, att_ref, x_ref, gain_ref, mine_ref, other_ref, mid_ref, scale_ref, h_ref
):
    att = att_ref[...]
    mine = jnp.dot(att, mine_ref[...], preferred_element_type=F32)
    other = jnp.dot(att, other_ref[...], preferred_element_type=F32)
    low, high = halves(core_ref, mine, other)
    low = x_ref[:, : D // 2].astype(F32) + low
    high = x_ref[:, D // 2 :].astype(F32) + high
    square = jnp.sum(low * low, axis=-1, keepdims=True) + jnp.sum(
        high * high, axis=-1, keepdims=True
    )
    scale = lax.rsqrt(square / D + NORM_EPSILON)
    scale_ref[...] = scale
    mid_ref[:, : D // 2] = low
    mid_ref[:, D // 2 :] = high
    h_ref[:, : D // 2] = (low * scale * gain_ref[:, : D // 2]).astype(BF)
    h_ref[:, D // 2 :] = (high * scale * gain_ref[:, D // 2 :]).astype(BF)


def middle_of(core, attended, rows, gain, mine, other):
    return pl.pallas_call(
        middle_kernel,
        in_specs=[pl.BlockSpec(memory_space=pltpu.SMEM)]
        + whole(5),
        out_specs=whole(3),
        out_shape=[
            jax.ShapeDtypeStruct((ROWS, D), F32),
            jax.ShapeDtypeStruct((ROWS, 1), F32),
            jax.ShapeDtypeStruct((ROWS, D), BF),
        ],
        compiler_params=pltpu.CompilerParams(vmem_limit_bytes=24 << 20),
        cost_estimate=cost(3),
    )(core, attended, rows, gain, mine, other)


def turning_kernel(core_ref, mid_ref, scale_ref, gain_ref, cot_ref, mine_ref, other_ref, *refs):
    mid_grad_ref, branch_ref, att_ref, gain_grad_ref, arrived, sems = refs[5:]
    copies = fetch([(refs[k], arrived.at[k]) for k in range(5)], sems)
    for copy in copies:
        copy.wait()
    grad = arrived[0].astype(F32)
    for k in range(1, 5):
        grad = grad + arrived[k].astype(F32)
    mid, scale = mid_ref[...], scale_ref[...]
    gain_grad_ref[...] = jnp.sum(grad * mid * scale, axis=0, keepdims=True)
    weighted = grad * gain_ref[...]
    mean = jnp.mean(weighted * mid, axis=-1, keepdims=True)
    grad = cot_ref[...].astype(F32) + scale * (weighted - mid * (scale * scale * mean))
    mid_grad_ref[...] = grad
    branch = grad.astype(BF)
    branch_ref[...] = branch
    mine, other = halves(core_ref, branch[:, : D // 2], branch[:, D // 2 :])
    att = contract_cols(mine, mine_ref[...]) + contract_cols(other, other_ref[...])
    att_ref[...] = att.astype(BF)


def turning(core, middle, scale, gain, cotangent, mine, other, parts):
    return pl.pallas_call(
        turning_kernel,
        in_specs=[pl.BlockSpec(memory_space=pltpu.SMEM)]
        + whole(6)
        + anywhere(5),
        out_specs=whole(4),
        out_shape=[
            jax.ShapeDtypeStruct((ROWS, D), F32),
            jax.ShapeDtypeStruct((ROWS, D), BF),
            jax.ShapeDtypeStruct((ROWS, D), BF),
            jax.ShapeDtypeStruct((1, D), F32),
        ],
        scratch_shapes=[pltpu.VMEM((5, ROWS, D), BF), pltpu.SemaphoreType.DMA((5,))],
        compiler_params=pltpu.CompilerParams(vmem_limit_bytes=32 << 20),
        cost_estimate=cost(4.2),
    )(core, middle, scale, gain, cotangent, mine, other, *parts)


def feed_kernel(held, order_ref, *refs):
    h_refs, c_ref, weights = refs[:4], refs[4], refs[5:7]
    up_w, packed, down_w, h_all, c_all, total_ref, rows_ref, sems, row_sems, in_sems = refs[-10:]
    outs = refs[7 + held : -10]
    act_refs, grad_refs, out_ref, part_refs = outs[:2], outs[2:4], outs[4], outs[5:]
    first = 4 if held else 0
    copies = []
    for side in range(2):
        for n, (rows, target) in enumerate(
            ((slice(0, SHARD), up_w), (slice(SHARD, SHARD + 96), packed))
        ):
            copy = pltpu.make_async_copy(
                weights[side].at[:, rows], target.at[side], sems.at[side, n]
            )
            copy.start()
            copies.append(copy)
    tokens = fetch(
        [(h_refs[i], rows_of(h_all, i)) for i in range(4)]
        + [(c_ref.at[order_ref[first + i]], rows_of(c_all, i)) for i in range(4)],
        in_sems,
    )
    for copy in tokens:
        copy.wait()
    for side in range(2):
        grad_ref = grad_refs[side]
        copies[2 * side].wait()
        up_now = up_w[side].reshape(D, 2 * COLS)
        gate_up = jnp.dot(h_all[...], up_now, preferred_element_type=F32)
        copies[2 * side + 1].wait()
        for g in range(8):
            for (r, c), (rows, cols) in piece_parts():
                down_w[PIECE * g + rows.start : PIECE * g + rows.stop, cols] = packed[side, g, r, c]
        grad_act = contract_cols(c_all[...], down_w[...])
        gate, up = gate_up[:, :COLS], gate_up[:, COLS:]
        sig = jax.nn.sigmoid(gate)
        silu = gate * sig
        act_refs[side][...] = (silu * up).astype(BF)
        rows = jnp.dot(act_refs[side][...], down_w[...], preferred_element_type=F32)
        grad_ref[:, :COLS] = (grad_act * up * sig * (1.0 + gate * (1.0 - sig))).astype(BF)
        grad_ref[:, COLS:] = (grad_act * silu).astype(BF)
        if side == 0:
            total_ref[...] = rows
            part = contract_cols(grad_ref[...], up_now)
        else:
            rows_ref[...] = (total_ref[...] + rows).astype(BF)
            copies = []
            for i in range(4):
                copy = pltpu.make_async_copy(
                    rows_ref.at[ROWS * i : ROWS * (i + 1)],
                    out_ref.at[order_ref[first + i]],
                    row_sems.at[i],
                )
                copy.start()
                copies.append(copy)
            part = part + contract_cols(grad_ref[...], up_now)
            for i in range(4):
                part_refs[i][...] = part[ROWS * i : ROWS * (i + 1)].astype(BF)
            for copy in copies:
                copy.wait()


def feed(order, h_blocks, cot_all, mine, other, held):
    tokens = 4 * ROWS
    at = 1 if held else 0
    widths = (COLS, COLS, 2 * COLS, 2 * COLS)
    outs = pl.pallas_call(
        functools.partial(feed_kernel, len(held)),
        grid=(1,),
        in_specs=scalars(1) + anywhere(7 + len(held)),
        out_specs=[pl.BlockSpec((tokens, w), lambda i: (at, 0)) for w in widths]
        + anywhere(1)
        + whole(4),
        out_shape=[jax.ShapeDtypeStruct((2 * tokens, w), BF) for w in widths]
        + [jax.ShapeDtypeStruct((8, ROWS, D), BF)]
        + [jax.ShapeDtypeStruct((ROWS, D), BF)] * 4,
        scratch_shapes=[
            pltpu.VMEM((2, 8, SHARD, 2 * COLS), BF),
            pltpu.VMEM((2, 8, 96, 2 * COLS), BF),
            pltpu.VMEM((COLS, D), BF),
            pltpu.VMEM((tokens, D), BF),
            pltpu.VMEM((tokens, D), BF),
            pltpu.VMEM((tokens, D), F32),
            pltpu.VMEM((tokens, D), BF),
            pltpu.SemaphoreType.DMA((2, 2)),
            pltpu.SemaphoreType.DMA((4,)),
            pltpu.SemaphoreType.DMA((8,)),
        ],
        input_output_aliases={8 + k: k for k in range(len(held))},
        compiler_params=pltpu.CompilerParams(vmem_limit_bytes=56 << 20),
        cost_estimate=cost(21),
    )(order, *h_blocks, cot_all, mine, other, *held)
    return tuple(outs[:5]), outs[5:]


def assemble_kernel(dq_ref, dkv_ref, branch_ref, cos_ref, sin_ref, both_ref, out_ref):
    dkv = dkv_ref[0].astype(F32)
    for k in range(1, 8):
        dkv = dkv + dkv_ref[k].astype(F32)
    for h in range(2):
        u = dkv[:, HEAD * h : HEAD * (h + 1)]
        u = u * cos_ref[...] - pltpu.roll(u, HEAD // 2, 1) * sin_ref[...]
        u = u.astype(BF)
        both_ref[6, :, HEAD * h : HEAD * (h + 1)] = u
        out_ref[:, WIDTH_Q + HEAD * h : WIDTH_Q + HEAD * (h + 1)] = u
    u = dkv[:, 256:].astype(BF)
    both_ref[7, :, :256] = u
    out_ref[:, WIDTH_Q + 256 :] = u
    for q in range(6):
        u = dq_ref[:, 256 * q : 256 * (q + 1)]
        both_ref[q, :, :256] = u
        out_ref[:, 256 * q : 256 * (q + 1)] = u
        both_ref[q, :, 256:] = branch_ref[:, 256 * q : 256 * (q + 1)]
    for q in range(6, 8):
        both_ref[q, :, 256:] = jnp.zeros((ROWS, 256), BF)


def assemble(dq, dkv, branch, cosine, signed):
    return pl.pallas_call(
        assemble_kernel,
        in_specs=whole(5),
        out_specs=whole(2),
        out_shape=[
            jax.ShapeDtypeStruct((8, ROWS, 512), BF),
            jax.ShapeDtypeStruct((ROWS, QKV), BF),
        ],
        compiler_params=pltpu.CompilerParams(vmem_limit_bytes=16 << 20),
        cost_estimate=cost(1.2),
    )(dq, dkv, branch, cosine, signed)


def on_device(hidden_in, norm_attn, w_qkv, b_qkv, w_out, norm_mlp, w_gate_up, w_down, cotangent):
    core = lax.axis_index("c")
    plane = lax.axis_index(PLANE)
    replica = lax.axis_index(REPLICA)
    group = lax.axis_index(GROUP)
    yl, zz = lax.axis_index("yl"), lax.axis_index("z")
    yh, xx = lax.axis_index("yh"), lax.axis_index("x")
    first_row = group * ROWS
    works = replica < ROLES
    role = jnp.minimum(replica, ROLES - 1)

    x_blocks = send_out(hidden_in[0], PLANE)
    pad = jnp.zeros((64,), BF)
    small = jnp.concatenate([b_qkv, norm_attn, pad, norm_mlp, pad]).reshape(3, 256)
    columns = lax.dynamic_slice(w_qkv, (0, plane * 256), (SHARD, 256))
    columns = jnp.concatenate([columns, small, jnp.zeros((13, 256), BF)], axis=0)
    columns = gather_direct(after(columns, *x_blocks[1:5]), GROUP)
    columns = after(columns, *x_blocks[5:])
    qkv_role = columns[:, :SHARD].reshape(D, 256)
    bias_full = columns[:, SHARD : SHARD + 1].astype(F32)
    gain_one = columns[:, SHARD + 1, :SHARD].reshape(1, D).astype(F32)
    gain_two = columns[:, SHARD + 2, :SHARD].reshape(1, D).astype(F32)

    out_half = lax.dynamic_slice(w_out, (0, core * 768), (SHARD, 768))
    out_mine = lax.all_gather(out_half, GROUP, axis=0, tiled=True)
    piece = lax.dynamic_slice(w_down, (role * PIECE, 0), (PIECE, D))
    piece = lax.ppermute(piece, EVERY, down_pairs())
    (packed,) = call(
        pack_kernel,
        1,
        [((SHARD + 96, 2 * COLS), BF)],
        scalars(1) + whole(3),
        works.astype(jnp.int32).reshape(1),
        lax.dynamic_slice(w_gate_up, (0, role * COLS), (SHARD, COLS)),
        lax.dynamic_slice(w_gate_up, (0, FF + role * COLS), (SHARD, COLS)),
        piece,
    )
    feed_mine = lax.all_gather(after(packed, x_blocks[1]), GROUP, axis=0)

    cosine, signed = rope_tables(first_row, ROWS, HEAD)
    turns = plane < 7
    order = jnp.stack([place(yl, zz, o, -1) for o in ALL_OFFSETS]).astype(jnp.int32)
    normed_one_all, heads = project(
        order,
        gain_one,
        qkv_role,
        pick(bias_full, plane),
        jnp.where(turns, cosine, 1.0),
        jnp.where(turns, signed, 0.0),
        x_blocks,
    )

    heads = lax.all_to_all(heads, PLANE, 0, 0, tiled=True)
    out_other = swap(after(out_mine, heads))
    grad_out = cotangent[0]
    cot_blocks = send_out(after(grad_out, *x_blocks), PLANE)
    kv_own = jnp.concatenate([heads[6], heads[7]], axis=1)
    kv_own = after(kv_own, *cot_blocks[1:5])
    kv_all = gather_direct(kv_own, GROUP)
    kv_all = after(kv_all, *cot_blocks)
    cot_all = arrange(order, cot_blocks)
    me = group.astype(jnp.int32).reshape(1)
    attended, logs = attend(me, heads, kv_all)
    which = core.astype(jnp.int32).reshape(1)
    middle, scale_two, normed_two = middle_of(
        which, attended, hidden_in[0], gain_two, out_mine, out_other
    )

    h_blocks = send_out(normed_two, PLANE)
    feed_other = swap(after(feed_mine, *h_blocks[1:3]))
    attended_all = lax.all_gather(after(attended, *h_blocks[1:5]), PLANE, axis=0)
    qkv_half = lax.dynamic_slice(w_qkv, (0, core * 1024), (SHARD, 1024))
    qkv_mine = lax.all_gather(after(qkv_half, *h_blocks[1:5]), GROUP, axis=0, tiled=True)
    held, back_blocks = (), {}
    for part in (slice(0, 4), slice(4, 8)):
        held, parts = feed(order, h_blocks[part], cot_all, feed_mine, feed_other, held)
        for o, block in zip(ALL_OFFSETS[part], parts):
            back_blocks[back(o)] = block
    second_parts, _, round_sums = send_parts(back_blocks, PLANE)

    held_h = after(tuple(h_blocks), parts, attended_all)
    given = weight_grads(order, held_h, cot_all, held[3], held[1])
    group_order = jnp.stack([place(yh, xx, o) for o in ALL_OFFSETS]).astype(jnp.int32)
    merged = merged_grads(
        order, group_order, after(held_h, qkv_mine), cot_all, held[2], held[0], swap(given)
    )
    second_parts = after(second_parts, merged)
    grad_middle, grad_branch, grad_attended, gain_two_grad = turning(
        which, middle, scale_two, gain_two, grad_out, out_mine, out_other, second_parts
    )
    grad_q, grad_kv = attend_back(me, heads, kv_all, grad_attended, logs, cosine, signed)
    mlp_parts, mlp_first, _ = send_parts(
        dict(zip(ALL_OFFSETS, merged)), GROUP
    )
    grad_kv = after(grad_kv, *mlp_first)
    grad_kv = lax.all_to_all(grad_kv, GROUP, 0, 0, tiled=True)

    out_rows = after(held[4], *second_parts).reshape(8 * ROWS, D)
    out_rows = lax.psum_scatter(out_rows, PLANE, scatter_dimension=0, tiled=True)
    result = (middle + out_rows.astype(F32)).astype(BF)[None]
    grad_kv = after(grad_kv, out_rows)

    both, grad_projected = assemble(grad_q, grad_kv, grad_branch, cosine, signed)
    qkv_other = swap(after(qkv_mine, both))
    assembled = both
    both = lax.all_to_all(both, PLANE, 0, 0, tiled=True)

    mlp_grad = total(after(tuple(mlp_parts), assembled)).astype(BF)
    down_grad = lax.ppermute(mlp_grad[SHARD:], EVERY, [(t, s) for s, t in down_pairs()])
    mlp_grad = jnp.concatenate([mlp_grad[:SHARD], down_grad], axis=0)
    grad_blocks = send_out(mlp_grad, PLANE)
    other_blocks = [swap(b) for b in grad_blocks]
    feed_grads = write_grads(which, order, grad_blocks, other_blocks, 0, 5, ())
    gate_up_grad, down_grad = write_grads(which, order, grad_blocks, other_blocks, 5, 8, feed_grads)

    grad_in, gain_one_grad = finish(
        which, grad_projected, qkv_mine, qkv_other, hidden_in[0], gain_one, grad_middle
    )
    gains = jnp.stack([gain_one_grad[0], gain_two_grad[0]]).astype(BF).reshape(2, 8, SHARD)
    gains = jnp.pad(gains.transpose(1, 0, 2), ((0, 0), (0, 14), (0, 64)))
    keep, give, bias_grad = attention_grads(which, normed_one_all, attended_all, both)
    (payload,) = call(
        payload_kernel, 1.4,
        [((8, SHARD + 16, 256), BF)],
        whole(4),
        keep,
        swap(give),
        gains,
        bias_grad,
    )
    payload = lax.all_to_all(payload, GROUP, 0, 0, tiled=True)
    (payload,) = call(sum_kernel, 1, [((8, SHARD + 16, 256), BF)], whole(1), payload)
    mine = lax.all_to_all(payload, PLANE, 0, 0, tiled=True)
    mine = after(mine, *feed_grads)
    other = swap(mine)
    qkv_grad, out_grad, gains, bias_grad = call(
        last_kernel,
        3,
        [((SHARD, QKV), F32), ((SHARD, D), F32), ((16, 256), F32), ((16, 256), F32)],
        [pl.BlockSpec(memory_space=pltpu.SMEM)] * 2 + whole(2),
        which,
        me,
        mine,
        other,
    )

    return (
        result,
        grad_in[None],
        gains[0, :SHARD],
        qkv_grad,
        bias_grad[2],
        out_grad,
        gains[1, :SHARD],
        gate_up_grad,
        down_grad,
    )


def solution(mesh):
    fine = Mesh(mesh.devices.reshape(2, 4, 2, 4, 2), EVERY)
    tokens = P(REPLICA, GROUP, None)
    matrix = P(GROUP, None)
    vector = P(GROUP)
    return jax.shard_map(
        on_device,
        mesh=fine,
        in_specs=(tokens, vector, matrix, vector, matrix, vector, matrix, matrix, tokens),
        out_specs=(tokens, tokens, vector, matrix, vector, matrix, vector, matrix, matrix),
        check_vma=False,
    )
```

time: 2400 us -> 562 us (0.23)
  the two profiles are of different devices: /device:TPU:7 before, /device:TPU:25 now
where the time goes in v1:
time: 562 us; the launch traced here: 552 us
  waiting for transfers between devices  200 us (36%)
  Pallas kernels  138 us (25%)
  starting transfers between devices  129 us (23%)
  local copies, waits for them, and re-layouts  41.6 us (7%)
  other arithmetic  14.9 us (3%)
  between operations  14.9 us (3%)
  blocking collectives  13.7 us (2%)
    ppermute x42, waiting for transfers between devices, send(): return lax.ppermute(block, axes, shift_pairs(offset))  120 us
    ppermute x42, starting transfers between devices, send(): return lax.ppermute(block, axes, shift_pairs(offset))  63.6 us
    pallas_call x2, Pallas kernels, feed(): pl.pallas_call(functools.partial(feed_kernel, len(held)), grid=(1,), in_s...  49.3 us
    pallas_call x9, Pallas kernels, call(): pl.pallas_call(kernel, in_specs=in_specs, out_specs=[pl.BlockSpec(memory_...  47 us
    all_gather x1, waiting for transfers between devices, on_device(): lax.all_gather(after(qkv_half, *h_blocks[1:5]), GROUP, axis=0, tiled=True)  34.9 us
    unnamed x114, local copies, waits for them, and re-layouts  27.3 us
    reduce_scatter x1, waiting for transfers between devices, on_device(): lax.psum_scatter(out_rows, PLANE, scatter_dimension=0, tiled=True)  20.8 us
    ppermute x14, starting transfers between devices, swap(): return lax.ppermute(block, 'c', [(0, 1), (1, 0)])  19.1 us
  transfers between devices with their start and end apart: 69, of which 28 were waited for; matrix products, arithmetic and copies ran while one was open for 5% of the time, Pallas kernels for 25%

profile of v1, /device:TPU:25, one launch (start us, length us, event | category | flops | bytes accessed | tf_op | source)
XLA Modules:
  0.0 551.7 jit_solution(11609377328920164602)
XLA Ops:
  27.5 6.0 %collective-permute-start.2 = (bf16[128,1536]{1,0:T(8,128)(2,1)S(1)}, bf16[128,1536]{1,0:T(8,128)(2,1)S(1)}, u32[]{:S(2)}, u32[]{:S(2)}) collective-permute-start(bf16[128,1536]{1,0:T(8,128)(2,1)S(1)} %bitcast.48), channel_id=1, source_target_pairs={{0,8},{2,10},{4,12},{6,14},{8,0},{10,2},{12,4},{14,6},{1,9},{3,11}... | collective-permute-start | bytes 1179656 | tf_op jit(solution)/shard_map/ppermute | solution.py:59
  63.4 13.3 %collective-permute-done.6.refs_7_ = bf16[128,1536]{1,0:T(8,128)(2,1)S(1)} collective-permute-done((bf16[128,1536]{1,0:T(8,128)(2,1)S(1)}, bf16[128,1536]{1,0:T(8,128)(2,1)S(1)}, u32[]{:S(2)}, u32[]{:S(2)}) %collective-permute-start.6) | collective-permute-done | bytes 393248 | tf_op jit(solution)/shard_map/ppermute | solution.py:59
  83.0 6.2 %shard_map.160 = (bf16[8,128,1536]{2,1,0:T(8,128)(2,1)S(1)}, bf16[8,128,256]{2,1,0:T(8,128)(2,1)S(1)}) custom-call(s32[8]{0:T(128)S(1)} %stack.69.order_ref.token_order_ref, f32[1,1536]{1,0:T(1,128)S(1)} %reshape.93.gain_ref, bf16[1536,256]{1,0:T(8,128)(2,1)S(1)} %bitcast.39, f32[1,256]{1,0:T(1,128)S(1)} %fusion.3.bias_ref, ...), custom_call_target="tpu_custom_call" | custom-call | flops 2320000000 | bytes 1000 | tf_op jit(solution)/shard_map/pallas_call | solution.py:492
  90.8 13.7 %all_to_all.35.heads_ref = bf16[8,128,256]{2,1,0:T(8,128)(2,1)S(1)} all-to-all(bf16[8,128,256]{2,1,0:T(8,128)(2,1)S(1)} %get-tuple-element.106), channel_id=1, replica_groups=mesh['yh'=2,'x'=4,'yl'=2,'z'=4,'c'=2] {'yl','z'}, dimensions={0} | all-to-all | bytes 1048576 | tf_op jit(solution)/shard_map/all_to_all | solution.py:874
  111.7 7.1 %collective-permute-done.7.refs_1_ = bf16[128,1536]{1,0:T(8,128)(2,1)S(1)} collective-permute-done((bf16[128,1536]{1,0:T(8,128)(2,1)S(1)}, bf16[128,1536]{1,0:T(8,128)(2,1)S(1)}, u32[]{:S(2)}, u32[]{:S(2)}) %collective-permute-start.7) | collective-permute-done | bytes 393248 | tf_op jit(solution)/shard_map/ppermute | solution.py:59
  120.1 6.8 %collective-permute-done.10.refs_4_ = bf16[128,1536]{1,0:T(8,128)(2,1)S(1)} collective-permute-done((bf16[128,1536]{1,0:T(8,128)(2,1)S(1)}, bf16[128,1536]{1,0:T(8,128)(2,1)S(1)}, u32[]{:S(2)}, u32[]{:S(2)}) %collective-permute-start.10) | collective-permute-done | bytes 393248 | tf_op jit(solution)/shard_map/ppermute | solution.py:59
  128.0 6.6 %all-to-all-start.2 = ((bf16[8,128,512]{2,1,0:T(8,128)(2,1)}), bf16[8,128,512]{2,1,0:T(8,128)(2,1)S(1)}, u32[]{:S(2)}, u32[]{:S(2)}) async-start(bf16[8,128,512]{2,1,0:T(8,128)(2,1)} %broadcast_in_dim.38), calls=%async_computation.2 | async-start | bytes 2097152 | tf_op jit(solution)/shard_map/all_to_all | solution.py:145
  145.4 22.5 %collective-permute-done.13.refs_7_ = bf16[128,1536]{1,0:T(8,128)(2,1)} collective-permute-done((bf16[128,1536]{1,0:T(8,128)(2,1)S(1)}, bf16[128,1536]{1,0:T(8,128)(2,1)}, u32[]{:S(2)}, u32[]{:S(2)}) %collective-permute-start.13) | collective-permute-done | bytes 393248 | tf_op jit(solution)/shard_map/ppermute | solution.py:59
  184.9 6.2 %collective-permute-done.21.refs_1_ = bf16[128,1536]{1,0:T(8,128)(2,1)} collective-permute-done((bf16[128,1536]{1,0:T(8,128)(2,1)}, bf16[128,1536]{1,0:T(8,128)(2,1)}, u32[]{:S(2)}, u32[]{:S(2)}) %collective-permute-start.21) | collective-permute-done | bytes 393248 | tf_op jit(solution)/shard_map/ppermute | solution.py:59
  211.3 24.4 %shard_map.165 = (bf16[1024,640]{1,0:T(8,128)(2,1)}, bf16[1024,640]{1,0:T(8,128)(2,1)}, bf16[1024,1280]{1,0:T(8,128)(2,1)}, bf16[1024,1280]{1,0:T(8,128)(2,1)}, ...) custom-call(s32[8]{0:T(128)} %copy-done.19, ...), custom_call_target="tpu_custom_call" | custom-call | flops 12179999744 | bytes 1000 | tf_op jit(solution)/shard_map/pallas_call | solution.py:757
  236.8 24.8 %shard_map.166 = (bf16[1024,640]{1,0:T(8,128)(2,1)}, bf16[1024,640]{1,0:T(8,128)(2,1)}, bf16[1024,1280]{1,0:T(8,128)(2,1)}, bf16[1024,1280]{1,0:T(8,128)(2,1)}, ...) custom-call(s32[8]{0:T(128)} %copy-done.19, ...), custom_call_target="tpu_custom_call", output_to_operand_aliasing={{0}: (8, {}), {1}: (9, {}), {2}: (10, {}), {3}: (11, {}), {... | custom-call | flops 12179999744 | bytes 1000 | tf_op jit(solution)/shard_map/pallas_call | solution.py:757
  266.1 13.5 %shard_map.167 = bf16[8,288,1280]{2,1,0:T(8,128)(2,1)} custom-call(s32[8]{0:T(128)S(1)} %copy-done.21, bf16[128,1536]{1,0:T(8,128)(2,1)} %get-tuple-element.140.refs_0_, bf16[128,1536]{1,0:T(8,128)(2,1)} %collective-permute-done.21.refs_1_, bf16[128,1536]{1,0:T(8,128)(2,1)} %collective-permute-done.22.refs_2_, ...), custom_call_target="tpu_custom_call" | custom-call | flops 6206000128 | bytes 1000 | tf_op jit(solution)/shard_map/pallas_call | solution.py:168
  284.2 34.9 %all-gather.9.cloned.1.call-done.mine_ref = bf16[1536,1024]{1,0:T(8,128)(2,1)} async-done(((bf16[192,1024]{1,0:T(8,128)(2,1)}), bf16[1536,1024]{1,0:T(8,128)(2,1)}) %all-gather.9.cloned.1.call-update) | async-done | bytes 3145744 | tf_op jit(solution)/shard_map/all_gather | solution.py:894
  323.0 14.9 %shard_map.168 = (bf16[288,1280]{1,0:T(8,128)(2,1)}, bf16[288,1280]{1,0:T(8,128)(2,1)}, bf16[288,1280]{1,0:T(8,128)(2,1)}, bf16[288,1280]{1,0:T(8,128)(2,1)}, bf...) custom-call(s32[8]{0:T(128)} %copy-done.19, ...), custom_call_target="tpu_custom_call" | custom-call | flops 8700000256 | bytes 1000 | tf_op jit(solution)/shard_map/pallas_call | solution.py:168
  353.4 8.7 %shard_map.170 = (bf16[128,1536]{1,0:T(8,128)(2,1)}, bf16[8,128,512]{2,1,0:T(8,128)(2,1)}) custom-call(s32[1]{0:T(128)} %bitcast.1.me_ref.group_ref, bf16[8,128,256]{2,1,0:T(8,128)(2,1)} %copy-done.5, bf16[8,128,512]{2,1,0:T(8,128)(2,1)} %copy-done.2, bf16[128,1536]{1,0:T(8,128)(2,1)} %copy-done.45, f32[12,128,1]{2,1,0:T(8,128)} %copy-done.48, ...), custom_call_target="tpu_custom_call" | custom-call | flops 5219999744 | bytes 1000 | tf_op jit(solution)/shard_map/pallas_call | solution.py:598
  368.0 7.0 %all-to-all-start.3 = ((bf16[8,128,512]{2,1,0:T(8,128)(2,1)}), bf16[8,128,512]{2,1,0:T(8,128)(2,1)S(1)}, u32[]{:S(2)}, u32[]{:S(2)}) async-start(bf16[8,128,512]{2,1,0:T(8,128)(2,1)} %get-tuple-element.171), calls=%async_computation.4 | async-start | bytes 2097152 | tf_op jit(solution)/shard_map/all_to_all | solution.py:917
  384.3 20.8 %reduce-scatter.2.cloned.1.call-done = bf16[128,1536]{1,0:T(8,128)(2,1)} async-done(((bf16[1024,1536]{1,0:T(8,128)(2,1)}), bf16[128,1536]{1,0:T(8,128)(2,1)}) %reduce-scatter.2.cloned.1.call-update) | async-done | bytes 393232 | tf_op jit(solution)/shard_map/reduce_scatter | solution.py:920
  415.1 15.3 %collective-permute-done.40 = bf16[288,1280]{1,0:T(8,128)(2,1)S(1)} collective-permute-done((bf16[288,1280]{1,0:T(8,128)(2,1)}, bf16[288,1280]{1,0:T(8,128)(2,1)S(1)}, u32[]{:S(2)}, u32[]{:S(2)}) %collective-permute-start.40) | collective-permute-done | bytes 737312 | tf_op jit(solution)/shard_map/ppermute | solution.py:59
  453.3 12.2 %collective-permute-done.42.refs_1_ = bf16[288,1280]{1,0:T(8,128)(2,1)} collective-permute-done((bf16[288,1280]{1,0:T(8,128)(2,1)}, bf16[288,1280]{1,0:T(8,128)(2,1)}, u32[]{:S(2)}, u32[]{:S(2)}) %collective-permute-start.42) | collective-permute-done | bytes 737312 | tf_op jit(solution)/shard_map/ppermute | solution.py:59
  484.7 10.2 %all-to-all-start.5 = ((bf16[8,208,256]{2,1,0:T(8,128)(2,1)}), bf16[8,208,256]{2,1,0:T(8,128)(2,1)S(1)}, u32[]{:S(2)}, u32[]{:S(2)}) async-start(bf16[8,208,256]{2,1,0:T(8,128)(2,1)} %shard_map.174), calls=%async_computation.6 | async-start | bytes 1703936 | tf_op jit(solution)/shard_map/all_to_all | solution.py:952
  499.8 7.8 %all-to-all-done.5.in_ref = bf16[8,208,256]{2,1,0:T(8,128)(2,1)S(1)} async-done(((bf16[8,208,256]{2,1,0:T(8,128)(2,1)}), bf16[8,208,256]{2,1,0:T(8,128)(2,1)S(1)}, u32[]{:S(2)}, u32[]{:S(2)}) %all-to-all-start.5) | async-done | bytes 852000 | tf_op jit(solution)/shard_map/all_to_all | solution.py:952
  515.8 6.8 %collective-permute-done.54.refs_2_ = bf16[288,1280]{1,0:T(8,128)(2,1)} collective-permute-done((bf16[288,1280]{1,0:T(8,128)(2,1)}, bf16[288,1280]{1,0:T(8,128)(2,1)}, u32[]{:S(2)}, u32[]{:S(2)}) %collective-permute-start.54) | collective-permute-done | bytes 737312 | tf_op jit(solution)/shard_map/ppermute | solution.py:59
  523.4 7.5 %shard_map.176 = (f32[192,17920]{1,0:T(8,128)}, f32[1120,1536]{1,0:T(8,128)}) custom-call(s32[1]{0:T(128)} %bitcast.core_ref, s32[8]{0:T(128)S(1)} %copy-done.22, bf16[288,1280]{1,0:T(8,128)(2,1)} %pad_maximum_fusion.refs_0_, bf16[288,1280]{1,0:T(8,128)(2,1)} %collective-permute-done.42.refs_1_, bf16[288,1280]{1,0:T(8,128)(2,1)} %collective-permute-done.43.refs_2_, ...), custom_call_target="tpu_custom_call" | custom-call | flops 5800000000 | bytes 1000 | tf_op jit(solution)/shard_map/pallas_call | solution.py:428
  534.3 6.3 %shard_map.178 = (f32[192,17920]{1,0:T(8,128)}, f32[1120,1536]{1,0:T(8,128)}) custom-call(s32[1]{0:T(128)} %bitcast.core_ref, s32[8]{0:T(128)S(1)} %copy-done.22, bf16[288,1280]{1,0:T(8,128)(2,1)S(1)} %collective-permute-done.52.refs_0_, bf16[288,1280]{1,0:T(8,128)(2,1)S(1)} %collective-permute-done.53.refs_1_, ...), custom_call_target="tpu_custom_call", output_to_operand_aliasing={{0}: (8, {}), {1}: (9, {})} | custom-call | flops 3480000000 | bytes 1000 | tf_op jit(solution)/shard_map/pallas_call | solution.py:428
  (298 shorter events, 233.2 us)
Async XLA Ops:
  7.2 97.3 %all-gather.7.cloned.1.call-start = ((), (), s32[]{:S(2)}) async-start(), calls=%async_computation.8 | async-start | bytes 2654208 | tf_op jit(solution)/shard_map/all_gather | solution.py:846
  9.1 187.2 %all-gather.11.cloned.1.call-start = ((), (), s32[]{:S(2)}) async-start(), calls=%async_computation.11 | async-start | bytes 6635520 | tf_op jit(solution)/shard_map/all_gather | solution.py:859
  45.0 32.5 %all-to-all-start = ((bf16[8,208,256]{2,1,0:T(8,128)(2,1)}), bf16[8,208,256]{2,1,0:T(8,128)(2,1)}, u32[]{:S(2)}, u32[]{:S(2)}) async-start(bf16[8,208,256]{2,1,0:T(8,128)(2,1)} %broadcast_in_dim.35), calls=%async_computation | async-start | bytes 1703936 | tf_op jit(solution)/shard_map/all_to_all | solution.py:145
  104.5 67.7 %collective-permute-start.14 = (bf16[1536,768]{1,0:T(8,128)(2,1)}, bf16[1536,768]{1,0:T(8,128)(2,1)}, u32[]{:S(2)}, u32[]{:S(2)}) collective-permute-start(bf16[1536,768]{1,0:T(8,128)(2,1)} %all-gather.7.cloned.1.call-done.mine_ref), channel_id=1, source_target_pairs={{0,1},{1,0},{2,3},{3,2},{4,5},{5,4},{6,7},{7,6},{8,9},{9,8},{10,11... | collective-permute-start | bytes 7077896 | tf_op jit(solution)/shard_map/ppermute | solution.py:141
  128.0 39.9 %all-to-all-start.2 = ((bf16[8,128,512]{2,1,0:T(8,128)(2,1)}), bf16[8,128,512]{2,1,0:T(8,128)(2,1)S(1)}, u32[]{:S(2)}, u32[]{:S(2)}) async-start(bf16[8,128,512]{2,1,0:T(8,128)(2,1)} %broadcast_in_dim.38), calls=%async_computation.2 | async-start | bytes 2097152 | tf_op jit(solution)/shard_map/all_to_all | solution.py:145
  134.6 127.1 %all-gather.13.cloned.1.call-start = ((), (), s32[]{:S(2)}) async-start(), calls=%async_computation.12 | async-start | bytes 3538944 | tf_op jit(solution)/shard_map/all_gather | solution.py:892
  138.0 29.9 %collective-permute-start.13 = (bf16[128,1536]{1,0:T(8,128)(2,1)S(1)}, bf16[128,1536]{1,0:T(8,128)(2,1)}, u32[]{:S(2)}, u32[]{:S(2)}) collective-permute-start(bf16[128,1536]{1,0:T(8,128)(2,1)S(1)} %collective-permute-done.10.refs_4_), channel_id=1, source_target_pairs={{0,8},{2,10},{4,12},{6,14},{8,0},{10,2},{12,4},{14,6},{1,9},{3,11}... | collective-permute-start | bytes 1179656 | tf_op jit(solution)/shard_map/ppermute | solution.py:59
  201.8 117.3 %all-gather.9.cloned.1.call-start = ((), (), s32[]{:S(2)}) async-start(), calls=%async_computation.9 | async-start | bytes 3538944 | tf_op jit(solution)/shard_map/all_gather | solution.py:894
  206.7 198.5 %reduce-scatter.2.cloned.1.call-start = ((), (), s32[]{:S(2)}) async-start(), calls=%async_computation.10 | async-start | bytes 3538944 | tf_op jit(solution)/shard_map/reduce_scatter | solution.py:920
  206.8 29.0 %collective-permute-start.17 = (bf16[128,1536]{1,0:T(8,128)(2,1)}, bf16[128,1536]{1,0:T(8,128)(2,1)S(1)}, u32[]{:S(2)}, u32[]{:S(2)}) collective-permute-start(bf16[128,1536]{1,0:T(8,128)(2,1)} %collective-permute-done.16.refs_3_), channel_id=1, source_target_pairs={{0,2},{2,4},{4,6},{6,0},{8,10},{10,12},{12,14},{14,8},{1,3},{3,5},... | collective-permute-start | bytes 1179656 | tf_op jit(solution)/shard_map/ppermute | solution.py:59
  206.8 29.0 %collective-permute-start.18 = (bf16[128,1536]{1,0:T(8,128)(2,1)}, bf16[128,1536]{1,0:T(8,128)(2,1)S(1)}, u32[]{:S(2)}, u32[]{:S(2)}) collective-permute-start(bf16[128,1536]{1,0:T(8,128)(2,1)} %collective-permute-done.16.refs_3_), channel_id=1, source_target_pairs={{0,6},{2,0},{4,2},{6,4},{8,14},{10,8},{12,10},{14,12},{1,7},{3,1},... | collective-permute-start | bytes 1179656 | tf_op jit(solution)/shard_map/ppermute | solution.py:59
  279.6 43.4 %collective-permute-start.31 = (bf16[8,288,1280]{2,1,0:T(8,128)(2,1)}, bf16[8,288,1280]{2,1,0:T(8,128)(2,1)}, u32[]{:S(2)}, u32[]{:S(2)}) collective-permute-start(bf16[8,288,1280]{2,1,0:T(8,128)(2,1)} %shard_map.167), channel_id=1, source_target_pairs={{0,1},{1,0},{2,3},{3,2},{4,5},{5,4},{6,7},{7,6},{8,9},{9,8},{10,11... | collective-permute-start | bytes 17694728 | tf_op jit(solution)/shard_map/ppermute | solution.py:141
  280.4 38.7 %collective-permute-start.26 = (bf16[128,1536]{1,0:T(8,128)(2,1)S(1)}, bf16[128,1536]{1,0:T(8,128)(2,1)S(1)}, u32[]{:S(2)}, u32[]{:S(2)}) collective-permute-start(bf16[128,1536]{1,0:T(8,128)(2,1)S(1)} %copy-done.56), channel_id=1, source_target_pairs={{0,8},{2,10},{4,12},{6,14},{8,0},{10,2},{12,4},{14,6},{1,9},{3,11}... | collective-permute-start | bytes 1179656 | tf_op jit(solution)/shard_map/ppermute | solution.py:59
  282.7 37.5 %collective-permute-start.29 = (bf16[128,1536]{1,0:T(8,128)(2,1)}, bf16[128,1536]{1,0:T(8,128)(2,1)}, u32[]{:S(2)}, u32[]{:S(2)}) collective-permute-start(bf16[128,1536]{1,0:T(8,128)(2,1)} %get-tuple-element.129), channel_id=1, source_target_pairs={{0,6},{2,0},{4,2},{6,4},{8,14},{10,8},{12,10},{14,12},{1,7},{3,1},... | collective-permute-start | bytes 1179656 | tf_op jit(solution)/shard_map/ppermute | solution.py:59
  284.0 36.5 %collective-permute-start.28 = (bf16[128,1536]{1,0:T(8,128)(2,1)}, bf16[128,1536]{1,0:T(8,128)(2,1)}, u32[]{:S(2)}, u32[]{:S(2)}) collective-permute-start(bf16[128,1536]{1,0:T(8,128)(2,1)} %get-tuple-element.128), channel_id=1, source_target_pairs={{0,2},{2,4},{4,6},{6,0},{8,10},{10,12},{12,14},{14,8},{1,3},{3,5},... | collective-permute-start | bytes 1179656 | tf_op jit(solution)/shard_map/ppermute | solution.py:59
  284.1 53.7 %collective-permute-start.24 = (bf16[128,1536]{1,0:T(8,128)(2,1)}, bf16[128,1536]{1,0:T(8,128)(2,1)S(1)}, u32[]{:S(2)}, u32[]{:S(2)}) collective-permute-start(bf16[128,1536]{1,0:T(8,128)(2,1)} %get-tuple-element.123), channel_id=1, source_target_pairs={{0,2},{2,4},{4,6},{6,0},{8,10},{10,12},{12,14},{14,8},{1,3},{3,5},... | collective-permute-start | bytes 1179656 | tf_op jit(solution)/shard_map/ppermute | solution.py:59
  375.1 39.9 %collective-permute-start.37 = (bf16[288,1280]{1,0:T(8,128)(2,1)}, bf16[288,1280]{1,0:T(8,128)(2,1)}, u32[]{:S(2)}, u32[]{:S(2)}) collective-permute-start(bf16[288,1280]{1,0:T(8,128)(2,1)} %get-tuple-element.153), channel_id=1, source_target_pairs={{0,16},{16,32},{32,48},{48,0},{64,80},{80,96},{96,112},{112,64},{1... | collective-permute-start | bytes 2211848 | tf_op jit(solution)/shard_map/ppermute | solution.py:59
  376.3 38.7 %collective-permute-start.38 = (bf16[288,1280]{1,0:T(8,128)(2,1)}, bf16[288,1280]{1,0:T(8,128)(2,1)}, u32[]{:S(2)}, u32[]{:S(2)}) collective-permute-start(bf16[288,1280]{1,0:T(8,128)(2,1)} %get-tuple-element.154), channel_id=1, source_target_pairs={{0,48},{16,0},{32,16},{48,32},{64,112},{80,64},{96,80},{112,96},{1... | collective-permute-start | bytes 2211848 | tf_op jit(solution)/shard_map/ppermute | solution.py:59
  380.2 34.8 %collective-permute-start.39 = (bf16[288,1280]{1,0:T(8,128)(2,1)}, bf16[288,1280]{1,0:T(8,128)(2,1)}, u32[]{:S(2)}, u32[]{:S(2)}) collective-permute-start(bf16[288,1280]{1,0:T(8,128)(2,1)} %add_convert_fusion.2), channel_id=1, source_target_pairs={{0,32},{16,48},{32,0},{48,16},{64,96},{80,112},{96,64},{112,80},{1... | collective-permute-start | bytes 2211848 | tf_op jit(solution)/shard_map/ppermute | solution.py:59
  407.2 65.6 %collective-permute-start.35 = (bf16[1536,1024]{1,0:T(8,128)(2,1)}, bf16[1536,1024]{1,0:T(8,128)(2,1)}, u32[]{:S(2)}, u32[]{:S(2)}) collective-permute-start(bf16[1536,1024]{1,0:T(8,128)(2,1)} %all-gather.9.cloned.1.call-done.mine_ref), channel_id=1, source_target_pairs={{0,1},{1,0},{2,3},{3,2},{4,5},{5,4},{6,7},{7,6},{8,9},{9,8},{10,11... | collective-permute-start | bytes 9437192 | tf_op jit(solution)/shard_map/ppermute | solution.py:141
  444.6 28.2 %collective-permute-start.36 = (bf16[1536,256]{1,0:T(8,128)(2,1)}, bf16[1536,256]{1,0:T(8,128)(2,1)S(1)}, u32[]{:S(2)}, u32[]{:S(2)}) collective-permute-start(bf16[1536,256]{1,0:T(8,128)(2,1)} %get-tuple-element.181), channel_id=1, source_target_pairs={{0,1},{1,0},{2,3},{3,2},{4,5},{5,4},{6,7},{7,6},{8,9},{9,8},{10,11... | collective-permute-start | bytes 2359304 | tf_op jit(solution)/shard_map/ppermute | solution.py:141
  452.1 42.8 %collective-permute-start.44 = (bf16[288,1280]{1,0:T(8,128)(2,1)}, bf16[288,1280]{1,0:T(8,128)(2,1)}, u32[]{:S(2)}, u32[]{:S(2)}) collective-permute-start(bf16[288,1280]{1,0:T(8,128)(2,1)} %pad_maximum_fusion.refs_0_), channel_id=1, source_target_pairs={{0,8},{2,10},{4,12},{6,14},{8,0},{10,2},{12,4},{14,6},{1,9},{3,11}... | collective-permute-start | bytes 2211848 | tf_op jit(solution)/shard_map/ppermute | solution.py:59
  465.5 31.2 %collective-permute-start.45 = (bf16[288,1280]{1,0:T(8,128)(2,1)}, bf16[288,1280]{1,0:T(8,128)(2,1)}, u32[]{:S(2)}, u32[]{:S(2)}) collective-permute-start(bf16[288,1280]{1,0:T(8,128)(2,1)} %pad_maximum_fusion.refs_0_), channel_id=1, source_target_pairs={{0,4},{2,6},{4,0},{6,2},{8,12},{10,14},{12,8},{14,10},{1,5},{3,7},... | collective-permute-start | bytes 2211848 | tf_op jit(solution)/shard_map/ppermute | solution.py:59
  468.7 29.0 %collective-permute-start.46 = (bf16[288,1280]{1,0:T(8,128)(2,1)}, bf16[288,1280]{1,0:T(8,128)(2,1)}, u32[]{:S(2)}, u32[]{:S(2)}) collective-permute-start(bf16[288,1280]{1,0:T(8,128)(2,1)} %pad_maximum_fusion.refs_0_), channel_id=1, source_target_pairs={{0,1},{1,0},{2,3},{3,2},{4,5},{5,4},{6,7},{7,6},{8,9},{9,8},{10,11... | collective-permute-start | bytes 2211848 | tf_op jit(solution)/shard_map/ppermute | solution.py:141
  (103 other events, 1492.8 us)
Sparse Core Ops, SparseCore 0:
  10.9 73.3 all-gather.6
  87.2 109.1 all-gather.10
  201.9 50.1 all-gather.12
  254.3 64.8 all-gather.8
  338.1 67.0 reduce-scatter.1

commit v2 on v1

--- a/solution.py
+++ b/solution.py
@@ -59,9 +59,10 @@
     return lax.ppermute(block, axes, shift_pairs(offset))
 
 
-def send_out(block, axes):
+def send_out(block, axes, row=False, hold=()):
     one, three = send(block, axes, (0, 1)), send(block, axes, (0, 3))
     across, two = send(block, axes, (1, 0)), send(block, axes, (0, 2))
+    across, two = after((across, two), *hold)
     return [
         block,
         one,
@@ -70,7 +71,7 @@
         two,
         send(across, axes, (0, 1)),
         send(across, axes, (0, 3)),
-        send(two, axes, (1, 0)),
+        send(across, axes, (0, 2)) if row else send(two, axes, (1, 0)),
     ]
 
 
@@ -206,7 +207,7 @@
     c_ref, grad_ref, act_ref = refs[8:11]
     copies = fetch(
         [(grad_ref, grad)]
-        + [(refs[k], rows_of(h_all, k)) for k in range(8)]
+        + [(refs[k].at[:ROWS], rows_of(h_all, k)) for k in range(8)]
         + [(act_ref, act)]
         + [(c_ref.at[order_ref[k]], rows_of(c_all, k)) for k in range(8)],
         sems,
@@ -322,27 +323,35 @@
     )
 
 
-def attention_grads_kernel(core_ref, normed_ref, att_ref, both_ref, keep_ref, give_ref, bias_ref):
+def attention_grads_kernel(core_ref, order_ref, normed_ref, both_ref, *refs):
+    keep_ref, give_ref, bias_ref, att_all, sems = refs[8:]
+    copies = fetch(
+        [(refs[k].at[ROWS:], att_all.at[order_ref[k]]) for k in range(8)], sems
+    )
     both = both_ref[...].reshape(8 * ROWS, 512)
     role = both[:, :256]
     bias_ref[...] = jnp.sum(role.astype(F32), axis=0, keepdims=True)
     qkv = contract_rows(normed_ref[...].reshape(8 * ROWS, D), role)
-    out = contract_rows(att_ref[...].reshape(8 * ROWS, D), both[:, 256:])
+    for copy in copies:
+        copy.wait()
+    out = contract_rows(att_all[...].reshape(8 * ROWS, D), both[:, 256:])
     keep, give = halves(core_ref, qkv, out)
     keep_ref[...] = keep
     give_ref[...] = give.astype(BF)
 
 
-def attention_grads(core, normed, attended, both):
+def attention_grads(core, order, normed, both, bundles):
     return call(
         attention_grads_kernel,
         5,
         [((D, 256), F32), ((D, 256), BF), ((1, 256), F32)],
-        [pl.BlockSpec(memory_space=pltpu.SMEM)] + whole(3),
+        scalars(2) + whole(2) + anywhere(8),
         core,
+        order,
         normed,
-        attended,
         both,
+        *bundles,
+        scratch_shapes=[pltpu.VMEM((8, ROWS, D), BF), pltpu.SemaphoreType.DMA((8,))],
     )
 
 
@@ -629,8 +638,9 @@
     scale_ref[...] = scale
     mid_ref[:, : D // 2] = low
     mid_ref[:, D // 2 :] = high
-    h_ref[:, : D // 2] = (low * scale * gain_ref[:, : D // 2]).astype(BF)
-    h_ref[:, D // 2 :] = (high * scale * gain_ref[:, D // 2 :]).astype(BF)
+    h_ref[:ROWS, : D // 2] = (low * scale * gain_ref[:, : D // 2]).astype(BF)
+    h_ref[:ROWS, D // 2 :] = (high * scale * gain_ref[:, D // 2 :]).astype(BF)
+    h_ref[ROWS:] = att
 
 
 def middle_of(core, attended, rows, gain, mine, other):
@@ -642,7 +652,7 @@
         out_shape=[
             jax.ShapeDtypeStruct((ROWS, D), F32),
             jax.ShapeDtypeStruct((ROWS, 1), F32),
-            jax.ShapeDtypeStruct((ROWS, D), BF),
+            jax.ShapeDtypeStruct((2 * ROWS, D), BF),
         ],
         compiler_params=pltpu.CompilerParams(vmem_limit_bytes=24 << 20),
         cost_estimate=cost(3),
@@ -706,7 +716,7 @@
             copy.start()
             copies.append(copy)
     tokens = fetch(
-        [(h_refs[i], rows_of(h_all, i)) for i in range(4)]
+        [(h_refs[i].at[:ROWS], rows_of(h_all, i)) for i in range(4)]
         + [(c_ref.at[order_ref[first + i]], rows_of(c_all, i)) for i in range(4)],
         in_sems,
     )
@@ -830,7 +840,7 @@
     works = replica < ROLES
     role = jnp.minimum(replica, ROLES - 1)
 
-    x_blocks = send_out(hidden_in[0], PLANE)
+    x_blocks = send_out(hidden_in[0], PLANE, True)
     pad = jnp.zeros((64,), BF)
     small = jnp.concatenate([b_qkv, norm_attn, pad, norm_mlp, pad]).reshape(3, 256)
     columns = lax.dynamic_slice(w_qkv, (0, plane * 256), (SHARD, 256))
@@ -871,12 +881,12 @@
         x_blocks,
     )
 
+    grad_out = cotangent[0]
+    cot_blocks = send_out(after(grad_out, *x_blocks), PLANE, True)
+    heads = after(heads, *cot_blocks[1:5])
     heads = lax.all_to_all(heads, PLANE, 0, 0, tiled=True)
     out_other = swap(after(out_mine, heads))
-    grad_out = cotangent[0]
-    cot_blocks = send_out(after(grad_out, *x_blocks), PLANE)
     kv_own = jnp.concatenate([heads[6], heads[7]], axis=1)
-    kv_own = after(kv_own, *cot_blocks[1:5])
     kv_all = gather_direct(kv_own, GROUP)
     kv_all = after(kv_all, *cot_blocks)
     cot_all = arrange(order, cot_blocks)
@@ -889,9 +899,8 @@
 
     h_blocks = send_out(normed_two, PLANE)
     feed_other = swap(after(feed_mine, *h_blocks[1:3]))
-    attended_all = lax.all_gather(after(attended, *h_blocks[1:5]), PLANE, axis=0)
     qkv_half = lax.dynamic_slice(w_qkv, (0, core * 1024), (SHARD, 1024))
-    qkv_mine = lax.all_gather(after(qkv_half, *h_blocks[1:5]), GROUP, axis=0, tiled=True)
+    qkv_mine = lax.all_gather(after(qkv_half, normed_two), GROUP, axis=0, tiled=True)
     held, back_blocks = (), {}
     for part in (slice(0, 4), slice(4, 8)):
         held, parts = feed(order, h_blocks[part], cot_all, feed_mine, feed_other, held)
@@ -899,11 +908,11 @@
             back_blocks[back(o)] = block
     second_parts, _, round_sums = send_parts(back_blocks, PLANE)
 
-    held_h = after(tuple(h_blocks), parts, attended_all)
+    held_h = after(tuple(h_blocks), parts, qkv_mine)
     given = weight_grads(order, held_h, cot_all, held[3], held[1])
     group_order = jnp.stack([place(yh, xx, o) for o in ALL_OFFSETS]).astype(jnp.int32)
     merged = merged_grads(
-        order, group_order, after(held_h, qkv_mine), cot_all, held[2], held[0], swap(given)
+        order, group_order, held_h, cot_all, held[2], held[0], swap(given)
     )
     second_parts = after(second_parts, merged)
     grad_middle, grad_branch, grad_attended, gain_two_grad = turning(
@@ -919,27 +928,18 @@
     out_rows = after(held[4], *second_parts).reshape(8 * ROWS, D)
     out_rows = lax.psum_scatter(out_rows, PLANE, scatter_dimension=0, tiled=True)
     result = (middle + out_rows.astype(F32)).astype(BF)[None]
-    grad_kv = after(grad_kv, out_rows)
 
     both, grad_projected = assemble(grad_q, grad_kv, grad_branch, cosine, signed)
     qkv_other = swap(after(qkv_mine, both))
     assembled = both
     both = lax.all_to_all(both, PLANE, 0, 0, tiled=True)
 
-    mlp_grad = total(after(tuple(mlp_parts), assembled)).astype(BF)
-    down_grad = lax.ppermute(mlp_grad[SHARD:], EVERY, [(t, s) for s, t in down_pairs()])
-    mlp_grad = jnp.concatenate([mlp_grad[:SHARD], down_grad], axis=0)
-    grad_blocks = send_out(mlp_grad, PLANE)
-    other_blocks = [swap(b) for b in grad_blocks]
-    feed_grads = write_grads(which, order, grad_blocks, other_blocks, 0, 5, ())
-    gate_up_grad, down_grad = write_grads(which, order, grad_blocks, other_blocks, 5, 8, feed_grads)
-
     grad_in, gain_one_grad = finish(
         which, grad_projected, qkv_mine, qkv_other, hidden_in[0], gain_one, grad_middle
     )
+    keep, give, bias_grad = attention_grads(which, order, normed_one_all, after(both, gain_one_grad, *mlp_parts), h_blocks)
     gains = jnp.stack([gain_one_grad[0], gain_two_grad[0]]).astype(BF).reshape(2, 8, SHARD)
     gains = jnp.pad(gains.transpose(1, 0, 2), ((0, 0), (0, 14), (0, 64)))
-    keep, give, bias_grad = attention_grads(which, normed_one_all, attended_all, both)
     (payload,) = call(
         payload_kernel, 1.4,
         [((8, SHARD + 16, 256), BF)],
@@ -949,7 +949,16 @@
         gains,
         bias_grad,
     )
+    mlp_grad = total(after(tuple(mlp_parts), out_rows)).astype(BF)
+    down_grad = lax.ppermute(mlp_grad[SHARD:], EVERY, [(t, s) for s, t in down_pairs()])
+    mlp_grad = jnp.concatenate([mlp_grad[:SHARD], down_grad], axis=0)
     payload = lax.all_to_all(payload, GROUP, 0, 0, tiled=True)
+    grad_blocks = send_out(mlp_grad, PLANE, hold=(payload,))
+    other_blocks = [swap(b) for b in grad_blocks]
+    feed_grads = write_grads(which, order, grad_blocks, other_blocks, 0, 5, ())
+    gate_up_grad, down_grad = write_grads(which, order, grad_blocks, other_blocks, 5, 8, feed_grads)
+
+
     (payload,) = call(sum_kernel, 1, [((8, SHARD + 16, 256), BF)], whole(1), payload)
     mine = lax.all_to_all(payload, PLANE, 0, 0, tiled=True)
     mine = after(mine, *feed_grads)

time: 562 us -> 538 us (0.957)
  the two profiles are of different devices: /device:TPU:25 before, /device:TPU:7 now
where the time goes in v2:
time: 538 us; the launch traced here: 528 us
  waiting for transfers between devices  163 us (30%)
  Pallas kernels  140 us (26%)
  starting transfers between devices  126 us (23%)
  local copies, waits for them, and re-layouts  40.1 us (7%)
  blocking collectives  33.7 us (6%)
  between operations  15 us (3%)
  other arithmetic  10.4 us (2%)
    ppermute x42, waiting for transfers between devices, send(): return lax.ppermute(block, axes, shift_pairs(offset))  147 us
    ppermute x42, starting transfers between devices, send(): return lax.ppermute(block, axes, shift_pairs(offset))  65.4 us
    pallas_call x9, Pallas kernels, call(): pl.pallas_call(kernel, in_specs=in_specs, out_specs=[pl.BlockSpec(memory_...  50.7 us
    pallas_call x2, Pallas kernels, feed(): pl.pallas_call(functools.partial(feed_kernel, len(held)), grid=(1,), in_s...  49.1 us
    unnamed x144, local copies, waits for them, and re-layouts  25.9 us
    all_to_all x1, blocking collectives, on_device(): grad_kv = lax.all_to_all(grad_kv, GROUP, 0, 0, tiled=True)  23.5 us
    ppermute x14, starting transfers between devices, swap(): return lax.ppermute(block, 'c', [(0, 1), (1, 0)])  22.2 us
    all_to_all x2, starting transfers between devices, gather_direct(): lax.all_to_all(jnp.broadcast_to(block[None], (8,) + block.shape), axes, 0...  12.8 us
  transfers between devices with their start and end apart: 67, of which 21 were waited for; matrix products, arithmetic and copies ran while one was open for 4% of the time, Pallas kernels for 24%

profile of v2, /device:TPU:7, one launch (start us, length us, event | category | flops | bytes accessed | tf_op | source)
XLA Modules:
  0.0 527.9 jit_solution(4693552872089682173)
XLA Ops:
  18.0 6.9 %collective-permute-done.20.piece_ref = bf16[80,1536]{1,0:T(8,128)(2,1)S(1)} collective-permute-done((bf16[80,1536]{1,0:T(8,128)(2,1)}, bf16[80,1536]{1,0:T(8,128)(2,1)S(1)}, u32[]{:S(2)}, u32[]{:S(2)}) %collective-permute-start.20) | collective-permute-done | bytes 245792 | tf_op jit(solution)/shard_map/ppermute | solution.py:858
  37.3 9.7 %collective-permute-done.1.refs_2_ = bf16[128,1536]{1,0:T(8,128)(2,1)S(1)} collective-permute-done((bf16[128,1536]{1,0:T(8,128)(2,1)S(1)}, bf16[128,1536]{1,0:T(8,128)(2,1)S(1)}, u32[]{:S(2)}, u32[]{:S(2)}) %collective-permute-start.1) | collective-permute-done | bytes 393248 | tf_op jit(solution)/shard_map/ppermute | solution.py:59
  99.9 10.2 %all_to_all.35.heads_ref = bf16[8,128,256]{2,1,0:T(8,128)(2,1)S(1)} all-to-all(bf16[8,128,256]{2,1,0:T(8,128)(2,1)S(1)} %get-tuple-element.101), channel_id=1, replica_groups=mesh['yh'=2,'x'=4,'yl'=2,'z'=4,'c'=2] {'yl','z'}, dimensions={0} | all-to-all | bytes 1048576 | tf_op jit(solution)/shard_map/all_to_all | solution.py:887
  115.3 7.3 %all-to-all-start.2 = ((bf16[8,128,512]{2,1,0:T(8,128)(2,1)}), bf16[8,128,512]{2,1,0:T(8,128)(2,1)S(1)}, u32[]{:S(2)}, u32[]{:S(2)}) async-start(bf16[8,128,512]{2,1,0:T(8,128)(2,1)} %broadcast_in_dim.38), calls=%async_computation.2 | async-start | bytes 2097152 | tf_op jit(solution)/shard_map/all_to_all | solution.py:146
  126.5 8.4 %collective-permute-done.11.refs_5_ = bf16[128,1536]{1,0:T(8,128)(2,1)S(1)} collective-permute-done((bf16[128,1536]{1,0:T(8,128)(2,1)S(1)}, bf16[128,1536]{1,0:T(8,128)(2,1)S(1)}, u32[]{:S(2)}, u32[]{:S(2)}) %collective-permute-start.11) | collective-permute-done | bytes 393248 | tf_op jit(solution)/shard_map/ppermute | solution.py:59
  152.1 15.6 %collective-permute-done.21.refs_1_ = bf16[256,1536]{1,0:T(8,128)(2,1)} collective-permute-done((bf16[256,1536]{1,0:T(8,128)(2,1)}, bf16[256,1536]{1,0:T(8,128)(2,1)}, u32[]{:S(2)}, u32[]{:S(2)}) %collective-permute-start.21) | collective-permute-done | bytes 786464 | tf_op jit(solution)/shard_map/ppermute | solution.py:59
  168.5 7.8 %all-gather.9.cloned.1.call-done = bf16[2304,1280]{1,0:T(8,128)(2,1)} async-done(((bf16[288,1280]{1,0:T(8,128)(2,1)}), bf16[2304,1280]{1,0:T(8,128)(2,1)}) %all-gather.9.cloned.1.call-update) | async-done | bytes 5898256 | tf_op jit(solution)/shard_map/all_gather | solution.py:869
  186.0 17.0 %collective-permute-done.16.refs_3_ = bf16[256,1536]{1,0:T(8,128)(2,1)S(1)} collective-permute-done((bf16[256,1536]{1,0:T(8,128)(2,1)}, bf16[256,1536]{1,0:T(8,128)(2,1)S(1)}, u32[]{:S(2)}, u32[]{:S(2)}) %collective-permute-start.16) | collective-permute-done | bytes 786464 | tf_op jit(solution)/shard_map/ppermute | solution.py:59
  206.2 24.3 %shard_map.165 = (bf16[1024,640]{1,0:T(8,128)(2,1)}, bf16[1024,640]{1,0:T(8,128)(2,1)}, bf16[1024,1280]{1,0:T(8,128)(2,1)}, bf16[1024,1280]{1,0:T(8,128)(2,1)}, ...) custom-call(s32[8]{0:T(128)} %copy-done.18, ...), custom_call_target="tpu_custom_call" | custom-call | flops 12179999744 | bytes 1000 | tf_op jit(solution)/shard_map/pallas_call | solution.py:767
  231.9 24.7 %shard_map.166 = (bf16[1024,640]{1,0:T(8,128)(2,1)}, bf16[1024,640]{1,0:T(8,128)(2,1)}, bf16[1024,1280]{1,0:T(8,128)(2,1)}, bf16[1024,1280]{1,0:T(8,128)(2,1)}, ...) custom-call(s32[8]{0:T(128)} %copy-done.18, ...), custom_call_target="tpu_custom_call", output_to_operand_aliasing={{0}: (8, {}), {1}: (9, {}), {2}: (10, {}), {3}: (11, {}), {... | custom-call | flops 12179999744 | bytes 1000 | tf_op jit(solution)/shard_map/pallas_call | solution.py:767
  259.0 13.5 %shard_map.167 = bf16[8,288,1280]{2,1,0:T(8,128)(2,1)} custom-call(s32[8]{0:T(128)S(1)} %copy-done.20, bf16[256,1536]{1,0:T(8,128)(2,1)} %get-tuple-element.124.refs_0_, bf16[256,1536]{1,0:T(8,128)(2,1)} %collective-permute-done.21.refs_1_, bf16[256,1536]{1,0:T(8,128)(2,1)} %collective-permute-done.22.refs_2_, bf16[256,1536]{1,0:T(8,128)(2,1)S(1)} %copy-done.25, ...), custom_call_target="tpu_custom_call" | custom-call | flops 6206000128 | bytes 1000 | tf_op jit(solution)/shard_map/pallas_call | solution.py:169
  281.1 8.4 %collective-permute-done.28 = bf16[128,1536]{1,0:T(8,128)(2,1)S(1)} collective-permute-done((bf16[128,1536]{1,0:T(8,128)(2,1)}, bf16[128,1536]{1,0:T(8,128)(2,1)S(1)}, u32[]{:S(2)}, u32[]{:S(2)}) %collective-permute-start.28) | collective-permute-done | bytes 393248 | tf_op jit(solution)/shard_map/ppermute | solution.py:59
  292.7 15.0 %shard_map.168 = (bf16[288,1280]{1,0:T(8,128)(2,1)}, bf16[288,1280]{1,0:T(8,128)(2,1)}, bf16[288,1280]{1,0:T(8,128)(2,1)}, bf16[288,1280]{1,0:T(8,128)(2,1)}, bf...) custom-call(s32[8]{0:T(128)} %copy-done.18, ...), custom_call_target="tpu_custom_call" | custom-call | flops 8700000256 | bytes 1000 | tf_op jit(solution)/shard_map/pallas_call | solution.py:169
  321.7 8.7 %shard_map.170 = (bf16[128,1536]{1,0:T(8,128)(2,1)}, bf16[8,128,512]{2,1,0:T(8,128)(2,1)}) custom-call(s32[1]{0:T(128)} %bitcast.1.me_ref.group_ref, bf16[8,128,256]{2,1,0:T(8,128)(2,1)} %copy-done.6, bf16[8,128,512]{2,1,0:T(8,128)(2,1)} %copy-done.3, bf16[128,1536]{1,0:T(8,128)(2,1)} %copy-done.57, f32[12,128,1]{2,1,0:T(8,128)} %copy-done.60, ...), custom_call_target="tpu_custom_call" | custom-call | flops 5219999744 | bytes 1000 | tf_op jit(solution)/shard_map/pallas_call | solution.py:607
  330.4 7.7 %collective-permute-done.34 = bf16[288,1280]{1,0:T(8,128)(2,1)S(1)} collective-permute-done((bf16[288,1280]{1,0:T(8,128)(2,1)}, bf16[288,1280]{1,0:T(8,128)(2,1)S(1)}, u32[]{:S(2)}, u32[]{:S(2)}) %collective-permute-start.34) | collective-permute-done | bytes 737312 | tf_op jit(solution)/shard_map/ppermute | solution.py:59
  338.1 23.5 %all_to_all.36.dkv_ref = bf16[8,128,512]{2,1,0:T(8,128)(2,1)S(1)} all-to-all(bf16[8,128,512]{2,1,0:T(8,128)(2,1)} %get-tuple-element.155), channel_id=1, replica_groups=mesh['yh'=2,'x'=4,'yl'=2,'z'=4,'c'=2] {'yh','x'}, dimensions={0} | all-to-all | bytes 2097152 | tf_op jit(solution)/shard_map/all_to_all | solution.py:926
  391.3 12.1 %collective-permute-done.38 = bf16[288,1280]{1,0:T(8,128)(2,1)} collective-permute-done((bf16[288,1280]{1,0:T(8,128)(2,1)}, bf16[288,1280]{1,0:T(8,128)(2,1)}, u32[]{:S(2)}, u32[]{:S(2)}) %collective-permute-start.38) | collective-permute-done | bytes 737312 | tf_op jit(solution)/shard_map/ppermute | solution.py:59
  403.4 8.4 %shard_map.173 = (f32[1536,256]{1,0:T(8,128)}, bf16[1536,256]{1,0:T(8,128)(2,1)}, f32[1,256]{1,0:T(1,128)S(1)}) custom-call(s32[1]{0:T(128)} %bitcast.core_ref, s32[8]{0:T(128)S(1)} %copy-done.21, bf16[8,128,1536]{2,1,0:T(8,128)(2,1)} %copy-done.50, bf16[8,128,512]{2,1,0:T(8,128)(2,1)} %all-to-all-done.4.both_ref, ...), custom_call_target="tpu_custom_call" | custom-call | flops 2900000000 | bytes 1000 | tf_op jit(solution)/shard_map/pallas_call | solution.py:169
  420.6 7.9 %all-to-all-start.5 = ((bf16[8,208,256]{2,1,0:T(8,128)(2,1)}), bf16[8,208,256]{2,1,0:T(8,128)(2,1)S(1)}, u32[]{:S(2)}, u32[]{:S(2)}) async-start(bf16[8,208,256]{2,1,0:T(8,128)(2,1)} %shard_map.174), calls=%async_computation.6 | async-start | bytes 1703936 | tf_op jit(solution)/shard_map/all_to_all | solution.py:955
  433.7 12.5 %collective-permute-start.45 = (bf16[288,1280]{1,0:T(8,128)(2,1)}, bf16[288,1280]{1,0:T(8,128)(2,1)}, u32[]{:S(2)}, u32[]{:S(2)}) collective-permute-start(bf16[288,1280]{1,0:T(8,128)(2,1)} %pad_maximum_fusion.refs_0_), channel_id=1, source_target_pairs={{0,4},{2,6},{4,0},{6,2},{8,12},{10,14},{12,8},{14,10},{1,5},{3,7},... | collective-permute-start | bytes 2211848 | tf_op jit(solution)/shard_map/ppermute | solution.py:59
  455.4 7.9 %collective-permute-done.45.refs_4_ = bf16[288,1280]{1,0:T(8,128)(2,1)} collective-permute-done((bf16[288,1280]{1,0:T(8,128)(2,1)}, bf16[288,1280]{1,0:T(8,128)(2,1)}, u32[]{:S(2)}, u32[]{:S(2)}) %collective-permute-start.45) | collective-permute-done | bytes 737312 | tf_op jit(solution)/shard_map/ppermute | solution.py:59
  463.8 15.2 %collective-permute-done.42.refs_1_ = bf16[288,1280]{1,0:T(8,128)(2,1)} collective-permute-done((bf16[288,1280]{1,0:T(8,128)(2,1)}, bf16[288,1280]{1,0:T(8,128)(2,1)}, u32[]{:S(2)}, u32[]{:S(2)}) %collective-permute-start.42) | collective-permute-done | bytes 737312 | tf_op jit(solution)/shard_map/ppermute | solution.py:59
  487.4 12.7 %collective-permute-done.52.refs_0_ = bf16[288,1280]{1,0:T(8,128)(2,1)S(1)} collective-permute-done((bf16[288,1280]{1,0:T(8,128)(2,1)}, bf16[288,1280]{1,0:T(8,128)(2,1)S(1)}, u32[]{:S(2)}, u32[]{:S(2)}) %collective-permute-start.52) | collective-permute-done | bytes 737312 | tf_op jit(solution)/shard_map/ppermute | solution.py:59
  503.0 7.9 %shard_map.176 = (f32[192,17920]{1,0:T(8,128)}, f32[1120,1536]{1,0:T(8,128)}) custom-call(s32[1]{0:T(128)} %bitcast.core_ref, s32[8]{0:T(128)S(1)} %copy-done.21, bf16[288,1280]{1,0:T(8,128)(2,1)} %pad_maximum_fusion.refs_0_, bf16[288,1280]{1,0:T(8,128)(2,1)} %collective-permute-done.42.refs_1_, bf16[288,1280]{1,0:T(8,128)(2,1)} %collective-permute-done.43.refs_2_, ...), custom_call_target="tpu_custom_call" | custom-call | flops 5800000000 | bytes 1000 | tf_op jit(solution)/shard_map/pallas_call | solution.py:437
  (324 shorter events, 219.7 us)
Async XLA Ops:
  7.2 103.0 %all-gather.5.cloned.1.call-start = ((), (), s32[]{:S(2)}) async-start(), calls=%async_computation.8 | async-start | bytes 2654208 | tf_op jit(solution)/shard_map/all_gather | solution.py:856
  9.1 167.2 %all-gather.9.cloned.1.call-start = ((), (), s32[]{:S(2)}) async-start(), calls=%async_computation.11 | async-start | bytes 6635520 | tf_op jit(solution)/shard_map/all_gather | solution.py:869
  48.0 33.1 %all-to-all-start = ((bf16[8,208,256]{2,1,0:T(8,128)(2,1)}), bf16[8,208,256]{2,1,0:T(8,128)(2,1)}, u32[]{:S(2)}, u32[]{:S(2)}) async-start(bf16[8,208,256]{2,1,0:T(8,128)(2,1)} %broadcast_in_dim.35), calls=%async_computation | async-start | bytes 1703936 | tf_op jit(solution)/shard_map/all_to_all | solution.py:146
  74.3 24.2 %collective-permute-start.9 = (bf16[128,1536]{1,0:T(8,128)(2,1)S(1)}, bf16[128,1536]{1,0:T(8,128)(2,1)S(1)}, u32[]{:S(2)}, u32[]{:S(2)}) collective-permute-start(bf16[128,1536]{1,0:T(8,128)(2,1)S(1)} %bitcast.39), channel_id=1, source_target_pairs={{0,8},{2,10},{4,12},{6,14},{8,0},{10,2},{12,4},{14,6},{1,9},{3,11}... | collective-permute-start | bytes 1179656 | tf_op jit(solution)/shard_map/ppermute | solution.py:59
  110.2 34.8 %collective-permute-start.14 = (bf16[1536,768]{1,0:T(8,128)(2,1)}, bf16[1536,768]{1,0:T(8,128)(2,1)}, u32[]{:S(2)}, u32[]{:S(2)}) collective-permute-start(bf16[1536,768]{1,0:T(8,128)(2,1)} %all-gather.5.cloned.1.call-done.mine_ref), channel_id=1, source_target_pairs={{0,1},{1,0},{2,3},{3,2},{4,5},{5,4},{6,7},{7,6},{8,9},{9,8},{10,11... | collective-permute-start | bytes 7077896 | tf_op jit(solution)/shard_map/ppermute | solution.py:142
  115.3 26.2 %all-to-all-start.2 = ((bf16[8,128,512]{2,1,0:T(8,128)(2,1)}), bf16[8,128,512]{2,1,0:T(8,128)(2,1)S(1)}, u32[]{:S(2)}, u32[]{:S(2)}) async-start(bf16[8,128,512]{2,1,0:T(8,128)(2,1)} %broadcast_in_dim.38), calls=%async_computation.2 | async-start | bytes 2097152 | tf_op jit(solution)/shard_map/all_to_all | solution.py:146
  122.6 134.1 %all-gather.7.cloned.1.call-start = ((), (), s32[]{:S(2)}) async-start(), calls=%async_computation.9 | async-start | bytes 3538944 | tf_op jit(solution)/shard_map/all_gather | solution.py:903
  176.3 29.9 %collective-permute-start.23 = (bf16[8,288,1280]{2,1,0:T(8,128)(2,1)}, bf16[8,288,1280]{2,1,0:T(8,128)(2,1)}, u32[]{:S(2)}, u32[]{:S(2)}) collective-permute-start(bf16[8,288,1280]{2,1,0:T(8,128)(2,1)} %bitcast.56), channel_id=1, source_target_pairs={{0,1},{1,0},{2,3},{3,2},{4,5},{5,4},{6,7},{7,6},{8,9},{9,8},{10,11... | collective-permute-start | bytes 17694728 | tf_op jit(solution)/shard_map/ppermute | solution.py:142
  179.2 234.3 %reduce-scatter.2.cloned.1.call-start = ((), (), s32[]{:S(2)}) async-start(), calls=%async_computation.10 | async-start | bytes 3538944 | tf_op jit(solution)/shard_map/reduce_scatter | solution.py:929
  179.6 26.1 %collective-permute-start.15 = (bf16[256,1536]{1,0:T(8,128)(2,1)}, bf16[256,1536]{1,0:T(8,128)(2,1)S(1)}, u32[]{:S(2)}, u32[]{:S(2)}) collective-permute-start(bf16[256,1536]{1,0:T(8,128)(2,1)} %get-tuple-element.124.refs_0_), channel_id=1, source_target_pairs={{0,4},{2,6},{4,0},{6,2},{8,12},{10,14},{12,8},{14,10},{1,5},{3,7},... | collective-permute-start | bytes 2359304 | tf_op jit(solution)/shard_map/ppermute | solution.py:59
  203.0 27.5 %collective-permute-start.17 = (bf16[256,1536]{1,0:T(8,128)(2,1)S(1)}, bf16[256,1536]{1,0:T(8,128)(2,1)S(1)}, u32[]{:S(2)}, u32[]{:S(2)}) collective-permute-start(bf16[256,1536]{1,0:T(8,128)(2,1)S(1)} %collective-permute-done.16.refs_3_), channel_id=1, source_target_pairs={{0,2},{2,4},{4,6},{6,0},{8,10},{10,12},{12,14},{14,8},{1,3},{3,5},... | collective-permute-start | bytes 2359304 | tf_op jit(solution)/shard_map/ppermute | solution.py:59
  204.3 26.3 %collective-permute-start.18 = (bf16[256,1536]{1,0:T(8,128)(2,1)S(1)}, bf16[256,1536]{1,0:T(8,128)(2,1)S(1)}, u32[]{:S(2)}, u32[]{:S(2)}) collective-permute-start(bf16[256,1536]{1,0:T(8,128)(2,1)S(1)} %collective-permute-done.16.refs_3_), channel_id=1, source_target_pairs={{0,6},{2,0},{4,2},{6,4},{8,14},{10,8},{12,10},{14,12},{1,7},{3,1},... | collective-permute-start | bytes 2359304 | tf_op jit(solution)/shard_map/ppermute | solution.py:59
  205.7 24.9 %collective-permute-start.19 = (bf16[256,1536]{1,0:T(8,128)(2,1)S(1)}, bf16[256,1536]{1,0:T(8,128)(2,1)S(1)}, u32[]{:S(2)}, u32[]{:S(2)}) collective-permute-start(bf16[256,1536]{1,0:T(8,128)(2,1)S(1)} %collective-permute-done.15.refs_0_.refs_4_), channel_id=1, source_target_pairs={{0,8},{2,10},{4,12},{6,14},{8,0},{10,2},{12,4},{14,6},{1,9},{3,11}... | collective-permute-start | bytes 2359304 | tf_op jit(solution)/shard_map/ppermute | solution.py:59
  281.1 26.6 %collective-permute-start.24 = (bf16[128,1536]{1,0:T(8,128)(2,1)}, bf16[128,1536]{1,0:T(8,128)(2,1)S(1)}, u32[]{:S(2)}, u32[]{:S(2)}) collective-permute-start(bf16[128,1536]{1,0:T(8,128)(2,1)} %get-tuple-element.116), channel_id=1, source_target_pairs={{0,2},{2,4},{4,6},{6,0},{8,10},{10,12},{12,14},{14,8},{1,3},{3,5},... | collective-permute-start | bytes 1179656 | tf_op jit(solution)/shard_map/ppermute | solution.py:59
  312.0 26.0 %collective-permute-start.34 = (bf16[288,1280]{1,0:T(8,128)(2,1)}, bf16[288,1280]{1,0:T(8,128)(2,1)S(1)}, u32[]{:S(2)}, u32[]{:S(2)}) collective-permute-start(bf16[288,1280]{1,0:T(8,128)(2,1)} %get-tuple-element.143), channel_id=1, source_target_pairs={{0,64},{16,80},{32,96},{48,112},{64,0},{80,16},{96,32},{112,48},{1... | collective-permute-start | bytes 2211848 | tf_op jit(solution)/shard_map/ppermute | solution.py:59
  371.0 32.4 %all-to-all-start.4 = ((bf16[8,128,512]{2,1,0:T(8,128)(2,1)}), bf16[8,128,512]{2,1,0:T(8,128)(2,1)}, u32[]{:S(2)}, u32[]{:S(2)}) async-start(bf16[8,128,512]{2,1,0:T(8,128)(2,1)} %get-tuple-element.158), calls=%async_computation.5 | async-start | bytes 2097152 | tf_op jit(solution)/shard_map/all_to_all | solution.py:935
  378.5 24.9 %collective-permute-start.38 = (bf16[288,1280]{1,0:T(8,128)(2,1)}, bf16[288,1280]{1,0:T(8,128)(2,1)}, u32[]{:S(2)}, u32[]{:S(2)}) collective-permute-start(bf16[288,1280]{1,0:T(8,128)(2,1)} %add_convert_fusion.2), channel_id=1, source_target_pairs={{0,32},{16,48},{32,0},{48,16},{64,96},{80,112},{96,64},{112,80},{1... | collective-permute-start | bytes 2211848 | tf_op jit(solution)/shard_map/ppermute | solution.py:59
  420.6 28.5 %all-to-all-start.5 = ((bf16[8,208,256]{2,1,0:T(8,128)(2,1)}), bf16[8,208,256]{2,1,0:T(8,128)(2,1)S(1)}, u32[]{:S(2)}, u32[]{:S(2)}) async-start(bf16[8,208,256]{2,1,0:T(8,128)(2,1)} %shard_map.174), calls=%async_computation.6 | async-start | bytes 1703936 | tf_op jit(solution)/shard_map/all_to_all | solution.py:955
  430.7 24.7 %collective-permute-start.44 = (bf16[288,1280]{1,0:T(8,128)(2,1)}, bf16[288,1280]{1,0:T(8,128)(2,1)}, u32[]{:S(2)}, u32[]{:S(2)}) collective-permute-start(bf16[288,1280]{1,0:T(8,128)(2,1)} %pad_maximum_fusion.refs_0_), channel_id=1, source_target_pairs={{0,8},{2,10},{4,12},{6,14},{8,0},{10,2},{12,4},{14,6},{1,9},{3,11}... | collective-permute-start | bytes 2211848 | tf_op jit(solution)/shard_map/ppermute | solution.py:59
  433.7 29.6 %collective-permute-start.45 = (bf16[288,1280]{1,0:T(8,128)(2,1)}, bf16[288,1280]{1,0:T(8,128)(2,1)}, u32[]{:S(2)}, u32[]{:S(2)}) collective-permute-start(bf16[288,1280]{1,0:T(8,128)(2,1)} %pad_maximum_fusion.refs_0_), channel_id=1, source_target_pairs={{0,4},{2,6},{4,0},{6,2},{8,12},{10,14},{12,8},{14,10},{1,5},{3,7},... | collective-permute-start | bytes 2211848 | tf_op jit(solution)/shard_map/ppermute | solution.py:59
  446.3 32.7 %collective-permute-start.42 = (bf16[288,1280]{1,0:T(8,128)(2,1)}, bf16[288,1280]{1,0:T(8,128)(2,1)}, u32[]{:S(2)}, u32[]{:S(2)}) collective-permute-start(bf16[288,1280]{1,0:T(8,128)(2,1)} %pad_maximum_fusion.refs_0_), channel_id=1, source_target_pairs={{0,2},{2,4},{4,6},{6,0},{8,10},{10,12},{12,14},{14,8},{1,3},{3,5},... | collective-permute-start | bytes 2211848 | tf_op jit(solution)/shard_map/ppermute | solution.py:59
  446.3 34.3 %collective-permute-start.43 = (bf16[288,1280]{1,0:T(8,128)(2,1)}, bf16[288,1280]{1,0:T(8,128)(2,1)}, u32[]{:S(2)}, u32[]{:S(2)}) collective-permute-start(bf16[288,1280]{1,0:T(8,128)(2,1)} %pad_maximum_fusion.refs_0_), channel_id=1, source_target_pairs={{0,6},{2,0},{4,2},{6,4},{8,14},{10,8},{12,10},{14,12},{1,7},{3,1},... | collective-permute-start | bytes 2211848 | tf_op jit(solution)/shard_map/ppermute | solution.py:59
  448.9 32.7 %collective-permute-start.46 = (bf16[288,1280]{1,0:T(8,128)(2,1)}, bf16[288,1280]{1,0:T(8,128)(2,1)}, u32[]{:S(2)}, u32[]{:S(2)}) collective-permute-start(bf16[288,1280]{1,0:T(8,128)(2,1)} %pad_maximum_fusion.refs_0_), channel_id=1, source_target_pairs={{0,1},{1,0},{2,3},{3,2},{4,5},{5,4},{6,7},{7,6},{8,9},{9,8},{10,11... | collective-permute-start | bytes 2211848 | tf_op jit(solution)/shard_map/ppermute | solution.py:142
  483.8 27.1 %all-to-all-start.6 = ((bf16[8,208,256]{2,1,0:T(8,128)(2,1)}), bf16[8,208,256]{2,1,0:T(8,128)(2,1)S(1)}, u32[]{:S(2)}, u32[]{:S(2)}) async-start(bf16[8,208,256]{2,1,0:T(8,128)(2,1)} %shard_map.175), calls=%async_computation.7 | async-start | bytes 1703936 | tf_op jit(solution)/shard_map/all_to_all | solution.py:963
  (116 other events, 1531.8 us)
Sparse Core Ops, SparseCore 0:
  10.3 67.1 all-gather.4
  80.4 95.8 all-gather.8
  179.3 72.6 all-gather.6
  307.8 66.1 reduce-scatter.1

commit v3 on v2

--- a/solution.py
+++ b/solution.py
@@ -898,7 +898,7 @@
     )
 
     h_blocks = send_out(normed_two, PLANE)
-    feed_other = swap(after(feed_mine, *h_blocks[1:3]))
+    feed_other = swap(after(feed_mine, *h_blocks[1:5]))
     qkv_half = lax.dynamic_slice(w_qkv, (0, core * 1024), (SHARD, 1024))
     qkv_mine = lax.all_gather(after(qkv_half, normed_two), GROUP, axis=0, tiled=True)
     held, back_blocks = (), {}
@@ -954,8 +954,9 @@
     mlp_grad = jnp.concatenate([mlp_grad[:SHARD], down_grad], axis=0)
     payload = lax.all_to_all(payload, GROUP, 0, 0, tiled=True)
     grad_blocks = send_out(mlp_grad, PLANE, hold=(payload,))
-    other_blocks = [swap(b) for b in grad_blocks]
+    other_blocks = [swap(b) for b in grad_blocks[:5]]
     feed_grads = write_grads(which, order, grad_blocks, other_blocks, 0, 5, ())
+    other_blocks += [swap(b) for b in after(tuple(grad_blocks[5:]), *feed_grads)]
     gate_up_grad, down_grad = write_grads(which, order, grad_blocks, other_blocks, 5, 8, feed_grads)
 
 

time: 538 us -> 533 us (level)
  waiting for transfers between devices: 163 us -> 142 us
  starting transfers between devices: 126 us -> 137 us
  local copies, waits for them, and re-layouts: 40.1 us -> 47.5 us
    ppermute x42, waiting for transfers between devices: 147 us -> 125 us  [send(): return lax.ppermute(block, axes, shift_pairs(offset))]
    ppermute x14, starting transfers between devices: 22.2 us -> 38 us  [swap(): return lax.ppermute(block, 'c', [(0, 1), (1, 0)])]
    all_gather x1, waiting for transfers between devices: 7.77 us -> 0.01 us  [on_device(): feed_mine = lax.all_gather(after(packed, x_blocks[1]), GROUP, axis=0)]
    unnamed x144 -> x164, local copies, waits for them, and re-layouts: 25.9 us -> 33.4 us
  transfers between devices with their start and end apart: 67 -> 67, of which waited for: 21 -> 24; matrix products, arithmetic and copies ran while one was open for 4% -> 4% of each run, Pallas kernels for 24% -> 24%
where the time goes in v3:
time: 533 us; the launch traced here: 524 us
  waiting for transfers between devices  142 us (27%)
  Pallas kernels  141 us (26%)
  starting transfers between devices  137 us (26%)
  local copies, waits for them, and re-layouts  47.5 us (9%)
  blocking collectives  31.3 us (6%)
  between operations  15.1 us (3%)
  other arithmetic  9.47 us (2%)
    ppermute x42, waiting for transfers between devices, send(): return lax.ppermute(block, axes, shift_pairs(offset))  125 us
    ppermute x42, starting transfers between devices, send(): return lax.ppermute(block, axes, shift_pairs(offset))  62.6 us
    pallas_call x9, Pallas kernels, call(): pl.pallas_call(kernel, in_specs=in_specs, out_specs=[pl.BlockSpec(memory_...  51.4 us
    pallas_call x2, Pallas kernels, feed(): pl.pallas_call(functools.partial(feed_kernel, len(held)), grid=(1,), in_s...  49.8 us
    ppermute x14, starting transfers between devices, swap(): return lax.ppermute(block, 'c', [(0, 1), (1, 0)])  38 us
    unnamed x164, local copies, waits for them, and re-layouts  33.4 us
    all_to_all x1, blocking collectives, on_device(): grad_kv = lax.all_to_all(grad_kv, GROUP, 0, 0, tiled=True)  21.1 us
    pallas_call x2, Pallas kernels, write_grads(): pl.pallas_call(functools.partial(write_kernel, low, count, len(held)), in...  13 us
  transfers between devices with their start and end apart: 67, of which 24 were waited for; matrix products, arithmetic and copies ran while one was open for 4% of the time, Pallas kernels for 24%

profile of v3, /device:TPU:7, one launch (start us, length us, event | category | flops | bytes accessed | tf_op | source)
XLA Modules:
  0.0 523.7 jit_solution(4704002052087233479)
XLA Ops:
  18.0 6.9 %collective-permute-done.20.piece_ref = bf16[80,1536]{1,0:T(8,128)(2,1)S(1)} collective-permute-done((bf16[80,1536]{1,0:T(8,128)(2,1)}, bf16[80,1536]{1,0:T(8,128)(2,1)S(1)}, u32[]{:S(2)}, u32[]{:S(2)}) %collective-permute-start.20) | collective-permute-done | bytes 245792 | tf_op jit(solution)/shard_map/ppermute | solution.py:858
  37.3 9.7 %collective-permute-done.1.refs_2_ = bf16[128,1536]{1,0:T(8,128)(2,1)S(1)} collective-permute-done((bf16[128,1536]{1,0:T(8,128)(2,1)S(1)}, bf16[128,1536]{1,0:T(8,128)(2,1)S(1)}, u32[]{:S(2)}, u32[]{:S(2)}) %collective-permute-start.1) | collective-permute-done | bytes 393248 | tf_op jit(solution)/shard_map/ppermute | solution.py:59
  100.0 10.2 %all_to_all.35.heads_ref = bf16[8,128,256]{2,1,0:T(8,128)(2,1)S(1)} all-to-all(bf16[8,128,256]{2,1,0:T(8,128)(2,1)S(1)} %get-tuple-element.104), channel_id=1, replica_groups=mesh['yh'=2,'x'=4,'yl'=2,'z'=4,'c'=2] {'yl','z'}, dimensions={0} | all-to-all | bytes 1048576 | tf_op jit(solution)/shard_map/all_to_all | solution.py:887
  115.3 7.3 %all-to-all-start.2 = ((bf16[8,128,512]{2,1,0:T(8,128)(2,1)}), bf16[8,128,512]{2,1,0:T(8,128)(2,1)S(1)}, u32[]{:S(2)}, u32[]{:S(2)}) async-start(bf16[8,128,512]{2,1,0:T(8,128)(2,1)} %broadcast_in_dim.38), calls=%async_computation.2 | async-start | bytes 2097152 | tf_op jit(solution)/shard_map/all_to_all | solution.py:146
  126.5 8.4 %collective-permute-done.11.refs_5_ = bf16[128,1536]{1,0:T(8,128)(2,1)S(1)} collective-permute-done((bf16[128,1536]{1,0:T(8,128)(2,1)S(1)}, bf16[128,1536]{1,0:T(8,128)(2,1)S(1)}, u32[]{:S(2)}, u32[]{:S(2)}) %collective-permute-start.11) | collective-permute-done | bytes 393248 | tf_op jit(solution)/shard_map/ppermute | solution.py:59
  134.9 6.6 %collective-permute-done.13.refs_7_ = bf16[128,1536]{1,0:T(8,128)(2,1)} collective-permute-done((bf16[128,1536]{1,0:T(8,128)(2,1)S(1)}, bf16[128,1536]{1,0:T(8,128)(2,1)}, u32[]{:S(2)}, u32[]{:S(2)}) %collective-permute-start.13) | collective-permute-done | bytes 393248 | tf_op jit(solution)/shard_map/ppermute | solution.py:59
  154.9 12.6 %collective-permute-done.15.refs_0_.refs_4_ = bf16[256,1536]{1,0:T(8,128)(2,1)S(1)} collective-permute-done((bf16[256,1536]{1,0:T(8,128)(2,1)S(1)}, bf16[256,1536]{1,0:T(8,128)(2,1)S(1)}, u32[]{:S(2)}, u32[]{:S(2)}) %collective-permute-start.15) | collective-permute-done | bytes 786464 | tf_op jit(solution)/shard_map/ppermute | solution.py:59
  167.5 12.1 %collective-permute-done.16.refs_3_ = bf16[256,1536]{1,0:T(8,128)(2,1)S(1)} collective-permute-done((bf16[256,1536]{1,0:T(8,128)(2,1)S(1)}, bf16[256,1536]{1,0:T(8,128)(2,1)S(1)}, u32[]{:S(2)}, u32[]{:S(2)}) %collective-permute-start.16) | collective-permute-done | bytes 786464 | tf_op jit(solution)/shard_map/ppermute | solution.py:59
  179.6 6.8 %collective-permute-done.21.refs_1_ = bf16[256,1536]{1,0:T(8,128)(2,1)S(1)} collective-permute-done((bf16[256,1536]{1,0:T(8,128)(2,1)S(1)}, bf16[256,1536]{1,0:T(8,128)(2,1)S(1)}, u32[]{:S(2)}, u32[]{:S(2)}) %collective-permute-start.21) | collective-permute-done | bytes 786464 | tf_op jit(solution)/shard_map/ppermute | solution.py:59
  197.4 24.7 %shard_map.165 = (bf16[1024,640]{1,0:T(8,128)(2,1)}, bf16[1024,640]{1,0:T(8,128)(2,1)}, bf16[1024,1280]{1,0:T(8,128)(2,1)}, bf16[1024,1280]{1,0:T(8,128)(2,1)}, ...) custom-call(s32[8]{0:T(128)} %copy-done.20, ...), custom_call_target="tpu_custom_call" | custom-call | flops 12179999744 | bytes 1000 | tf_op jit(solution)/shard_map/pallas_call | solution.py:767
  223.5 25.1 %shard_map.166 = (bf16[1024,640]{1,0:T(8,128)(2,1)}, bf16[1024,640]{1,0:T(8,128)(2,1)}, bf16[1024,1280]{1,0:T(8,128)(2,1)}, bf16[1024,1280]{1,0:T(8,128)(2,1)}, ...) custom-call(s32[8]{0:T(128)} %copy-done.20, ...), custom_call_target="tpu_custom_call", output_to_operand_aliasing={{0}: (8, {}), {1}: (9, {}), {2}: (10, {}), {3}: (11, {}), {... | custom-call | flops 12179999744 | bytes 1000 | tf_op jit(solution)/shard_map/pallas_call | solution.py:767
  257.9 13.7 %shard_map.167 = bf16[8,288,1280]{2,1,0:T(8,128)(2,1)} custom-call(s32[8]{0:T(128)S(1)} %copy-done.22, bf16[256,1536]{1,0:T(8,128)(2,1)S(1)} %copy-done.27, bf16[256,1536]{1,0:T(8,128)(2,1)S(1)} %copy-done.38, bf16[256,1536]{1,0:T(8,128)(2,1)} %collective-permute-done.22.refs_2_, bf16[256,1536]{1,0:T(8,128)(2,1)S(1)} %copy-done.35, ...), custom_call_target="tpu_custom_call" | custom-call | flops 6206000128 | bytes 1000 | tf_op jit(solution)/shard_map/pallas_call | solution.py:169
  277.7 8.4 %collective-permute-done.28 = bf16[128,1536]{1,0:T(8,128)(2,1)S(1)} collective-permute-done((bf16[128,1536]{1,0:T(8,128)(2,1)}, bf16[128,1536]{1,0:T(8,128)(2,1)S(1)}, u32[]{:S(2)}, u32[]{:S(2)}) %collective-permute-start.28) | collective-permute-done | bytes 393248 | tf_op jit(solution)/shard_map/ppermute | solution.py:59
  290.3 15.0 %shard_map.168 = (bf16[288,1280]{1,0:T(8,128)(2,1)}, bf16[288,1280]{1,0:T(8,128)(2,1)}, bf16[288,1280]{1,0:T(8,128)(2,1)}, bf16[288,1280]{1,0:T(8,128)(2,1)}, bf...) custom-call(s32[8]{0:T(128)} %copy-done.20, ...), custom_call_target="tpu_custom_call" | custom-call | flops 8700000256 | bytes 1000 | tf_op jit(solution)/shard_map/pallas_call | solution.py:169
  317.9 8.7 %shard_map.170 = (bf16[128,1536]{1,0:T(8,128)(2,1)}, bf16[8,128,512]{2,1,0:T(8,128)(2,1)}) custom-call(s32[1]{0:T(128)} %bitcast.1.me_ref.group_ref, bf16[8,128,256]{2,1,0:T(8,128)(2,1)} %copy-done.6, bf16[8,128,512]{2,1,0:T(8,128)(2,1)} %copy-done.3, bf16[128,1536]{1,0:T(8,128)(2,1)} %copy-done.67, f32[12,128,1]{2,1,0:T(8,128)} %copy-done.70, ...), custom_call_target="tpu_custom_call" | custom-call | flops 5219999744 | bytes 1000 | tf_op jit(solution)/shard_map/pallas_call | solution.py:607
  330.4 21.1 %all_to_all.36.dkv_ref = bf16[8,128,512]{2,1,0:T(8,128)(2,1)S(1)} all-to-all(bf16[8,128,512]{2,1,0:T(8,128)(2,1)} %get-tuple-element.158), channel_id=1, replica_groups=mesh['yh'=2,'x'=4,'yl'=2,'z'=4,'c'=2] {'yh','x'}, dimensions={0} | all-to-all | bytes 2097152 | tf_op jit(solution)/shard_map/all_to_all | solution.py:926
  352.7 14.4 %collective-permute-start.35 = (bf16[1536,1024]{1,0:T(8,128)(2,1)}, bf16[1536,1024]{1,0:T(8,128)(2,1)}, u32[]{:S(2)}, u32[]{:S(2)}) collective-permute-start(bf16[1536,1024]{1,0:T(8,128)(2,1)} %all-gather.7.cloned.1.call-done.mine_ref), channel_id=1, source_target_pairs={{0,1},{1,0},{2,3},{3,2},{4,5},{5,4},{6,7},{7,6},{8,9},{9,8},{10,11... | collective-permute-start | bytes 9437192 | tf_op jit(solution)/shard_map/ppermute | solution.py:142
  380.1 6.3 %shard_map.172 = (f32[128,1536]{1,0:T(8,128)}, f32[1,1536]{1,0:T(1,128)S(1)}) custom-call(s32[1]{0:T(128)} %bitcast.core_ref, bf16[128,2048]{1,0:T(8,128)(2,1)S(1)} %copy-done.62, bf16[1536,1024]{1,0:T(8,128)(2,1)} %all-gather.7.cloned.1.call-done.mine_ref, bf16[1536,1024]{1,0:T(8,128)(2,1)} %collective-permute-done.35.other_ref, ...), custom_call_target="tpu_custom_call" | custom-call | flops 2900000000 | bytes 1000 | tf_op jit(solution)/shard_map/pallas_call | solution.py:169
  389.0 12.9 %collective-permute-done.38 = bf16[288,1280]{1,0:T(8,128)(2,1)} collective-permute-done((bf16[288,1280]{1,0:T(8,128)(2,1)}, bf16[288,1280]{1,0:T(8,128)(2,1)}, u32[]{:S(2)}, u32[]{:S(2)}) %collective-permute-start.38) | collective-permute-done | bytes 737312 | tf_op jit(solution)/shard_map/ppermute | solution.py:59
  404.1 8.7 %shard_map.173 = (f32[1536,256]{1,0:T(8,128)}, bf16[1536,256]{1,0:T(8,128)(2,1)}, f32[1,256]{1,0:T(1,128)S(1)}) custom-call(s32[1]{0:T(128)} %bitcast.core_ref, s32[8]{0:T(128)S(1)} %copy-done.23, bf16[8,128,1536]{2,1,0:T(8,128)(2,1)} %copy-done.60, bf16[8,128,512]{2,1,0:T(8,128)(2,1)} %all-to-all-done.4.both_ref, bf16[256,1536]{1,0:T(8,128)(2,1)S(1)} %copy-done.28, ...), custom_call_target="tpu_custom_call" | custom-call | flops 2900000000 | bytes 1000 | tf_op jit(solution)/shard_map/pallas_call | solution.py:169
  421.9 8.0 %all-to-all-start.5 = ((bf16[8,208,256]{2,1,0:T(8,128)(2,1)}), bf16[8,208,256]{2,1,0:T(8,128)(2,1)S(1)}, u32[]{:S(2)}, u32[]{:S(2)}) async-start(bf16[8,208,256]{2,1,0:T(8,128)(2,1)} %shard_map.174), calls=%async_computation.6 | async-start | bytes 1703936 | tf_op jit(solution)/shard_map/all_to_all | solution.py:955
  430.6 12.0 %collective-permute-start.45 = (bf16[288,1280]{1,0:T(8,128)(2,1)S(1)}, bf16[288,1280]{1,0:T(8,128)(2,1)}, u32[]{:S(2)}, u32[]{:S(2)}) collective-permute-start(bf16[288,1280]{1,0:T(8,128)(2,1)S(1)} %pad_maximum_fusion.refs_0_), channel_id=1, source_target_pairs={{0,4},{2,6},{4,0},{6,2},{8,12},{10,14},{12,8},{14,10},{1,5},{3,7},... | collective-permute-start | bytes 2211848 | tf_op jit(solution)/shard_map/ppermute | solution.py:59
  462.9 12.6 %collective-permute-done.42.refs_1_ = bf16[288,1280]{1,0:T(8,128)(2,1)} collective-permute-done((bf16[288,1280]{1,0:T(8,128)(2,1)S(1)}, bf16[288,1280]{1,0:T(8,128)(2,1)}, u32[]{:S(2)}, u32[]{:S(2)}) %collective-permute-start.42) | collective-permute-done | bytes 737312 | tf_op jit(solution)/shard_map/ppermute | solution.py:59
  484.7 8.2 %shard_map.176 = (f32[192,17920]{1,0:T(8,128)}, f32[1120,1536]{1,0:T(8,128)}) custom-call(s32[1]{0:T(128)} %bitcast.core_ref, s32[8]{0:T(128)S(1)} %copy-done.23, bf16[288,1280]{1,0:T(8,128)(2,1)S(1)} %copy-done.8, bf16[288,1280]{1,0:T(8,128)(2,1)} %collective-permute-done.42.refs_1_, bf16[288,1280]{1,0:T(8,128)(2,1)} %collective-permute-done.43.refs_2_, ...), custom_call_target="tpu_custom_call" | custom-call | flops 5800000000 | bytes 1000 | tf_op jit(solution)/shard_map/pallas_call | solution.py:437
  (344 shorter events, 228.3 us)
Async XLA Ops:
  7.2 103.0 %all-gather.5.cloned.1.call-start = ((), (), s32[]{:S(2)}) async-start(), calls=%async_computation.8 | async-start | bytes 2654208 | tf_op jit(solution)/shard_map/all_gather | solution.py:856
  9.1 178.2 %all-gather.9.cloned.1.call-start = ((), (), s32[]{:S(2)}) async-start(), calls=%async_computation.11 | async-start | bytes 6635520 | tf_op jit(solution)/shard_map/all_gather | solution.py:869
  48.0 33.1 %all-to-all-start = ((bf16[8,208,256]{2,1,0:T(8,128)(2,1)}), bf16[8,208,256]{2,1,0:T(8,128)(2,1)}, u32[]{:S(2)}, u32[]{:S(2)}) async-start(bf16[8,208,256]{2,1,0:T(8,128)(2,1)} %broadcast_in_dim.35), calls=%async_computation | async-start | bytes 1703936 | tf_op jit(solution)/shard_map/all_to_all | solution.py:146
  110.2 34.8 %collective-permute-start.14 = (bf16[1536,768]{1,0:T(8,128)(2,1)}, bf16[1536,768]{1,0:T(8,128)(2,1)}, u32[]{:S(2)}, u32[]{:S(2)}) collective-permute-start(bf16[1536,768]{1,0:T(8,128)(2,1)} %all-gather.5.cloned.1.call-done.mine_ref), channel_id=1, source_target_pairs={{0,1},{1,0},{2,3},{3,2},{4,5},{5,4},{6,7},{7,6},{8,9},{9,8},{10,11... | collective-permute-start | bytes 7077896 | tf_op jit(solution)/shard_map/ppermute | solution.py:142
  115.3 26.2 %all-to-all-start.2 = ((bf16[8,128,512]{2,1,0:T(8,128)(2,1)}), bf16[8,128,512]{2,1,0:T(8,128)(2,1)S(1)}, u32[]{:S(2)}, u32[]{:S(2)}) async-start(bf16[8,128,512]{2,1,0:T(8,128)(2,1)} %broadcast_in_dim.38), calls=%async_computation.2 | async-start | bytes 2097152 | tf_op jit(solution)/shard_map/all_to_all | solution.py:146
  122.6 130.8 %all-gather.7.cloned.1.call-start = ((), (), s32[]{:S(2)}) async-start(), calls=%async_computation.9 | async-start | bytes 3538944 | tf_op jit(solution)/shard_map/all_gather | solution.py:903
  151.2 28.4 %collective-permute-start.16 = (bf16[256,1536]{1,0:T(8,128)(2,1)S(1)}, bf16[256,1536]{1,0:T(8,128)(2,1)S(1)}, u32[]{:S(2)}, u32[]{:S(2)}) collective-permute-start(bf16[256,1536]{1,0:T(8,128)(2,1)S(1)} %get-tuple-element.127.refs_0_), channel_id=1, source_target_pairs={{0,8},{2,10},{4,12},{6,14},{8,0},{10,2},{12,4},{14,6},{1,9},{3,11}... | collective-permute-start | bytes 2359304 | tf_op jit(solution)/shard_map/ppermute | solution.py:59
  152.2 34.2 %collective-permute-start.21 = (bf16[256,1536]{1,0:T(8,128)(2,1)S(1)}, bf16[256,1536]{1,0:T(8,128)(2,1)S(1)}, u32[]{:S(2)}, u32[]{:S(2)}) collective-permute-start(bf16[256,1536]{1,0:T(8,128)(2,1)S(1)} %get-tuple-element.127.refs_0_), channel_id=1, source_target_pairs={{0,2},{2,4},{4,6},{6,0},{8,10},{10,12},{12,14},{14,8},{1,3},{3,5},... | collective-permute-start | bytes 2359304 | tf_op jit(solution)/shard_map/ppermute | solution.py:59
  152.7 34.7 %collective-permute-start.22 = (bf16[256,1536]{1,0:T(8,128)(2,1)S(1)}, bf16[256,1536]{1,0:T(8,128)(2,1)}, u32[]{:S(2)}, u32[]{:S(2)}) collective-permute-start(bf16[256,1536]{1,0:T(8,128)(2,1)S(1)} %get-tuple-element.127.refs_0_), channel_id=1, source_target_pairs={{0,6},{2,0},{4,2},{6,4},{8,14},{10,8},{12,10},{14,12},{1,7},{3,1},... | collective-permute-start | bytes 2359304 | tf_op jit(solution)/shard_map/ppermute | solution.py:59
  189.6 225.1 %reduce-scatter.2.cloned.1.call-start = ((), (), s32[]{:S(2)}) async-start(), calls=%async_computation.10 | async-start | bytes 3538944 | tf_op jit(solution)/shard_map/reduce_scatter | solution.py:929
  193.4 28.8 %collective-permute-start.17 = (bf16[256,1536]{1,0:T(8,128)(2,1)S(1)}, bf16[256,1536]{1,0:T(8,128)(2,1)S(1)}, u32[]{:S(2)}, u32[]{:S(2)}) collective-permute-start(bf16[256,1536]{1,0:T(8,128)(2,1)S(1)} %copy-done.34), channel_id=1, source_target_pairs={{0,2},{2,4},{4,6},{6,0},{8,10},{10,12},{12,14},{14,8},{1,3},{3,5},... | collective-permute-start | bytes 2359304 | tf_op jit(solution)/shard_map/ppermute | solution.py:59
  194.5 27.7 %collective-permute-start.18 = (bf16[256,1536]{1,0:T(8,128)(2,1)S(1)}, bf16[256,1536]{1,0:T(8,128)(2,1)S(1)}, u32[]{:S(2)}, u32[]{:S(2)}) collective-permute-start(bf16[256,1536]{1,0:T(8,128)(2,1)S(1)} %copy-done.34), channel_id=1, source_target_pairs={{0,6},{2,0},{4,2},{6,4},{8,14},{10,8},{12,10},{14,12},{1,7},{3,1},... | collective-permute-start | bytes 2359304 | tf_op jit(solution)/shard_map/ppermute | solution.py:59
  196.0 26.1 %collective-permute-start.19 = (bf16[256,1536]{1,0:T(8,128)(2,1)S(1)}, bf16[256,1536]{1,0:T(8,128)(2,1)S(1)}, u32[]{:S(2)}, u32[]{:S(2)}) collective-permute-start(bf16[256,1536]{1,0:T(8,128)(2,1)S(1)} %copy-done.30), channel_id=1, source_target_pairs={{0,8},{2,10},{4,12},{6,14},{8,0},{10,2},{12,4},{14,6},{1,9},{3,11}... | collective-permute-start | bytes 2359304 | tf_op jit(solution)/shard_map/ppermute | solution.py:59
  277.6 27.7 %collective-permute-start.24 = (bf16[128,1536]{1,0:T(8,128)(2,1)}, bf16[128,1536]{1,0:T(8,128)(2,1)S(1)}, u32[]{:S(2)}, u32[]{:S(2)}) collective-permute-start(bf16[128,1536]{1,0:T(8,128)(2,1)} %get-tuple-element.119), channel_id=1, source_target_pairs={{0,2},{2,4},{4,6},{6,0},{8,10},{10,12},{12,14},{14,8},{1,3},{3,5},... | collective-permute-start | bytes 1179656 | tf_op jit(solution)/shard_map/ppermute | solution.py:59
  352.7 24.2 %collective-permute-start.35 = (bf16[1536,1024]{1,0:T(8,128)(2,1)}, bf16[1536,1024]{1,0:T(8,128)(2,1)}, u32[]{:S(2)}, u32[]{:S(2)}) collective-permute-start(bf16[1536,1024]{1,0:T(8,128)(2,1)} %all-gather.7.cloned.1.call-done.mine_ref), channel_id=1, source_target_pairs={{0,1},{1,0},{2,3},{3,2},{4,5},{5,4},{6,7},{7,6},{8,9},{9,8},{10,11... | collective-permute-start | bytes 9437192 | tf_op jit(solution)/shard_map/ppermute | solution.py:142
  370.0 31.8 %all-to-all-start.4 = ((bf16[8,128,512]{2,1,0:T(8,128)(2,1)}), bf16[8,128,512]{2,1,0:T(8,128)(2,1)}, u32[]{:S(2)}, u32[]{:S(2)}) async-start(bf16[8,128,512]{2,1,0:T(8,128)(2,1)} %get-tuple-element.161), calls=%async_computation.5 | async-start | bytes 2097152 | tf_op jit(solution)/shard_map/all_to_all | solution.py:935
  375.4 26.4 %collective-permute-start.38 = (bf16[288,1280]{1,0:T(8,128)(2,1)}, bf16[288,1280]{1,0:T(8,128)(2,1)}, u32[]{:S(2)}, u32[]{:S(2)}) collective-permute-start(bf16[288,1280]{1,0:T(8,128)(2,1)} %add_convert_fusion.2), channel_id=1, source_target_pairs={{0,32},{16,48},{32,0},{48,16},{64,96},{80,112},{96,64},{112,80},{1... | collective-permute-start | bytes 2211848 | tf_op jit(solution)/shard_map/ppermute | solution.py:59
  421.9 27.5 %all-to-all-start.5 = ((bf16[8,208,256]{2,1,0:T(8,128)(2,1)}), bf16[8,208,256]{2,1,0:T(8,128)(2,1)S(1)}, u32[]{:S(2)}, u32[]{:S(2)}) async-start(bf16[8,208,256]{2,1,0:T(8,128)(2,1)} %shard_map.174), calls=%async_computation.6 | async-start | bytes 1703936 | tf_op jit(solution)/shard_map/all_to_all | solution.py:955
  430.5 24.7 %collective-permute-start.44 = (bf16[288,1280]{1,0:T(8,128)(2,1)S(1)}, bf16[288,1280]{1,0:T(8,128)(2,1)}, u32[]{:S(2)}, u32[]{:S(2)}) collective-permute-start(bf16[288,1280]{1,0:T(8,128)(2,1)S(1)} %pad_maximum_fusion.refs_0_), channel_id=1, source_target_pairs={{0,8},{2,10},{4,12},{6,14},{8,0},{10,2},{12,4},{14,6},{1,9},{3,11}... | collective-permute-start | bytes 2211848 | tf_op jit(solution)/shard_map/ppermute | solution.py:59
  430.6 26.5 %collective-permute-start.45 = (bf16[288,1280]{1,0:T(8,128)(2,1)S(1)}, bf16[288,1280]{1,0:T(8,128)(2,1)}, u32[]{:S(2)}, u32[]{:S(2)}) collective-permute-start(bf16[288,1280]{1,0:T(8,128)(2,1)S(1)} %pad_maximum_fusion.refs_0_), channel_id=1, source_target_pairs={{0,4},{2,6},{4,0},{6,2},{8,12},{10,14},{12,8},{14,10},{1,5},{3,7},... | collective-permute-start | bytes 2211848 | tf_op jit(solution)/shard_map/ppermute | solution.py:59
  442.6 32.9 %collective-permute-start.42 = (bf16[288,1280]{1,0:T(8,128)(2,1)S(1)}, bf16[288,1280]{1,0:T(8,128)(2,1)}, u32[]{:S(2)}, u32[]{:S(2)}) collective-permute-start(bf16[288,1280]{1,0:T(8,128)(2,1)S(1)} %pad_maximum_fusion.refs_0_), channel_id=1, source_target_pairs={{0,2},{2,4},{4,6},{6,0},{8,10},{10,12},{12,14},{14,8},{1,3},{3,5},... | collective-permute-start | bytes 2211848 | tf_op jit(solution)/shard_map/ppermute | solution.py:59
  442.6 33.3 %collective-permute-start.43 = (bf16[288,1280]{1,0:T(8,128)(2,1)S(1)}, bf16[288,1280]{1,0:T(8,128)(2,1)}, u32[]{:S(2)}, u32[]{:S(2)}) collective-permute-start(bf16[288,1280]{1,0:T(8,128)(2,1)S(1)} %pad_maximum_fusion.refs_0_), channel_id=1, source_target_pairs={{0,6},{2,0},{4,2},{6,4},{8,14},{10,8},{12,10},{14,12},{1,7},{3,1},... | collective-permute-start | bytes 2211848 | tf_op jit(solution)/shard_map/ppermute | solution.py:59
  445.3 30.7 %collective-permute-start.46 = (bf16[288,1280]{1,0:T(8,128)(2,1)S(1)}, bf16[288,1280]{1,0:T(8,128)(2,1)}, u32[]{:S(2)}, u32[]{:S(2)}) collective-permute-start(bf16[288,1280]{1,0:T(8,128)(2,1)S(1)} %pad_maximum_fusion.refs_0_), channel_id=1, source_target_pairs={{0,1},{1,0},{2,3},{3,2},{4,5},{5,4},{6,7},{7,6},{8,9},{9,8},{10,11... | collective-permute-start | bytes 2211848 | tf_op jit(solution)/shard_map/ppermute | solution.py:142
  479.8 25.2 %all-to-all-start.6 = ((bf16[8,208,256]{2,1,0:T(8,128)(2,1)}), bf16[8,208,256]{2,1,0:T(8,128)(2,1)S(1)}, u32[]{:S(2)}, u32[]{:S(2)}) async-start(bf16[8,208,256]{2,1,0:T(8,128)(2,1)} %shard_map.175), calls=%async_computation.7 | async-start | bytes 1703936 | tf_op jit(solution)/shard_map/all_to_all | solution.py:964
  (126 other events, 1555.7 us)
Sparse Core Ops, SparseCore 0:
  10.3 67.1 all-gather.4
  80.4 104.4 all-gather.8
  189.7 63.6 all-gather.6
  305.5 63.2 reduce-scatter.1

commit v4 on v3

--- a/solution.py
+++ b/solution.py
@@ -898,7 +898,7 @@
     )
 
     h_blocks = send_out(normed_two, PLANE)
-    feed_other = swap(after(feed_mine, *h_blocks[1:5]))
+    feed_other = swap(after(feed_mine, *h_blocks[3:5]))
     qkv_half = lax.dynamic_slice(w_qkv, (0, core * 1024), (SHARD, 1024))
     qkv_mine = lax.all_gather(after(qkv_half, normed_two), GROUP, axis=0, tiled=True)
     held, back_blocks = (), {}

time: 533 us -> 536 us (level)
  waiting for transfers between devices: 142 us -> 155 us
  starting transfers between devices: 137 us -> 129 us
    ppermute x14, starting transfers between devices: 38 us -> 23.5 us  [swap(): return lax.ppermute(block, 'c', [(0, 1), (1, 0)])]
    ppermute x42, waiting for transfers between devices: 125 us -> 138 us  [send(): return lax.ppermute(block, axes, shift_pairs(offset))]
    unnamed x164 -> x148, local copies, waits for them, and re-layouts: 33.4 us -> 28.8 us
  transfers between devices with their start and end apart: 67 -> 67, of which waited for: 24 -> 22; matrix products, arithmetic and copies ran while one was open for 4% -> 4% of each run, Pallas kernels for 24% -> 24%
where the time goes in v4:
time: 536 us; the launch traced here: 526 us
  waiting for transfers between devices  155 us (29%)
  Pallas kernels  141 us (26%)
  starting transfers between devices  129 us (24%)
  local copies, waits for them, and re-layouts  43 us (8%)
  blocking collectives  34.1 us (6%)
  between operations  15 us (3%)
  other arithmetic  9.47 us (2%)
    ppermute x42, waiting for transfers between devices, send(): return lax.ppermute(block, axes, shift_pairs(offset))  138 us
    ppermute x42, starting transfers between devices, send(): return lax.ppermute(block, axes, shift_pairs(offset))  67.3 us
    pallas_call x9, Pallas kernels, call(): pl.pallas_call(kernel, in_specs=in_specs, out_specs=[pl.BlockSpec(memory_...  50.7 us
    pallas_call x2, Pallas kernels, feed(): pl.pallas_call(functools.partial(feed_kernel, len(held)), grid=(1,), in_s...  49 us
    unnamed x148, local copies, waits for them, and re-layouts  28.8 us
    all_to_all x1, blocking collectives, on_device(): grad_kv = lax.all_to_all(grad_kv, GROUP, 0, 0, tiled=True)  23.9 us
    ppermute x14, starting transfers between devices, swap(): return lax.ppermute(block, 'c', [(0, 1), (1, 0)])  23.5 us
    pallas_call x2, Pallas kernels, write_grads(): pl.pallas_call(functools.partial(write_kernel, low, count, len(held)), in...  13 us
  transfers between devices with their start and end apart: 67, of which 22 were waited for; matrix products, arithmetic and copies ran while one was open for 4% of the time, Pallas kernels for 24%

profile of v4, /device:TPU:7, one launch (start us, length us, event | category | flops | bytes accessed | tf_op | source)
XLA Modules:
  0.0 526.4 jit_solution(16127442140000329545)
XLA Ops:
  18.0 6.9 %collective-permute-done.20.piece_ref = bf16[80,1536]{1,0:T(8,128)(2,1)S(1)} collective-permute-done((bf16[80,1536]{1,0:T(8,128)(2,1)}, bf16[80,1536]{1,0:T(8,128)(2,1)S(1)}, u32[]{:S(2)}, u32[]{:S(2)}) %collective-permute-start.20) | collective-permute-done | bytes 245792 | tf_op jit(solution)/shard_map/ppermute | solution.py:858
  37.3 9.7 %collective-permute-done.1.refs_2_ = bf16[128,1536]{1,0:T(8,128)(2,1)S(1)} collective-permute-done((bf16[128,1536]{1,0:T(8,128)(2,1)S(1)}, bf16[128,1536]{1,0:T(8,128)(2,1)S(1)}, u32[]{:S(2)}, u32[]{:S(2)}) %collective-permute-start.1) | collective-permute-done | bytes 393248 | tf_op jit(solution)/shard_map/ppermute | solution.py:59
  99.9 10.2 %all_to_all.35.heads_ref = bf16[8,128,256]{2,1,0:T(8,128)(2,1)S(1)} all-to-all(bf16[8,128,256]{2,1,0:T(8,128)(2,1)S(1)} %get-tuple-element.104), channel_id=1, replica_groups=mesh['yh'=2,'x'=4,'yl'=2,'z'=4,'c'=2] {'yl','z'}, dimensions={0} | all-to-all | bytes 1048576 | tf_op jit(solution)/shard_map/all_to_all | solution.py:887
  115.3 7.3 %all-to-all-start.2 = ((bf16[8,128,512]{2,1,0:T(8,128)(2,1)}), bf16[8,128,512]{2,1,0:T(8,128)(2,1)S(1)}, u32[]{:S(2)}, u32[]{:S(2)}) async-start(bf16[8,128,512]{2,1,0:T(8,128)(2,1)} %broadcast_in_dim.38), calls=%async_computation.2 | async-start | bytes 2097152 | tf_op jit(solution)/shard_map/all_to_all | solution.py:146
  126.5 8.4 %collective-permute-done.11.refs_5_ = bf16[128,1536]{1,0:T(8,128)(2,1)S(1)} collective-permute-done((bf16[128,1536]{1,0:T(8,128)(2,1)S(1)}, bf16[128,1536]{1,0:T(8,128)(2,1)S(1)}, u32[]{:S(2)}, u32[]{:S(2)}) %collective-permute-start.11) | collective-permute-done | bytes 393248 | tf_op jit(solution)/shard_map/ppermute | solution.py:59
  134.9 6.6 %collective-permute-done.13.refs_7_ = bf16[128,1536]{1,0:T(8,128)(2,1)} collective-permute-done((bf16[128,1536]{1,0:T(8,128)(2,1)S(1)}, bf16[128,1536]{1,0:T(8,128)(2,1)}, u32[]{:S(2)}, u32[]{:S(2)}) %collective-permute-start.13) | collective-permute-done | bytes 393248 | tf_op jit(solution)/shard_map/ppermute | solution.py:59
  153.1 15.6 %collective-permute-done.15.refs_0_.refs_4_ = bf16[256,1536]{1,0:T(8,128)(2,1)} collective-permute-done((bf16[256,1536]{1,0:T(8,128)(2,1)}, bf16[256,1536]{1,0:T(8,128)(2,1)}, u32[]{:S(2)}, u32[]{:S(2)}) %collective-permute-start.15) | collective-permute-done | bytes 786464 | tf_op jit(solution)/shard_map/ppermute | solution.py:59
  168.6 11.0 %collective-permute-done.16.refs_3_ = bf16[256,1536]{1,0:T(8,128)(2,1)} collective-permute-done((bf16[256,1536]{1,0:T(8,128)(2,1)}, bf16[256,1536]{1,0:T(8,128)(2,1)}, u32[]{:S(2)}, u32[]{:S(2)}) %collective-permute-start.16) | collective-permute-done | bytes 786464 | tf_op jit(solution)/shard_map/ppermute | solution.py:59
  197.1 11.8 %collective-permute-done.22.refs_1_ = bf16[256,1536]{1,0:T(8,128)(2,1)S(1)} collective-permute-done((bf16[256,1536]{1,0:T(8,128)(2,1)}, bf16[256,1536]{1,0:T(8,128)(2,1)S(1)}, u32[]{:S(2)}, u32[]{:S(2)}) %collective-permute-start.22) | collective-permute-done | bytes 786464 | tf_op jit(solution)/shard_map/ppermute | solution.py:59
  210.1 24.3 %shard_map.165 = (bf16[1024,640]{1,0:T(8,128)(2,1)}, bf16[1024,640]{1,0:T(8,128)(2,1)}, bf16[1024,1280]{1,0:T(8,128)(2,1)}, bf16[1024,1280]{1,0:T(8,128)(2,1)}, ...) custom-call(s32[8]{0:T(128)} %copy-done.20, ...), custom_call_target="tpu_custom_call" | custom-call | flops 12179999744 | bytes 1000 | tf_op jit(solution)/shard_map/pallas_call | solution.py:767
  235.8 24.7 %shard_map.166 = (bf16[1024,640]{1,0:T(8,128)(2,1)}, bf16[1024,640]{1,0:T(8,128)(2,1)}, bf16[1024,1280]{1,0:T(8,128)(2,1)}, bf16[1024,1280]{1,0:T(8,128)(2,1)}, ...) custom-call(s32[8]{0:T(128)} %copy-done.20, ...), custom_call_target="tpu_custom_call", output_to_operand_aliasing={{0}: (8, {}), {1}: (9, {}), {2}: (10, {}), {3}: (11, {}), {... | custom-call | flops 12179999744 | bytes 1000 | tf_op jit(solution)/shard_map/pallas_call | solution.py:767
  262.9 13.5 %shard_map.167 = bf16[8,288,1280]{2,1,0:T(8,128)(2,1)} custom-call(s32[8]{0:T(128)S(1)} %copy-done.22, bf16[256,1536]{1,0:T(8,128)(2,1)} %get-tuple-element.127.refs_0_, bf16[256,1536]{1,0:T(8,128)(2,1)S(1)} %copy-done.27, bf16[256,1536]{1,0:T(8,128)(2,1)S(1)} %copy-done.30, bf16[256,1536]{1,0:T(8,128)(2,1)} %collective-permute-done.16.refs_3_, ...), custom_call_target="tpu_custom_call" | custom-call | flops 6206000128 | bytes 1000 | tf_op jit(solution)/shard_map/pallas_call | solution.py:169
  282.1 7.5 %collective-permute-done.28 = bf16[128,1536]{1,0:T(8,128)(2,1)S(1)} collective-permute-done((bf16[128,1536]{1,0:T(8,128)(2,1)}, bf16[128,1536]{1,0:T(8,128)(2,1)S(1)}, u32[]{:S(2)}, u32[]{:S(2)}) %collective-permute-start.28) | collective-permute-done | bytes 393248 | tf_op jit(solution)/shard_map/ppermute | solution.py:59
  293.9 15.0 %shard_map.168 = (bf16[288,1280]{1,0:T(8,128)(2,1)}, bf16[288,1280]{1,0:T(8,128)(2,1)}, bf16[288,1280]{1,0:T(8,128)(2,1)}, bf16[288,1280]{1,0:T(8,128)(2,1)}, bf...) custom-call(s32[8]{0:T(128)} %copy-done.20, ...), custom_call_target="tpu_custom_call" | custom-call | flops 8700000256 | bytes 1000 | tf_op jit(solution)/shard_map/pallas_call | solution.py:169
  322.2 8.7 %shard_map.170 = (bf16[128,1536]{1,0:T(8,128)(2,1)}, bf16[8,128,512]{2,1,0:T(8,128)(2,1)}) custom-call(s32[1]{0:T(128)} %bitcast.1.me_ref.group_ref, bf16[8,128,256]{2,1,0:T(8,128)(2,1)} %copy-done.6, bf16[8,128,512]{2,1,0:T(8,128)(2,1)} %copy-done.3, bf16[128,1536]{1,0:T(8,128)(2,1)} %copy-done.59, f32[12,128,1]{2,1,0:T(8,128)} %copy-done.62, ...), custom_call_target="tpu_custom_call" | custom-call | flops 5219999744 | bytes 1000 | tf_op jit(solution)/shard_map/pallas_call | solution.py:607
  334.6 23.9 %all_to_all.36.dkv_ref = bf16[8,128,512]{2,1,0:T(8,128)(2,1)S(1)} all-to-all(bf16[8,128,512]{2,1,0:T(8,128)(2,1)} %get-tuple-element.158), channel_id=1, replica_groups=mesh['yh'=2,'x'=4,'yl'=2,'z'=4,'c'=2] {'yh','x'}, dimensions={0} | all-to-all | bytes 2097152 | tf_op jit(solution)/shard_map/all_to_all | solution.py:926
  359.8 9.8 %collective-permute-start.35 = (bf16[1536,1024]{1,0:T(8,128)(2,1)}, bf16[1536,1024]{1,0:T(8,128)(2,1)}, u32[]{:S(2)}, u32[]{:S(2)}) collective-permute-start(bf16[1536,1024]{1,0:T(8,128)(2,1)} %all-gather.7.cloned.1.call-done.mine_ref), channel_id=1, source_target_pairs={{0,1},{1,0},{2,3},{3,2},{4,5},{5,4},{6,7},{7,6},{8,9},{9,8},{10,11... | collective-permute-start | bytes 9437192 | tf_op jit(solution)/shard_map/ppermute | solution.py:142
  391.5 13.2 %collective-permute-done.38 = bf16[288,1280]{1,0:T(8,128)(2,1)} collective-permute-done((bf16[288,1280]{1,0:T(8,128)(2,1)}, bf16[288,1280]{1,0:T(8,128)(2,1)}, u32[]{:S(2)}, u32[]{:S(2)}) %collective-permute-start.38) | collective-permute-done | bytes 737312 | tf_op jit(solution)/shard_map/ppermute | solution.py:59
  404.7 8.4 %shard_map.173 = (f32[1536,256]{1,0:T(8,128)}, bf16[1536,256]{1,0:T(8,128)(2,1)}, f32[1,256]{1,0:T(1,128)S(1)}) custom-call(s32[1]{0:T(128)} %bitcast.core_ref, s32[8]{0:T(128)S(1)} %copy-done.23, bf16[8,128,1536]{2,1,0:T(8,128)(2,1)} %copy-done.52, bf16[8,128,512]{2,1,0:T(8,128)(2,1)} %all-to-all-done.4.both_ref, ...), custom_call_target="tpu_custom_call" | custom-call | flops 2900000000 | bytes 1000 | tf_op jit(solution)/shard_map/pallas_call | solution.py:169
  421.6 8.2 %all-to-all-start.5 = ((bf16[8,208,256]{2,1,0:T(8,128)(2,1)}), bf16[8,208,256]{2,1,0:T(8,128)(2,1)S(1)}, u32[]{:S(2)}, u32[]{:S(2)}) async-start(bf16[8,208,256]{2,1,0:T(8,128)(2,1)} %shard_map.174), calls=%async_computation.6 | async-start | bytes 1703936 | tf_op jit(solution)/shard_map/all_to_all | solution.py:955
  433.5 12.4 %collective-permute-start.45 = (bf16[288,1280]{1,0:T(8,128)(2,1)S(1)}, bf16[288,1280]{1,0:T(8,128)(2,1)}, u32[]{:S(2)}, u32[]{:S(2)}) collective-permute-start(bf16[288,1280]{1,0:T(8,128)(2,1)S(1)} %pad_maximum_fusion.refs_0_), channel_id=1, source_target_pairs={{0,4},{2,6},{4,0},{6,2},{8,12},{10,14},{12,8},{14,10},{1,5},{3,7},... | collective-permute-start | bytes 2211848 | tf_op jit(solution)/shard_map/ppermute | solution.py:59
  454.8 8.0 %collective-permute-done.45.refs_4_ = bf16[288,1280]{1,0:T(8,128)(2,1)} collective-permute-done((bf16[288,1280]{1,0:T(8,128)(2,1)S(1)}, bf16[288,1280]{1,0:T(8,128)(2,1)}, u32[]{:S(2)}, u32[]{:S(2)}) %collective-permute-start.45) | collective-permute-done | bytes 737312 | tf_op jit(solution)/shard_map/ppermute | solution.py:59
  463.3 14.9 %collective-permute-done.42.refs_1_ = bf16[288,1280]{1,0:T(8,128)(2,1)} collective-permute-done((bf16[288,1280]{1,0:T(8,128)(2,1)S(1)}, bf16[288,1280]{1,0:T(8,128)(2,1)}, u32[]{:S(2)}, u32[]{:S(2)}) %collective-permute-start.42) | collective-permute-done | bytes 737312 | tf_op jit(solution)/shard_map/ppermute | solution.py:59
  487.3 8.2 %shard_map.176 = (f32[192,17920]{1,0:T(8,128)}, f32[1120,1536]{1,0:T(8,128)}) custom-call(s32[1]{0:T(128)} %bitcast.core_ref, s32[8]{0:T(128)S(1)} %copy-done.23, bf16[288,1280]{1,0:T(8,128)(2,1)S(1)} %copy-done.8, bf16[288,1280]{1,0:T(8,128)(2,1)} %collective-permute-done.42.refs_1_, bf16[288,1280]{1,0:T(8,128)(2,1)} %collective-permute-done.43.refs_2_, ...), custom_call_target="tpu_custom_call" | custom-call | flops 5800000000 | bytes 1000 | tf_op jit(solution)/shard_map/pallas_call | solution.py:437
  (328 shorter events, 223.4 us)
Async XLA Ops:
  7.2 103.0 %all-gather.5.cloned.1.call-start = ((), (), s32[]{:S(2)}) async-start(), calls=%async_computation.8 | async-start | bytes 2654208 | tf_op jit(solution)/shard_map/all_gather | solution.py:856
  9.1 174.8 %all-gather.9.cloned.1.call-start = ((), (), s32[]{:S(2)}) async-start(), calls=%async_computation.11 | async-start | bytes 6635520 | tf_op jit(solution)/shard_map/all_gather | solution.py:869
  48.0 33.1 %all-to-all-start = ((bf16[8,208,256]{2,1,0:T(8,128)(2,1)}), bf16[8,208,256]{2,1,0:T(8,128)(2,1)}, u32[]{:S(2)}, u32[]{:S(2)}) async-start(bf16[8,208,256]{2,1,0:T(8,128)(2,1)} %broadcast_in_dim.35), calls=%async_computation | async-start | bytes 1703936 | tf_op jit(solution)/shard_map/all_to_all | solution.py:146
  74.3 24.2 %collective-permute-start.9 = (bf16[128,1536]{1,0:T(8,128)(2,1)S(1)}, bf16[128,1536]{1,0:T(8,128)(2,1)S(1)}, u32[]{:S(2)}, u32[]{:S(2)}) collective-permute-start(bf16[128,1536]{1,0:T(8,128)(2,1)S(1)} %bitcast.39), channel_id=1, source_target_pairs={{0,8},{2,10},{4,12},{6,14},{8,0},{10,2},{12,4},{14,6},{1,9},{3,11}... | collective-permute-start | bytes 1179656 | tf_op jit(solution)/shard_map/ppermute | solution.py:59
  110.2 34.8 %collective-permute-start.14 = (bf16[1536,768]{1,0:T(8,128)(2,1)}, bf16[1536,768]{1,0:T(8,128)(2,1)}, u32[]{:S(2)}, u32[]{:S(2)}) collective-permute-start(bf16[1536,768]{1,0:T(8,128)(2,1)} %all-gather.5.cloned.1.call-done.mine_ref), channel_id=1, source_target_pairs={{0,1},{1,0},{2,3},{3,2},{4,5},{5,4},{6,7},{7,6},{8,9},{9,8},{10,11... | collective-permute-start | bytes 7077896 | tf_op jit(solution)/shard_map/ppermute | solution.py:142
  115.3 26.2 %all-to-all-start.2 = ((bf16[8,128,512]{2,1,0:T(8,128)(2,1)}), bf16[8,128,512]{2,1,0:T(8,128)(2,1)S(1)}, u32[]{:S(2)}, u32[]{:S(2)}) async-start(bf16[8,128,512]{2,1,0:T(8,128)(2,1)} %broadcast_in_dim.38), calls=%async_computation.2 | async-start | bytes 2097152 | tf_op jit(solution)/shard_map/all_to_all | solution.py:146
  122.5 138.0 %all-gather.7.cloned.1.call-start = ((), (), s32[]{:S(2)}) async-start(), calls=%async_computation.9 | async-start | bytes 3538944 | tf_op jit(solution)/shard_map/all_gather | solution.py:903
  152.0 27.6 %collective-permute-start.16 = (bf16[256,1536]{1,0:T(8,128)(2,1)}, bf16[256,1536]{1,0:T(8,128)(2,1)}, u32[]{:S(2)}, u32[]{:S(2)}) collective-permute-start(bf16[256,1536]{1,0:T(8,128)(2,1)} %get-tuple-element.127.refs_0_), channel_id=1, source_target_pairs={{0,8},{2,10},{4,12},{6,14},{8,0},{10,2},{12,4},{14,6},{1,9},{3,11}... | collective-permute-start | bytes 2359304 | tf_op jit(solution)/shard_map/ppermute | solution.py:59
  183.9 25.2 %collective-permute-start.21 = (bf16[8,288,1280]{2,1,0:T(8,128)(2,1)}, bf16[8,288,1280]{2,1,0:T(8,128)(2,1)}, u32[]{:S(2)}, u32[]{:S(2)}) collective-permute-start(bf16[8,288,1280]{2,1,0:T(8,128)(2,1)} %bitcast.56), channel_id=1, source_target_pairs={{0,1},{1,0},{2,3},{3,2},{4,5},{5,4},{6,7},{7,6},{8,9},{9,8},{10,11... | collective-permute-start | bytes 17694728 | tf_op jit(solution)/shard_map/ppermute | solution.py:142
  187.3 227.1 %reduce-scatter.2.cloned.1.call-start = ((), (), s32[]{:S(2)}) async-start(), calls=%async_computation.10 | async-start | bytes 3538944 | tf_op jit(solution)/shard_map/reduce_scatter | solution.py:929
  194.4 40.0 %collective-permute-start.17 = (bf16[256,1536]{1,0:T(8,128)(2,1)}, bf16[256,1536]{1,0:T(8,128)(2,1)S(1)}, u32[]{:S(2)}, u32[]{:S(2)}) collective-permute-start(bf16[256,1536]{1,0:T(8,128)(2,1)} %collective-permute-done.16.refs_3_), channel_id=1, source_target_pairs={{0,2},{2,4},{4,6},{6,0},{8,10},{10,12},{12,14},{14,8},{1,3},{3,5},... | collective-permute-start | bytes 2359304 | tf_op jit(solution)/shard_map/ppermute | solution.py:59
  194.4 40.0 %collective-permute-start.18 = (bf16[256,1536]{1,0:T(8,128)(2,1)}, bf16[256,1536]{1,0:T(8,128)(2,1)S(1)}, u32[]{:S(2)}, u32[]{:S(2)}) collective-permute-start(bf16[256,1536]{1,0:T(8,128)(2,1)} %collective-permute-done.16.refs_3_), channel_id=1, source_target_pairs={{0,6},{2,0},{4,2},{6,4},{8,14},{10,8},{12,10},{14,12},{1,7},{3,1},... | collective-permute-start | bytes 2359304 | tf_op jit(solution)/shard_map/ppermute | solution.py:59
  208.9 25.5 %collective-permute-start.19 = (bf16[256,1536]{1,0:T(8,128)(2,1)}, bf16[256,1536]{1,0:T(8,128)(2,1)S(1)}, u32[]{:S(2)}, u32[]{:S(2)}) collective-permute-start(bf16[256,1536]{1,0:T(8,128)(2,1)} %collective-permute-done.15.refs_0_.refs_4_), channel_id=1, source_target_pairs={{0,8},{2,10},{4,12},{6,14},{8,0},{10,2},{12,4},{14,6},{1,9},{3,11}... | collective-permute-start | bytes 2359304 | tf_op jit(solution)/shard_map/ppermute | solution.py:59
  282.1 26.7 %collective-permute-start.24 = (bf16[128,1536]{1,0:T(8,128)(2,1)}, bf16[128,1536]{1,0:T(8,128)(2,1)S(1)}, u32[]{:S(2)}, u32[]{:S(2)}) collective-permute-start(bf16[128,1536]{1,0:T(8,128)(2,1)} %get-tuple-element.119), channel_id=1, source_target_pairs={{0,2},{2,4},{4,6},{6,0},{8,10},{10,12},{12,14},{14,8},{1,3},{3,5},... | collective-permute-start | bytes 1179656 | tf_op jit(solution)/shard_map/ppermute | solution.py:59
  311.1 23.6 %collective-permute-start.34 = (bf16[288,1280]{1,0:T(8,128)(2,1)}, bf16[288,1280]{1,0:T(8,128)(2,1)S(1)}, u32[]{:S(2)}, u32[]{:S(2)}) collective-permute-start(bf16[288,1280]{1,0:T(8,128)(2,1)} %get-tuple-element.146), channel_id=1, source_target_pairs={{0,64},{16,80},{32,96},{48,112},{64,0},{80,16},{96,32},{112,48},{1... | collective-permute-start | bytes 2211848 | tf_op jit(solution)/shard_map/ppermute | solution.py:59
  372.2 32.4 %all-to-all-start.4 = ((bf16[8,128,512]{2,1,0:T(8,128)(2,1)}), bf16[8,128,512]{2,1,0:T(8,128)(2,1)}, u32[]{:S(2)}, u32[]{:S(2)}) async-start(bf16[8,128,512]{2,1,0:T(8,128)(2,1)} %get-tuple-element.161), calls=%async_computation.5 | async-start | bytes 2097152 | tf_op jit(solution)/shard_map/all_to_all | solution.py:935
  379.8 24.9 %collective-permute-start.38 = (bf16[288,1280]{1,0:T(8,128)(2,1)}, bf16[288,1280]{1,0:T(8,128)(2,1)}, u32[]{:S(2)}, u32[]{:S(2)}) collective-permute-start(bf16[288,1280]{1,0:T(8,128)(2,1)} %add_convert_fusion.2), channel_id=1, source_target_pairs={{0,32},{16,48},{32,0},{48,16},{64,96},{80,112},{96,64},{112,80},{1... | collective-permute-start | bytes 2211848 | tf_op jit(solution)/shard_map/ppermute | solution.py:59
  421.6 27.9 %all-to-all-start.5 = ((bf16[8,208,256]{2,1,0:T(8,128)(2,1)}), bf16[8,208,256]{2,1,0:T(8,128)(2,1)S(1)}, u32[]{:S(2)}, u32[]{:S(2)}) async-start(bf16[8,208,256]{2,1,0:T(8,128)(2,1)} %shard_map.174), calls=%async_computation.6 | async-start | bytes 1703936 | tf_op jit(solution)/shard_map/all_to_all | solution.py:955
  430.8 24.1 %collective-permute-start.44 = (bf16[288,1280]{1,0:T(8,128)(2,1)S(1)}, bf16[288,1280]{1,0:T(8,128)(2,1)}, u32[]{:S(2)}, u32[]{:S(2)}) collective-permute-start(bf16[288,1280]{1,0:T(8,128)(2,1)S(1)} %pad_maximum_fusion.refs_0_), channel_id=1, source_target_pairs={{0,8},{2,10},{4,12},{6,14},{8,0},{10,2},{12,4},{14,6},{1,9},{3,11}... | collective-permute-start | bytes 2211848 | tf_op jit(solution)/shard_map/ppermute | solution.py:59
  433.5 29.3 %collective-permute-start.45 = (bf16[288,1280]{1,0:T(8,128)(2,1)S(1)}, bf16[288,1280]{1,0:T(8,128)(2,1)}, u32[]{:S(2)}, u32[]{:S(2)}) collective-permute-start(bf16[288,1280]{1,0:T(8,128)(2,1)S(1)} %pad_maximum_fusion.refs_0_), channel_id=1, source_target_pairs={{0,4},{2,6},{4,0},{6,2},{8,12},{10,14},{12,8},{14,10},{1,5},{3,7},... | collective-permute-start | bytes 2211848 | tf_op jit(solution)/shard_map/ppermute | solution.py:59
  445.9 32.3 %collective-permute-start.42 = (bf16[288,1280]{1,0:T(8,128)(2,1)S(1)}, bf16[288,1280]{1,0:T(8,128)(2,1)}, u32[]{:S(2)}, u32[]{:S(2)}) collective-permute-start(bf16[288,1280]{1,0:T(8,128)(2,1)S(1)} %pad_maximum_fusion.refs_0_), channel_id=1, source_target_pairs={{0,2},{2,4},{4,6},{6,0},{8,10},{10,12},{12,14},{14,8},{1,3},{3,5},... | collective-permute-start | bytes 2211848 | tf_op jit(solution)/shard_map/ppermute | solution.py:59
  446.0 32.7 %collective-permute-start.43 = (bf16[288,1280]{1,0:T(8,128)(2,1)S(1)}, bf16[288,1280]{1,0:T(8,128)(2,1)}, u32[]{:S(2)}, u32[]{:S(2)}) collective-permute-start(bf16[288,1280]{1,0:T(8,128)(2,1)S(1)} %pad_maximum_fusion.refs_0_), channel_id=1, source_target_pairs={{0,6},{2,0},{4,2},{6,4},{8,14},{10,8},{12,10},{14,12},{1,7},{3,1},... | collective-permute-start | bytes 2211848 | tf_op jit(solution)/shard_map/ppermute | solution.py:59
  448.6 30.1 %collective-permute-start.46 = (bf16[288,1280]{1,0:T(8,128)(2,1)S(1)}, bf16[288,1280]{1,0:T(8,128)(2,1)}, u32[]{:S(2)}, u32[]{:S(2)}) collective-permute-start(bf16[288,1280]{1,0:T(8,128)(2,1)S(1)} %pad_maximum_fusion.refs_0_), channel_id=1, source_target_pairs={{0,1},{1,0},{2,3},{3,2},{4,5},{5,4},{6,7},{7,6},{8,9},{9,8},{10,11... | collective-permute-start | bytes 2211848 | tf_op jit(solution)/shard_map/ppermute | solution.py:142
  482.4 25.4 %all-to-all-start.6 = ((bf16[8,208,256]{2,1,0:T(8,128)(2,1)}), bf16[8,208,256]{2,1,0:T(8,128)(2,1)S(1)}, u32[]{:S(2)}, u32[]{:S(2)}) async-start(bf16[8,208,256]{2,1,0:T(8,128)(2,1)} %shard_map.175), calls=%async_computation.7 | async-start | bytes 1703936 | tf_op jit(solution)/shard_map/all_to_all | solution.py:964
  (118 other events, 1512.5 us)
Sparse Core Ops, SparseCore 0:
  10.3 67.1 all-gather.4
  80.4 103.3 all-gather.8
  187.4 67.8 all-gather.6
  309.1 64.7 reduce-scatter.1
